TPU v7x, 256 devices: a whole 4x4x8 slice. The times are simulated.
256 devices in a mesh: ctx: 16 (over z_lo, x, core), ch: 16 (over z_hi, y).
Axes of the slice: x: 4, y: 4, z: 8 (z_hi: 4, z_lo: 2; z = z_hi * 2 + z_lo), core: 2. Of those that a mesh axis runs over, the one named last changes fastest.
Arguments:
- seq_input: bfloat16 [32768, 2048], P('ctx', 'ch'), may hold values from -6 to 6
- out_grad: bfloat16 [32768, 2048], P('ctx', 'ch'), may hold values from -6 to 6
- filters: bfloat16 [32768, 128], P('ctx', 'ch'), may hold values from -1.1 to 1.1
Outputs:
- conv_out: bfloat16 [32768, 2048], P('ctx', 'ch')
- input_grad: bfloat16 [32768, 2048], P('ctx', 'ch')
- filter_grad: float32 [32768, 128], P('ctx')
All inputs are finite; a program needn't handle non-finite values.
Results may differ from a plain program's by a relative error of at most 0.02.
Values may be sent and summed in bfloat16 or wider, within the bound.
No kernel may reach another device: no remote copies, remote signals or barrier semaphores. Data moves between devices by JAX's collectives and lax.ppermute only.
A program may use at most 128 MiB of HBM per device.

v0:
```python
import math

import jax
import jax.numpy as jnp
from jax import lax
from jax.sharding import PartitionSpec as P

P_SIZE = 256


def counting(length):
    return jnp.arange(length, dtype=jnp.int32)


def angle_table(row_index, col_index, modulus, direction):
    product = row_index[:, None] * col_index[None, :] % modulus
    angles = direction * 2.0 * math.pi / modulus * product.astype(jnp.float32)
    return (jnp.cos(angles), jnp.sin(angles))


def complex_block(cosine, sine_table):
    cos_half = cosine.astype(jnp.bfloat16)
    sin_half = sine_table.astype(jnp.bfloat16)
    return jnp.stack([jnp.stack([cos_half, -sin_half]), jnp.stack([sin_half, cos_half])])


def products(x_spec, dy_spec, h_spec):
    x_real = x_spec[0].astype(jnp.float32)
    x_imag = x_spec[1].astype(jnp.float32)
    dy_real = dy_spec[0].astype(jnp.float32)
    dy_imag = dy_spec[1].astype(jnp.float32)
    h_real = h_spec[0].astype(jnp.float32)
    h_imag = h_spec[1].astype(jnp.float32)
    y_spec = jnp.stack(
        [x_real * h_real - x_imag * h_imag, x_real * h_imag + x_imag * h_real]
    ).astype(jnp.bfloat16)
    dx_spec = jnp.stack(
        [dy_real * h_real + dy_imag * h_imag, dy_imag * h_real - dy_real * h_imag]
    ).astype(jnp.bfloat16)
    group_part = jnp.stack(
        [dy_real * x_real + dy_imag * x_imag, dy_imag * x_real - dy_real * x_imag]
    )
    return (y_spec, dx_spec, group_part)


def forward_spread(signal):
    tok_count, signal_width = signal.shape
    ctx_count = lax.axis_size("ctx")
    position = lax.axis_index("ctx")
    full_len = 2 * tok_count * ctx_count
    second_len = full_len // P_SIZE
    half_len = P_SIZE // 2
    row_count = half_len // ctx_count
    col_count = second_len // ctx_count
    row_block = signal.reshape(row_count, second_len, signal_width)
    spread = lax.all_to_all(row_block, "ctx", split_axis=1, concat_axis=0, tiled=True)
    flattened = spread.reshape(half_len, col_count * signal_width)
    cosine, sine_table = angle_table(counting(P_SIZE), counting(half_len), P_SIZE, -1.0)
    first_real = jnp.dot(cosine.astype(jnp.bfloat16), flattened, preferred_element_type=jnp.float32)
    first_imag = jnp.dot(
        sine_table.astype(jnp.bfloat16), flattened, preferred_element_type=jnp.float32
    )
    first_real = first_real.reshape(P_SIZE, col_count, signal_width)
    first_imag = first_imag.reshape(P_SIZE, col_count, signal_width)
    tw_cos, tw_sin = angle_table(
        counting(P_SIZE), position * col_count + counting(col_count), full_len, -1.0
    )
    tw_cos = tw_cos[:, :, None]
    tw_sin = tw_sin[:, :, None]
    second_real = (first_real * tw_cos - first_imag * tw_sin).astype(jnp.bfloat16)
    second_imag = (first_real * tw_sin + first_imag * tw_cos).astype(jnp.bfloat16)
    arrived = lax.all_to_all(
        jnp.stack([second_real, second_imag]), "ctx", split_axis=1, concat_axis=2, tiled=True
    )
    cosine, sine_table = angle_table(counting(second_len), counting(second_len), second_len, -1.0)
    table = complex_block(cosine, sine_table)
    return jnp.einsum("zwyq,wkqc->zkyc", table, arrived, preferred_element_type=jnp.float32).astype(
        jnp.bfloat16
    )


def inverse_spread(spectrum):
    second_len = spectrum.shape[2]
    signal_width = spectrum.shape[3]
    ctx_count = lax.axis_size("ctx")
    position = lax.axis_index("ctx")
    full_len = P_SIZE * second_len
    half_len = P_SIZE // 2
    col_count = second_len // ctx_count
    freq_count = P_SIZE // ctx_count
    cosine, sine_table = angle_table(counting(second_len), counting(second_len), second_len, 1.0)
    first_pass = jnp.einsum(
        "zwyq,wkqc->zkyc",
        complex_block(cosine, sine_table),
        spectrum,
        preferred_element_type=jnp.float32,
    )
    tw_cos, tw_sin = angle_table(
        position * freq_count + counting(freq_count), counting(second_len), full_len, 1.0
    )
    tw_cos = tw_cos[:, :, None]
    tw_sin = tw_sin[:, :, None]
    back_real = (first_pass[0] * tw_cos - first_pass[1] * tw_sin).astype(jnp.bfloat16)
    back_imag = (first_pass[0] * tw_sin + first_pass[1] * tw_cos).astype(jnp.bfloat16)
    arrived = lax.all_to_all(
        jnp.stack([back_real, back_imag]), "ctx", split_axis=2, concat_axis=1, tiled=True
    )
    cosine, sine_table = angle_table(counting(half_len), counting(P_SIZE), P_SIZE, 1.0)
    flat_real = arrived[0].reshape(P_SIZE, col_count * signal_width)
    flat_imag = arrived[1].reshape(P_SIZE, col_count * signal_width)
    result = jnp.dot(cosine.astype(jnp.bfloat16), flat_real, preferred_element_type=jnp.float32)
    result = result - jnp.dot(
        sine_table.astype(jnp.bfloat16), flat_imag, preferred_element_type=jnp.float32
    )
    return (result * (1.0 / full_len)).reshape(half_len, col_count, signal_width)


def local(seq_input, out_grad, filters):
    gathered = lax.all_gather(filters, "ch", axis=1, tiled=True)
    tok_count, channel_count = seq_input.shape
    ctx_count = lax.axis_size("ctx")
    ch_count = lax.axis_size("ch")
    grad_scale = 1.0 / math.sqrt(tok_count * ctx_count * ch_count)
    signals = jnp.concatenate([seq_input, out_grad, gathered], axis=1)
    spectra = forward_spread(signals)
    y_spec, dx_spec, group_part = products(
        spectra[..., :channel_count],
        spectra[..., channel_count : 2 * channel_count],
        spectra[..., 2 * channel_count :],
    )
    group_spec = lax.psum(group_part.astype(jnp.bfloat16), "ch")
    combined = jnp.concatenate([y_spec, dx_spec, group_spec], axis=3)
    result = inverse_spread(combined)
    outputs = lax.all_to_all(
        result[..., : 2 * channel_count].astype(jnp.bfloat16),
        "ctx",
        split_axis=0,
        concat_axis=1,
        tiled=True,
    )
    outputs = outputs.reshape(tok_count, 2 * channel_count)
    gradient = lax.all_to_all(
        (result[..., 2 * channel_count :] * grad_scale).astype(jnp.bfloat16),
        "ctx",
        split_axis=0,
        concat_axis=1,
        tiled=True,
    ).astype(jnp.float32)
    filter_grad = gradient.reshape(tok_count, gradient.shape[2])
    conv_out = outputs[:, :channel_count]
    input_grad = outputs[:, channel_count:]
    return (conv_out, input_grad, filter_grad)


def solution(mesh):
    placed = (P("ctx", "ch"), P("ctx", "ch"), P("ctx", "ch"))
    return jax.shard_map(
        local,
        mesh=mesh,
        in_specs=placed,
        out_specs=(P("ctx", "ch"), P("ctx", "ch"), P("ctx", None)),
        check_vma=False,
    )
```

profile of v0, /device:TPU:1, one launch (start us, length us, event | category | flops | bytes accessed | tf_op | source)
XLA Modules:
  0.0 545.7 jit_solution(13678319610482159220)
XLA Ops:
  7.2 43.7 %all_gather.3 = bf16[2048,128]{0,1:T(8,128)(2,1)S(1)} all-gather(bf16[2048,8]{0,1:T(8,128)(2,1)} %param.5), channel_id=1, replica_groups=mesh['ctx'=16,'ch'=16] {'ch'}, dimensions={1}, use_global_device_ids=true | all-gather | bytes 557056 | tf_op jit(solution)/shard_map/all_gather | solution.py:119
  50.8 0.3 copy.52
  51.1 1.4 pad_maximum_fusion.3
  52.5 2.1 copy.53
  54.6 13.9 %all-to-all-start = ((bf16[8,256,384]{2,0,1:T(8,128)(2,1)}), bf16[8,256,384]{2,0,1:T(8,128)(2,1)S(1)}, u32[]{:S(2)}, u32[]{:S(2)}) async-start(bf16[8,256,384]{2,0,1:T(8,128)(2,1)} %copy.53), calls=%async_computation | async-start | bytes 3145728 | tf_op jit(solution)/shard_map/all_to_all | solution.py:56
  68.6 0.2 fusion.80
  68.7 21.6 %all-to-all-done = bf16[8,256,384]{2,0,1:T(8,128)(2,1)S(1)} async-done(((bf16[8,256,384]{2,0,1:T(8,128)(2,1)}), bf16[8,256,384]{2,0,1:T(8,128)(2,1)S(1)}, u32[]{:S(2)}, u32[]{:S(2)}) %all-to-all-start) | async-done | bytes 1572896 | tf_op jit(solution)/shard_map/all_to_all | solution.py:56
  90.3 0.9 copy.56
  91.2 1.4 fusion.54
  92.6 3.5 fusion.16
  96.2 0.7 pad_maximum_fusion
  96.9 6.4 %copy.57 = bf16[2,256,16,384]{3,2,0,1:T(8,128)(2,1)} copy(bf16[2,256,16,384]{3,1,2,0:T(8,128)(2,1)S(1)} %pad_maximum_fusion) | data formatting | bytes 12582912 | tf_op jit(solution)/shard_map/stack | solution.py:73
  103.3 5.2 all-to-all-start.1
  108.5 0.2 all-reduce.2.cloned.1.call-start
  108.7 1.0 fusion.63
  109.7 1.1 sine_convert_fusion.1
  110.9 84.9 %all-to-all-done.1 = bf16[2,256,16,384]{3,2,0,1:T(8,128)(2,1)} async-done(((bf16[2,256,16,384]{3,2,0,1:T(8,128)(2,1)}), bf16[2,256,16,384]{3,2,0,1:T(8,128)(2,1)}, u32[]{:S(2)}, u32[]{:S(2)}) %all-to-all-start.1) | async-done | bytes 6291488 | tf_op jit(solution)/shard_map/all_to_all | solution.py:72
  195.7 3.9 copy.59
  199.6 3.8 fusion.1
  203.5 1.7 fusion.19
  205.1 2.2 fusion.25
  207.3 1.5 pad_maximum_fusion.2
  208.8 0.0 all-reduce.2.cloned.1.call-update
  208.9 1.0 fusion.64
  209.8 1.1 sine_convert_fusion
  211.0 0.7 maximum_bitcast_fusion.10
  211.7 0.2 fusion.78
  211.8 168.1 %all-reduce.2.cloned.1.call-done = bf16[2,16,256,128]{2,3,0,1:T(8,128)(2,1)} async-done(((bf16[2,16,256,128]{2,3,0,1:T(8,128)(2,1)}), bf16[2,16,256,128]{2,3,0,1:T(8,128)(2,1)}) %all-reduce.2.cloned.1.call-update) | async-done | bytes 2097168 | tf_op jit(solution)/shard_map/psum | solution.py:131
  380.0 5.1 fusion.13
  385.1 1.9 subtract_convert_fusion
  387.0 3.2 pad_maximum_fusion.1
  390.3 16.3 %copy.61 = bf16[2,16,256,384]{3,0,1,2:T(2,128)(2,1)} copy(bf16[2,16,256,384]{2,3,0,1:T(8,128)(2,1)} %pad_maximum_fusion.1) | data formatting | bytes 12582912 | tf_op jit(solution)/shard_map/stack | solution.py:106
  406.6 86.0 %all_to_all.72 = bf16[2,16,256,384]{3,0,1,2:T(2,128)(2,1)S(1)} all-to-all(bf16[2,16,256,384]{3,0,1,2:T(2,128)(2,1)} %copy.61), channel_id=1, replica_groups=mesh['ctx'=16,'ch'=16] {'ctx'}, dimensions={2} | all-to-all | bytes 12582912 | tf_op jit(solution)/shard_map/all_to_all | solution.py:105
  492.6 2.3 copy.62
  494.9 0.6 fusion.99
  495.5 0.5 copy.63
  496.0 0.9 copy.75
  496.9 1.1 fusion.52
  498.0 0.5 copy.64
  498.5 0.9 copy.76
  499.4 1.1 fusion
  500.6 0.5 copy.77
  501.1 0.9 fusion.30
  502.0 5.1 all-to-all-start.4
  507.2 1.1 slice.116
  508.3 8.9 %all-to-all-done.4 = bf16[128,16,128]{2,1,0:T(8,128)(2,1)} async-done(((bf16[128,16,128]{2,1,0:T(8,128)(2,1)}), bf16[128,16,128]{2,1,0:T(8,128)(2,1)}, u32[]{:S(2)}, u32[]{:S(2)}) %all-to-all-start.4) | async-done | bytes 524320 | tf_op jit(solution)/shard_map/all_to_all | solution.py:142
  517.2 4.6 all-to-all-start.3
  521.8 2.1 copy.66
  523.9 13.8 %all-to-all-done.3 = bf16[128,16,256]{2,1,0:T(8,128)(2,1)S(1)} async-done(((bf16[128,16,256]{2,1,0:T(8,128)(2,1)}), bf16[128,16,256]{2,1,0:T(8,128)(2,1)S(1)}, u32[]{:S(2)}, u32[]{:S(2)}) %all-to-all-start.3) | async-done | bytes 1048608 | tf_op jit(solution)/shard_map/all_to_all | solution.py:134
  537.7 0.1 copy.65
  537.8 1.0 fusion.100
  (2 shorter events, 0.0 us)
Async XLA Ops:
  54.6 35.7 %all-to-all-start = ((bf16[8,256,384]{2,0,1:T(8,128)(2,1)}), bf16[8,256,384]{2,0,1:T(8,128)(2,1)S(1)}, u32[]{:S(2)}, u32[]{:S(2)}) async-start(bf16[8,256,384]{2,0,1:T(8,128)(2,1)} %copy.53), calls=%async_computation | async-start | bytes 3145728 | tf_op jit(solution)/shard_map/all_to_all | solution.py:56
  103.3 92.5 %all-to-all-start.1 = ((bf16[2,256,16,384]{3,2,0,1:T(8,128)(2,1)}), bf16[2,256,16,384]{3,2,0,1:T(8,128)(2,1)}, u32[]{:S(2)}, u32[]{:S(2)}) async-start(bf16[2,256,16,384]{3,2,0,1:T(8,128)(2,1)} %copy.57), calls=%async_computation.1 | async-start | bytes 12582912 | tf_op jit(solution)/shard_map/all_to_all | solution.py:72
  108.5 271.5 %all-reduce.2.cloned.1.call-start = ((), (), s32[]{:S(2)}) async-start(), calls=%async_computation.5 | async-start | bytes 4194304 | tf_op jit(solution)/shard_map/psum | solution.py:131
  502.0 15.1 %all-to-all-start.4 = ((bf16[128,16,128]{2,1,0:T(8,128)(2,1)}), bf16[128,16,128]{2,1,0:T(8,128)(2,1)}, u32[]{:S(2)}, u32[]{:S(2)}) async-start(bf16[128,16,128]{2,1,0:T(8,128)(2,1)} %fusion.30), calls=%async_computation.4 | async-start | bytes 1048576 | tf_op jit(solution)/shard_map/all_to_all | solution.py:142
  517.2 20.5 %all-to-all-start.3 = ((bf16[128,16,256]{2,1,0:T(8,128)(2,1)}), bf16[128,16,256]{2,1,0:T(8,128)(2,1)S(1)}, u32[]{:S(2)}, u32[]{:S(2)}) async-start(bf16[128,16,256]{2,1,0:T(8,128)(2,1)} %slice.116), calls=%async_computation.3 | async-start | bytes 2097152 | tf_op jit(solution)/shard_map/all_to_all | solution.py:134
Sparse Core Ops, SparseCore 0:
  209.0 170.9 all-reduce.1
where the time goes:
time: 547 us; the launch traced here: 546 us
  waiting for transfers between devices  297 us (54%)
  blocking collectives  130 us (24%)
  local copies, waits for them, and re-layouts  40.5 us (7%)
  starting transfers between devices  29.1 us (5%)
  other arithmetic  18.8 us (3%)
  matrix products  16 us (3%)
  between operations  14.2 us (3%)
    psum x1, waiting for transfers between devices, local(): group_spec = lax.psum(group_part.astype(jnp.bfloat16), 'ch')  168 us
    all_to_all x1, blocking collectives, inverse_spread(): lax.all_to_all(jnp.stack([back_real, back_imag]), 'ctx', split_axis=2, co...  86 us
    all_to_all x1, waiting for transfers between devices, forward_spread(): lax.all_to_all(jnp.stack([second_real, second_imag]), 'ctx', split_axis=1...  84.9 us
    all_gather x1, blocking collectives, local(): gathered = lax.all_gather(filters, 'ch', axis=1, tiled=True)  43.7 us
    all_to_all x1, waiting for transfers between devices, forward_spread(): lax.all_to_all(row_block, 'ctx', split_axis=1, concat_axis=0, tiled=True)  21.6 us
    another operation x1, local copies, waits for them, and re-layouts, inverse_spread(): jnp.stack([back_real, back_imag])  16.3 us
    all_to_all x1, starting transfers between devices, forward_spread(): lax.all_to_all(row_block, 'ctx', split_axis=1, concat_axis=0, tiled=True)  13.9 us
    all_to_all x1, waiting for transfers between devices, local(): lax.all_to_all(result[..., :2 * channel_count].astype(jnp.bfloat16), 'ctx...  13.8 us
  transfers between devices with their start and end apart: 5, of which 5 were waited for; matrix products, arithmetic and copies ran while one was open for 2% of the time, Pallas kernels for 0%

commit v1 on v0

v1 whole, which is shorter than its diff:
```python
import functools
import math

import jax
import jax.numpy as jnp
import numpy as np
from jax import lax
from jax.experimental import pallas as pl
from jax.experimental.pallas import tpu as pltpu
from jax.sharding import Mesh
from jax.sharding import PartitionSpec as P

BF = jnp.bfloat16
F32 = jnp.float32
FACTOR = 256
HALF = 128
FULL = FACTOR * FACTOR
CTX = 16
SUB = HALF // CTX
TOK = SUB * FACTOR
COLS = 8
ZH = 4
Y = 4
GRAD_SCALE = 1.0 / math.sqrt(524288)


def unit(product, modulus):
    angles = np.float32(2.0 * math.pi / modulus) * (product % modulus).astype(np.float32)
    return np.cos(angles).astype(np.float32), np.sin(angles).astype(np.float32)


def tables():
    row = np.arange(HALF)
    n1 = (row % CTX) * SUB + row // CTX
    k1 = np.arange(HALF)
    n2 = np.arange(FACTOR)
    cos1, sin1 = unit((2 * k1[:, None] + 1) * n1[None, :], 2 * FACTOR)
    cos2, sin2 = unit(n2[:, None] * n2[None, :], FACTOR)
    tw_cos, tw_sin = unit((2 * k1[:, None] + 1) * n2[None, :], 2 * FULL)
    first = np.concatenate([cos1, -sin1], 0)
    second = np.block([[cos2, -sin2], [sin2, cos2]])
    back_first = np.block([[cos2, sin2], [-sin2, cos2]])
    back_last = np.concatenate([cos1.T, -sin1.T], 1) * np.float32(2.0 / FULL)
    half = lambda a: jnp.asarray(a, dtype=BF)
    return half(first), half(second), half(back_first), half(back_last), jnp.asarray(tw_cos), jnp.asarray(tw_sin)


def mm(a, b):
    return jnp.dot(a, b, preferred_element_type=F32)


def column(rows):
    return jnp.concatenate([rows[:, k * FACTOR : (k + 1) * FACTOR] for k in range(SUB)], axis=0)


def flat(block):
    return jnp.concatenate([block[k * CTX : (k + 1) * CTX] for k in range(SUB)], axis=1)


def permute_rows(dst, perm, src):
    step = 512
    for at in range(0, TOK, step):
        dst[:, at : at + step] = mm(perm[...], src[:, at : at + step]).astype(BF)


def twist(first, cos, sin):
    real, imag = first[:HALF], first[HALF:]
    return jnp.concatenate([real * cos + imag * sin, imag * cos - real * sin], axis=1).astype(BF)


def untwist(first, cos, sin):
    real, imag = first[:, :FACTOR], first[:, FACTOR:]
    return jnp.concatenate([real * cos - imag * sin, real * sin + imag * cos], axis=0).astype(BF)


def split(spec):
    return spec[:, :FACTOR].astype(F32), spec[:, FACTOR:].astype(F32)


def spread_kernel(x_ref, dy_ref, f_ref, perm_ref, eye_ref, out_ref, taps_ref):
    nt = (((1,), (1,)), ((), ()))
    step = 512
    for at in range(0, TOK, step):
        both = jnp.concatenate([x_ref[at : at + step], dy_ref[at : at + step]], axis=1)
        out_ref[:, at : at + step] = lax.dot_general(perm_ref[...], both, nt, preferred_element_type=F32).astype(BF)
    taps_ref[...] = lax.dot_general(eye_ref[...], f_ref[...], nt, preferred_element_type=F32).astype(BF)


def filter_kernel(r_ref, perm_ref, t1_ref, t2_ref, cos_ref, sin_ref, spec_ref, rp_ref):
    permute_rows(rp_ref, perm_ref, r_ref)

    def body(at, carry):
        cos, sin = cos_ref[...], sin_ref[...]
        parts = []
        for k in range(2):
            rows = rp_ref[pl.ds(pl.multiple_of((at * 2 + k) * CTX, CTX), CTX), :]
            parts.append(column(rows))
        first = mm(t1_ref[...], jnp.concatenate(parts, axis=1))
        second = jnp.concatenate([twist(first[:, k * FACTOR : (k + 1) * FACTOR], cos, sin) for k in range(2)], axis=0)
        spec = mm(second, t2_ref[...]).astype(BF)
        for k in range(2):
            spec_ref[at * 2 + k] = spec[k * HALF : (k + 1) * HALF]
        return carry

    lax.fori_loop(0, COLS // 2, body, 0)


def forward_kernel(r_ref, perm_ref, gperm_ref, t1_ref, t2_ref, t2i_ref, t1i_ref, cos_ref, sin_ref, spec_ref, g_ref, rp_ref, gs_ref):
    permute_rows(rp_ref, perm_ref, r_ref)

    def body(c, carry):
        cos, sin = cos_ref[...], sin_ref[...]
        parts = []
        for s in range(2):
            rows = rp_ref[pl.ds(pl.multiple_of(s * HALF + c * CTX, CTX), CTX), :]
            parts.append(column(rows))
        first = mm(t1_ref[...], jnp.concatenate(parts, axis=1))
        second = jnp.concatenate([twist(first[:, k * FACTOR : (k + 1) * FACTOR], cos, sin) for k in range(2)], axis=0)
        spec = mm(second, t2_ref[...])
        spec_ref[c] = spec.astype(BF)
        x_real, x_imag = split(spec[:HALF])
        dy_real, dy_imag = split(spec[HALF:])
        group = jnp.concatenate(
            [dy_real * x_real + dy_imag * x_imag, dy_imag * x_real - dy_real * x_imag], axis=1
        ).astype(BF)
        back = untwist(mm(group, t2i_ref[...]), cos, sin)
        out = mm(t1i_ref[...], back) * GRAD_SCALE
        gs_ref[pl.ds(pl.multiple_of(c * CTX, CTX), CTX), :] = flat(out.astype(BF))
        return carry

    lax.fori_loop(0, COLS, body, 0)
    permute_rows(g_ref, gperm_ref, gs_ref)


def backward_kernel(spec_ref, h_ref, perm_ref, t2i_ref, t1i_ref, cos_ref, sin_ref, out_ref, os_ref):
    def body(c, carry):
        cos, sin = cos_ref[...], sin_ref[...]
        spec = spec_ref[c]
        x_real, x_imag = split(spec[:HALF])
        dy_real, dy_imag = split(spec[HALF:])
        h_real, h_imag = split(h_ref[c])
        y = jnp.concatenate([x_real * h_real - x_imag * h_imag, x_real * h_imag + x_imag * h_real], axis=1)
        dx = jnp.concatenate([dy_real * h_real + dy_imag * h_imag, dy_imag * h_real - dy_real * h_imag], axis=1)
        both = jnp.concatenate([y.astype(BF), dx.astype(BF)], axis=0)
        first = mm(both, t2i_ref[...])
        back = jnp.concatenate([untwist(first[s * HALF : (s + 1) * HALF], cos, sin) for s in range(2)], axis=1)
        out = mm(t1i_ref[...], back).astype(BF)
        for s in range(2):
            at = pl.multiple_of(s * HALF + c * CTX, CTX)
            os_ref[pl.ds(at, CTX), :] = flat(out[:, s * FACTOR : (s + 1) * FACTOR])
        return carry

    lax.fori_loop(0, COLS, body, 0)
    permute_rows(out_ref, perm_ref, os_ref)


def place_kernel(r_ref, perm_ref, a_ref, b_ref):
    tn = (((0,), (0,)), ((), ()))
    step = 512
    for at in range(0, TOK, step):
        both = lax.dot_general(r_ref[:, at : at + step], perm_ref[...], tn, preferred_element_type=F32).astype(BF)
        a_ref[at : at + step] = both[:, :HALF]
        b_ref[at : at + step] = both[:, HALF:]


def grad_kernel(r_ref, perm_ref, out_ref):
    tn = (((0,), (0,)), ((), ()))
    step = 512
    for at in range(0, TOK, step):
        out_ref[at : at + step] = lax.dot_general(r_ref[:, at : at + step], perm_ref[...], tn, preferred_element_type=F32)


def call(kernel, outs, scratch, flops, moved, *args):
    return pl.pallas_call(
        kernel,
        out_shape=[jax.ShapeDtypeStruct(*o) for o in outs],
        scratch_shapes=[pltpu.VMEM(*s) for s in scratch],
        compiler_params=pltpu.CompilerParams(vmem_limit_bytes=40 * 1024 * 1024),
        cost_estimate=pl.CostEstimate(flops=flops, bytes_accessed=moved, transcendentals=0),
    )(*args)


def one_hot(index, count):
    out = np.zeros((len(index), count), np.float32)
    out[np.arange(len(index)), index] = 1.0
    return jnp.asarray(out, dtype=BF)


def rows_of(*sizes):
    return np.unravel_index(np.arange(int(np.prod(sizes))), sizes)


def spread_perm():
    d, s, c = rows_of(CTX, 2, COLS)
    return one_hot(s * HALF + d * COLS + c, 2 * HALF)


def arrive_perm():
    s, c, d = rows_of(2, COLS, CTX)
    return one_hot(d * 2 * COLS + s * COLS + c, 2 * HALF)


def leave_perm():
    d, s, c = rows_of(CTX, 2, COLS)
    return one_hot(s * HALF + c * CTX + d, 2 * HALF)


def place_perm():
    d, s, c = rows_of(CTX, 2, COLS)
    return one_hot(s * HALF + d * COLS + c, 2 * HALF)


def relative(sign, my_zh, my_y):
    ky, kzh, c = rows_of(Y, ZH, COLS)
    block = (my_zh + sign * kzh) % ZH * Y + (my_y + sign * ky) % Y
    return block, c


def hot(index):
    return (index[:, None] == jnp.arange(HALF)[None, :]).astype(BF)


def shifted(x, axis, size, k):
    return lax.ppermute(x, axis, [(s, (s + k) % size) for s in range(size)])


def swap(x):
    return lax.ppermute(x, ("ctx", "zh", "y"), [(a * CTX + b, b * CTX + a) for a in range(CTX) for b in range(CTX)])


def gather(x):
    rows = x.shape[0]
    x = jnp.concatenate([x] + [shifted(x, "zh", ZH, k) for k in range(1, ZH)], axis=0)
    return jnp.concatenate([x] + [shifted(x, "y", Y, k) for k in range(1, Y)], axis=0)


def scatter_sum(x):
    for axis, size in (("y", Y), ("zh", ZH)):
        rows = x.shape[0] // size
        parts = [x[:rows]] + [shifted(x[k * rows : (k + 1) * rows], axis, size, k) for k in range(1, size)]
        x = sum(p.astype(F32) for p in parts).astype(BF)
    return x


def local(seq_input, out_grad, filters):
    first, second, back_first, back_last, tw_cos, tw_sin = tables()
    my_zh, my_y = lax.axis_index("zh"), lax.axis_index("y")
    come, c = relative(-1, my_zh, my_y)
    go, _ = relative(1, my_zh, my_y)
    filter_perm = hot(c * CTX + come).T
    leave_grad = hot(c * CTX + go)
    place_grad = hot(come * COLS + c)

    spread, taps = call(
        spread_kernel,
        [((2 * HALF, TOK), BF), ((COLS, TOK), BF)],
        [],
        2 * 256 * 256 * 2048,
        3 << 20,
        seq_input,
        out_grad,
        filters,
        spread_perm(),
        jnp.eye(COLS, dtype=BF),
    )
    arrived = lax.all_to_all(spread.reshape(CTX, 2 * COLS, TOK), "ctx", 0, 0, tiled=True).reshape(2 * HALF, TOK)
    taps = gather(swap(taps))
    (h_spec,) = call(
        filter_kernel,
        [((COLS, HALF, 2 * FACTOR), BF)],
        [((HALF, TOK), BF)],
        2 * 8 * 42 * 10**6,
        3 << 20,
        taps,
        filter_perm,
        first,
        second,
        tw_cos,
        tw_sin,
    )
    spec, grads = call(
        forward_kernel,
        [((COLS, 2 * HALF, 2 * FACTOR), BF), ((HALF, TOK), BF)],
        [((2 * HALF, TOK), BF), ((HALF, TOK), BF)],
        2 * 24 * 42 * 10**6,
        6 << 20,
        arrived,
        arrive_perm(),
        leave_grad,
        first,
        second,
        back_first,
        back_last,
        tw_cos,
        tw_sin,
    )
    (leaving,) = call(
        backward_kernel,
        [((2 * HALF, TOK), BF)],
        [((2 * HALF, TOK), BF)],
        2 * 16 * 42 * 10**6,
        6 << 20,
        spec,
        h_spec,
        leave_perm(),
        back_first,
        back_last,
        tw_cos,
        tw_sin,
    )
    back = lax.all_to_all(leaving.reshape(CTX, 2 * COLS, TOK), "ctx", 0, 0, tiled=True).reshape(2 * HALF, TOK)
    grads = gather(swap(scatter_sum(grads)))
    conv_out, input_grad = call(
        place_kernel,
        [((TOK, HALF), BF), ((TOK, HALF), BF)],
        [],
        2 * 256 * 256 * 2048,
        2 << 20,
        back,
        place_perm(),
    )
    (filter_grad,) = call(
        grad_kernel, [((TOK, HALF), F32)], [], 2 * 128 * 128 * 2048, 2 << 20, grads, place_grad
    )
    return conv_out, input_grad, filter_grad


def solution(mesh):
    inner = Mesh(mesh.devices.reshape(CTX, ZH, Y), ("ctx", "zh", "y"))
    placed = P("ctx", ("zh", "y"))
    return jax.shard_map(
        local,
        mesh=inner,
        in_specs=(placed, placed, placed),
        out_specs=(placed, placed, P("ctx", None)),
        check_vma=False,
    )
```

time: 547 us -> 127 us (0.23)
  the two profiles are of different devices: /device:TPU:1 before, /device:TPU:8 now
where the time goes in v1:
time: 127 us; the launch traced here: 126 us
  starting transfers between devices  77.2 us (61%)
  waiting for transfers between devices  24.4 us (19%)
  Pallas kernels  19 us (15%)
  local copies, waits for them, and re-layouts  4.25 us (3%)
    ppermute x18, starting transfers between devices, shifted(): return lax.ppermute(x, axis, [(s, (s + k) % size) for s in range(size)])  57.3 us
    ppermute x18, waiting for transfers between devices, shifted(): return lax.ppermute(x, axis, [(s, (s + k) % size) for s in range(size)])  20.4 us
    pallas_call x6, Pallas kernels, call(): pl.pallas_call(kernel, out_shape=[jax.ShapeDtypeStruct(*o) for o in outs]...  19 us
    all_to_all x1, starting transfers between devices, local(): lax.all_to_all(leaving.reshape(CTX, 2 * COLS, TOK), 'ctx', 0, 0, tiled=True)  7.11 us
    ppermute x2, starting transfers between devices, swap(): lax.ppermute(x, ('ctx', 'zh', 'y'), [(a * CTX + b, b * CTX + a) for a in...  7.05 us
    all_to_all x1, starting transfers between devices, local(): lax.all_to_all(spread.reshape(CTX, 2 * COLS, TOK), 'ctx', 0, 0, tiled=True)  5.75 us
    unnamed x45, local copies, waits for them, and re-layouts  4.18 us
    ppermute x2, waiting for transfers between devices, swap(): lax.ppermute(x, ('ctx', 'zh', 'y'), [(a * CTX + b, b * CTX + a) for a in...  4.06 us
  transfers between devices with their start and end apart: 22, of which 12 were waited for; matrix products, arithmetic and copies ran while one was open for 0% of the time, Pallas kernels for 13%

profile of v1, /device:TPU:8, one launch (start us, length us, event | category | flops | bytes accessed | tf_op | source)
XLA Modules:
  0.0 126.2 jit_solution(17287117554065633195)
XLA Ops:
  0.6 0.0 copy-start.11
  0.7 0.0 copy-start.12
  0.7 0.0 copy-start.13
  0.7 0.0 copy-start.14
  0.7 0.0 copy-start.15
  0.7 0.0 copy-start.16
  0.7 1.0 copy.23.f_ref
  1.8 0.0 copy-start.1
  1.8 1.0 copy-done.1
  2.8 1.0 copy-done.2
  3.9 0.9 copy-done.3
  4.8 0.0 copy-start.8
  4.8 0.0 copy-start.9
  4.8 0.0 copy-start.10
  4.8 1.4 %shard_map.211 = (bf16[256,2048]{1,0:T(8,128)(2,1)}, bf16[8,2048]{1,0:T(8,128)(2,1)S(1)}) custom-call(bf16[2048,128]{1,0:T(8,128)(2,1)S(1)} %copy-done.1, bf16[2048,128]{1,0:T(8,128)(2,1)S(1)} %copy-done.2, bf16[2048,8]{1,0:T(8,128)(2,1)S(1)} %copy.23.f_ref, bf16[256,256]{1,0:T(8,128)(2,1)S(1)} %copy-done.3, bf16[8,8]{1,0:T(8,128)(2,1)S(1)} %fusion.3.eye_ref), custom_call_target="tpu_custom_call" | custom-call | flops 268435456 | bytes 3145728 | tf_op jit(solution)/shard_map/pallas_call | solution.py:174
  6.3 5.8 %all-to-all-start = ((bf16[16,16,2048]{2,1,0:T(8,128)(2,1)}), bf16[16,16,2048]{2,1,0:T(8,128)(2,1)S(1)}, u32[]{:S(2)}, u32[]{:S(2)}) async-start(bf16[16,16,2048]{2,1,0:T(8,128)(2,1)} %bitcast), calls=%async_computation | async-start | bytes 2097152 | tf_op jit(solution)/shard_map/all_to_all | solution.py:266
  12.0 2.4 %collective-permute-start = (bf16[8,2048]{1,0:T(8,128)(2,1)S(1)}, bf16[8,2048]{1,0:T(8,128)(2,1)S(1)}, u32[]{:S(2)}, u32[]{:S(2)}) collective-permute-start(bf16[8,2048]{1,0:T(8,128)(2,1)S(1)} %get-tuple-element.11), channel_id=1, source_target_pairs={{0,0},{1,16},{2,32},{3,48},{4,64},{5,80},{6,96},{7,112},{8,128},{9... | collective-permute-start | bytes 98312 | tf_op jit(solution)/shard_map/ppermute | solution.py:228
  14.5 0.1 fusion.gperm_ref
  14.6 2.7 %collective-permute-done = bf16[8,2048]{1,0:T(8,128)(2,1)S(1)} collective-permute-done((bf16[8,2048]{1,0:T(8,128)(2,1)S(1)}, bf16[8,2048]{1,0:T(8,128)(2,1)S(1)}, u32[]{:S(2)}, u32[]{:S(2)}) %collective-permute-start) | collective-permute-done | bytes 32800 | tf_op jit(solution)/shard_map/ppermute | solution.py:228
  17.3 13.4 %collective-permute-start.1 = (bf16[8,2048]{1,0:T(8,128)(2,1)S(1)}, bf16[8,2048]{1,0:T(8,128)(2,1)S(1)}, u32[]{:S(2)}, u32[]{:S(2)}) collective-permute-start(bf16[8,2048]{1,0:T(8,128)(2,1)S(1)} %collective-permute-done), channel_id=1, source_target_pairs={{0,4},{4,8},{8,12},{12,0},{1,5},{5,9},{9,13},{13,1},{2,6},{6,10},{... | collective-permute-start | bytes 98312 | tf_op jit(solution)/shard_map/ppermute | solution.py:224
  30.7 4.3 %collective-permute-start.2 = (bf16[8,2048]{1,0:T(8,128)(2,1)S(1)}, bf16[8,2048]{1,0:T(8,128)(2,1)S(1)}, u32[]{:S(2)}, u32[]{:S(2)}) collective-permute-start(bf16[8,2048]{1,0:T(8,128)(2,1)S(1)} %collective-permute-done), channel_id=1, source_target_pairs={{0,8},{4,12},{8,0},{12,4},{1,9},{5,13},{9,1},{13,5},{2,10},{6,14},... | collective-permute-start | bytes 98312 | tf_op jit(solution)/shard_map/ppermute | solution.py:224
  35.0 0.0 collective-permute-start.3
  35.0 0.0 collective-permute-done.1
  35.0 3.5 %collective-permute-done.2 = bf16[8,2048]{1,0:T(8,128)(2,1)S(1)} collective-permute-done((bf16[8,2048]{1,0:T(8,128)(2,1)S(1)}, bf16[8,2048]{1,0:T(8,128)(2,1)S(1)}, u32[]{:S(2)}, u32[]{:S(2)}) %collective-permute-start.2) | collective-permute-done | bytes 32800 | tf_op jit(solution)/shard_map/ppermute | solution.py:224
  38.5 1.3 %collective-permute-done.3 = bf16[8,2048]{1,0:T(8,128)(2,1)S(1)} collective-permute-done((bf16[8,2048]{1,0:T(8,128)(2,1)S(1)}, bf16[8,2048]{1,0:T(8,128)(2,1)S(1)}, u32[]{:S(2)}, u32[]{:S(2)}) %collective-permute-start.3) | collective-permute-done | bytes 32800 | tf_op jit(solution)/shard_map/ppermute | solution.py:224
  39.8 2.0 %collective-permute-start.4 = (bf16[32,2048]{1,0:T(8,128)(2,1)S(1)}, bf16[32,2048]{1,0:T(8,128)(2,1)S(1)}, u32[]{:S(2)}, u32[]{:S(2)}) collective-permute-start(bf16[32,2048]{1,0:T(8,128)(2,1)S(1)} %get-tuple-element.31), channel_id=1, source_target_pairs={{0,1},{1,2},{2,3},{3,0},{4,5},{5,6},{6,7},{7,4},{8,9},{9,10},{10,1... | collective-permute-start | bytes 393224 | tf_op jit(solution)/shard_map/ppermute | solution.py:224
  41.8 1.4 %collective-permute-start.5 = (bf16[32,2048]{1,0:T(8,128)(2,1)S(1)}, bf16[32,2048]{1,0:T(8,128)(2,1)S(1)}, u32[]{:S(2)}, u32[]{:S(2)}) collective-permute-start(bf16[32,2048]{1,0:T(8,128)(2,1)S(1)} %get-tuple-element.31), channel_id=1, source_target_pairs={{0,2},{1,3},{2,0},{3,1},{4,6},{5,7},{6,4},{7,5},{8,10},{9,11},{10,... | collective-permute-start | bytes 393224 | tf_op jit(solution)/shard_map/ppermute | solution.py:224
  43.3 1.2 collective-permute-start.6
  44.5 2.7 %collective-permute-done.4 = bf16[32,2048]{1,0:T(8,128)(2,1)S(1)} collective-permute-done((bf16[32,2048]{1,0:T(8,128)(2,1)S(1)}, bf16[32,2048]{1,0:T(8,128)(2,1)S(1)}, u32[]{:S(2)}, u32[]{:S(2)}) %collective-permute-start.4) | collective-permute-done | bytes 131104 | tf_op jit(solution)/shard_map/ppermute | solution.py:224
  47.2 1.4 %collective-permute-done.5 = bf16[32,2048]{1,0:T(8,128)(2,1)S(1)} collective-permute-done((bf16[32,2048]{1,0:T(8,128)(2,1)S(1)}, bf16[32,2048]{1,0:T(8,128)(2,1)S(1)}, u32[]{:S(2)}, u32[]{:S(2)}) %collective-permute-start.5) | collective-permute-done | bytes 131104 | tf_op jit(solution)/shard_map/ppermute | solution.py:224
  48.6 0.0 all-to-all-done
  48.6 7.2 %shard_map.212 = (bf16[8,256,512]{2,1,0:T(8,128)(2,1)S(1)}, bf16[128,2048]{1,0:T(8,128)(2,1)S(1)}) custom-call(bf16[256,2048]{1,0:T(8,128)(2,1)S(1)} %bitcast.5, bf16[256,256]{1,0:T(8,128)(2,1)S(1)} %copy-done.5, bf16[128,128]{1,0:T(8,128)(2,1)S(1)} %fusion.gperm_ref, bf16[256,128]{1,0:T(8,128)(2,1)S(1)} %copy-done.10, bf16[512,512]{1,0:T(8,128)(2,1)S(1)} %copy-done.9, ...), custom_call_target="tpu_custom_call" | custom-call | flops 2016000000 | bytes 6291456 | tf_op jit(solution)/shard_map/pallas_call | solution.py:174
  55.9 2.0 %collective-permute-start.9 = (bf16[32,2048]{1,0:T(8,128)(2,1)S(1)}, bf16[32,2048]{1,0:T(8,128)(2,1)S(1)}, u32[]{:S(2)}, u32[]{:S(2)}) collective-permute-start(bf16[32,2048]{1,0:T(8,128)(2,1)S(1)} %get-tuple-element.18), channel_id=1, source_target_pairs={{0,3},{1,0},{2,1},{3,2},{4,7},{5,4},{6,5},{7,6},{8,11},{9,8},{10,9... | collective-permute-start | bytes 393224 | tf_op jit(solution)/shard_map/ppermute | solution.py:224
  57.9 0.6 collective-permute-start.8
  58.5 2.3 %collective-permute-start.7 = (bf16[32,2048]{1,0:T(8,128)(2,1)S(1)}, bf16[32,2048]{1,0:T(8,128)(2,1)S(1)}, u32[]{:S(2)}, u32[]{:S(2)}) collective-permute-start(bf16[32,2048]{1,0:T(8,128)(2,1)S(1)} %get-tuple-element.17), channel_id=1, source_target_pairs={{0,1},{1,2},{2,3},{3,0},{4,5},{5,6},{6,7},{7,4},{8,9},{9,10},{10,1... | collective-permute-start | bytes 393224 | tf_op jit(solution)/shard_map/ppermute | solution.py:224
  60.8 0.0 collective-permute-done.6
  60.9 2.2 %shard_map.213.h_ref = bf16[8,128,512]{2,1,0:T(8,128)(2,1)S(1)} custom-call(bf16[128,2048]{1,0:T(8,128)(2,1)S(1)} %constant_dynamic-update-slice_fusion.4.r_ref, bf16[128,128]{1,0:T(8,128)(2,1)S(1)} %fusion.1.perm_ref, bf16[256,128]{1,0:T(8,128)(2,1)S(1)} %copy-done.10, bf16[512,512]{1,0:T(8,128)(2,1)S(1)} %copy-done.9, f32[128,256]{1,0:T(8,128)S(1)} %copy-done.6, ...), custom_call_target="tpu_custom_call" | custom-call | flops 672000000 | bytes 3145728 | tf_op jit(solution)/shard_map/pallas_call | solution.py:174
  63.0 0.0 collective-permute-done.9
  63.1 1.3 %collective-permute-done.8 = bf16[32,2048]{1,0:T(8,128)(2,1)S(1)} collective-permute-done((bf16[32,2048]{1,0:T(8,128)(2,1)S(1)}, bf16[32,2048]{1,0:T(8,128)(2,1)S(1)}, u32[]{:S(2)}, u32[]{:S(2)}) %collective-permute-start.8) | collective-permute-done | bytes 131104 | tf_op jit(solution)/shard_map/ppermute | solution.py:224
  64.4 0.0 collective-permute-done.7
  64.4 0.1 add_convert_fusion
  64.5 2.4 %collective-permute-start.12 = (bf16[8,2048]{1,0:T(8,128)(2,1)S(1)}, bf16[8,2048]{1,0:T(8,128)(2,1)S(1)}, u32[]{:S(2)}, u32[]{:S(2)}) collective-permute-start(bf16[8,2048]{1,0:T(8,128)(2,1)S(1)} %get-tuple-element.21), channel_id=1, source_target_pairs={{0,12},{4,0},{8,4},{12,8},{1,13},{5,1},{9,5},{13,9},{2,14},{6,2},{... | collective-permute-start | bytes 98312 | tf_op jit(solution)/shard_map/ppermute | solution.py:224
  66.9 2.6 %collective-permute-start.11 = (bf16[8,2048]{1,0:T(8,128)(2,1)S(1)}, bf16[8,2048]{1,0:T(8,128)(2,1)S(1)}, u32[]{:S(2)}, u32[]{:S(2)}) collective-permute-start(bf16[8,2048]{1,0:T(8,128)(2,1)S(1)} %get-tuple-element.22), channel_id=1, source_target_pairs={{0,8},{4,12},{8,0},{12,4},{1,9},{5,13},{9,1},{13,5},{2,10},{6,14},... | collective-permute-start | bytes 98312 | tf_op jit(solution)/shard_map/ppermute | solution.py:224
  69.6 1.4 %collective-permute-start.10 = (bf16[8,2048]{1,0:T(8,128)(2,1)S(1)}, bf16[8,2048]{1,0:T(8,128)(2,1)S(1)}, u32[]{:S(2)}, u32[]{:S(2)}) collective-permute-start(bf16[8,2048]{1,0:T(8,128)(2,1)S(1)} %get-tuple-element.20), channel_id=1, source_target_pairs={{0,4},{4,8},{8,12},{12,0},{1,5},{5,9},{9,13},{13,1},{2,6},{6,10},{... | collective-permute-start | bytes 98312 | tf_op jit(solution)/shard_map/ppermute | solution.py:224
  71.0 5.3 %shard_map.214 = bf16[256,2048]{1,0:T(8,128)(2,1)} custom-call(bf16[8,256,512]{2,1,0:T(8,128)(2,1)S(1)} %get-tuple-element.10.spec_ref, bf16[8,128,512]{2,1,0:T(8,128)(2,1)S(1)} %shard_map.213.h_ref, bf16[256,256]{1,0:T(8,128)(2,1)S(1)} %copy-done.5, bf16[512,512]{1,0:T(8,128)(2,1)S(1)} %copy-done, bf16[128,256]{1,0:T(8,128)(2,1)S(1)} %copy-done.8, ...), custom_call_target="tpu_custom_call" | custom-call | flops 1344000000 | bytes 6291456 | tf_op jit(solution)/shard_map/pallas_call | solution.py:174
  76.3 7.1 %all-to-all-start.1 = ((bf16[16,16,2048]{2,1,0:T(8,128)(2,1)}), bf16[16,16,2048]{2,1,0:T(8,128)(2,1)S(1)}, u32[]{:S(2)}, u32[]{:S(2)}) async-start(bf16[16,16,2048]{2,1,0:T(8,128)(2,1)} %bitcast.2), calls=%async_computation.1 | async-start | bytes 2097152 | tf_op jit(solution)/shard_map/all_to_all | solution.py:311
  83.4 0.0 collective-permute-done.12
  83.4 0.0 collective-permute-done.10
  83.5 4.7 %collective-permute-start.13 = (bf16[8,2048]{1,0:T(8,128)(2,1)S(1)}, bf16[8,2048]{1,0:T(8,128)(2,1)S(1)}, u32[]{:S(2)}, u32[]{:S(2)}) collective-permute-start(bf16[8,2048]{1,0:T(8,128)(2,1)S(1)} %add_convert_fusion.1), channel_id=1, source_target_pairs={{0,0},{1,16},{2,32},{3,48},{4,64},{5,80},{6,96},{7,112},{8,128},{9... | collective-permute-start | bytes 98312 | tf_op jit(solution)/shard_map/ppermute | solution.py:228
  88.2 1.4 %collective-permute-done.13 = bf16[8,2048]{1,0:T(8,128)(2,1)S(1)} collective-permute-done((bf16[8,2048]{1,0:T(8,128)(2,1)S(1)}, bf16[8,2048]{1,0:T(8,128)(2,1)S(1)}, u32[]{:S(2)}, u32[]{:S(2)}) %collective-permute-start.13) | collective-permute-done | bytes 32800 | tf_op jit(solution)/shard_map/ppermute | solution.py:228
  89.6 14.5 %collective-permute-start.14 = (bf16[8,2048]{1,0:T(8,128)(2,1)S(1)}, bf16[8,2048]{1,0:T(8,128)(2,1)S(1)}, u32[]{:S(2)}, u32[]{:S(2)}) collective-permute-start(bf16[8,2048]{1,0:T(8,128)(2,1)S(1)} %collective-permute-done.13), channel_id=1, source_target_pairs={{0,4},{4,8},{8,12},{12,0},{1,5},{5,9},{9,13},{13,1},{2,6},{6,10},{... | collective-permute-start | bytes 98312 | tf_op jit(solution)/shard_map/ppermute | solution.py:224
  104.1 4.5 %collective-permute-start.15 = (bf16[8,2048]{1,0:T(8,128)(2,1)S(1)}, bf16[8,2048]{1,0:T(8,128)(2,1)S(1)}, u32[]{:S(2)}, u32[]{:S(2)}) collective-permute-start(bf16[8,2048]{1,0:T(8,128)(2,1)S(1)} %collective-permute-done.13), channel_id=1, source_target_pairs={{0,8},{4,12},{8,0},{12,4},{1,9},{5,13},{9,1},{13,5},{2,10},{6,14},... | collective-permute-start | bytes 98312 | tf_op jit(solution)/shard_map/ppermute | solution.py:224
  108.6 3.3 %collective-permute-done.15 = bf16[8,2048]{1,0:T(8,128)(2,1)S(1)} collective-permute-done((bf16[8,2048]{1,0:T(8,128)(2,1)S(1)}, bf16[8,2048]{1,0:T(8,128)(2,1)S(1)}, u32[]{:S(2)}, u32[]{:S(2)}) %collective-permute-start.15) | collective-permute-done | bytes 32800 | tf_op jit(solution)/shard_map/ppermute | solution.py:224
  111.9 1.5 %collective-permute-done.16 = bf16[8,2048]{1,0:T(8,128)(2,1)S(1)} collective-permute-done((bf16[8,2048]{1,0:T(8,128)(2,1)S(1)}, bf16[8,2048]{1,0:T(8,128)(2,1)S(1)}, u32[]{:S(2)}, u32[]{:S(2)}) %collective-permute-start.16) | collective-permute-done | bytes 32800 | tf_op jit(solution)/shard_map/ppermute | solution.py:224
  113.4 1.9 %collective-permute-start.17 = (bf16[32,2048]{1,0:T(8,128)(2,1)S(1)}, bf16[32,2048]{1,0:T(8,128)(2,1)S(1)}, u32[]{:S(2)}, u32[]{:S(2)}) collective-permute-start(bf16[32,2048]{1,0:T(8,128)(2,1)S(1)} %get-tuple-element.23), channel_id=1, source_target_pairs={{0,1},{1,2},{2,3},{3,0},{4,5},{5,6},{6,7},{7,4},{8,9},{9,10},{10,1... | collective-permute-start | bytes 393224 | tf_op jit(solution)/shard_map/ppermute | solution.py:224
  115.4 0.1 fusion.2.perm_ref
  115.4 1.7 %collective-permute-start.18 = (bf16[32,2048]{1,0:T(8,128)(2,1)S(1)}, bf16[32,2048]{1,0:T(8,128)(2,1)S(1)}, u32[]{:S(2)}, u32[]{:S(2)}) collective-permute-start(bf16[32,2048]{1,0:T(8,128)(2,1)S(1)} %get-tuple-element.23), channel_id=1, source_target_pairs={{0,2},{1,3},{2,0},{3,1},{4,6},{5,7},{6,4},{7,5},{8,10},{9,11},{10,... | collective-permute-start | bytes 393224 | tf_op jit(solution)/shard_map/ppermute | solution.py:224
  117.1 0.9 collective-permute-start.19
  118.0 0.4 collective-permute-done.17
  118.4 3.7 %collective-permute-done.18 = bf16[32,2048]{1,0:T(8,128)(2,1)S(1)} collective-permute-done((bf16[32,2048]{1,0:T(8,128)(2,1)S(1)}, bf16[32,2048]{1,0:T(8,128)(2,1)S(1)}, u32[]{:S(2)}, u32[]{:S(2)}) %collective-permute-start.18) | collective-permute-done | bytes 131104 | tf_op jit(solution)/shard_map/ppermute | solution.py:224
  122.1 1.3 %collective-permute-done.19 = bf16[32,2048]{1,0:T(8,128)(2,1)S(1)} collective-permute-done((bf16[32,2048]{1,0:T(8,128)(2,1)S(1)}, bf16[32,2048]{1,0:T(8,128)(2,1)S(1)}, u32[]{:S(2)}, u32[]{:S(2)}) %collective-permute-start.19) | collective-permute-done | bytes 131104 | tf_op jit(solution)/shard_map/ppermute | solution.py:224
  123.4 1.3 %shard_map.216 = f32[2048,128]{1,0:T(8,128)} custom-call(bf16[128,2048]{1,0:T(8,128)(2,1)S(1)} %constant_dynamic-update-slice_fusion.15.r_ref, bf16[128,128]{1,0:T(8,128)(2,1)S(1)} %fusion.2.perm_ref), custom_call_target="tpu_custom_call" | custom-call | flops 67108864 | bytes 2097152 | tf_op jit(solution)/shard_map/pallas_call | solution.py:174
  124.7 0.0 all-to-all-done.1
  124.7 1.5 %shard_map.215 = (bf16[2048,128]{1,0:T(8,128)(2,1)}, bf16[2048,128]{1,0:T(8,128)(2,1)}) custom-call(bf16[256,2048]{1,0:T(8,128)(2,1)S(1)} %bitcast.4, bf16[256,256]{1,0:T(8,128)(2,1)S(1)} %copy-done.4), custom_call_target="tpu_custom_call" | custom-call | flops 268435456 | bytes 2097152 | tf_op jit(solution)/shard_map/pallas_call | solution.py:174
  (45 shorter events, 0.3 us)
Async XLA Ops:
  0.6 13.8 %copy-start.11 = (s32[128]{0:T(128)S(1)}, s32[128]{0:T(128)}, u32[]{:S(2)}) copy-start(s32[128]{0:T(128)} %constant.79.clone) | copy-start | bytes 1540
  0.7 13.8 %copy-start.12 = (s32[128]{0:T(128)S(1)}, s32[128]{0:T(128)}, u32[]{:S(2)}) copy-start(s32[128]{0:T(128)} %constant.75.clone) | copy-start | bytes 1540
  0.7 13.8 %copy-start.13 = (s32[128]{0:T(128)S(1)}, s32[128]{0:T(128)}, u32[]{:S(2)}) copy-start(s32[128]{0:T(128)} %constant.74.clone) | copy-start | bytes 1540
  0.7 13.8 %copy-start.14 = (s32[128]{0:T(128)S(1)}, s32[128]{0:T(128)}, u32[]{:S(2)}) copy-start(s32[128]{0:T(128)} %constant.78.clone) | copy-start | bytes 1540
  0.7 13.8 %copy-start.15 = (s32[128]{0:T(128)S(1)}, s32[128]{0:T(128)}, u32[]{:S(2)}) copy-start(s32[128]{0:T(128)} %constant.77.clone) | copy-start | bytes 1540
  0.7 13.8 %copy-start.16 = (s32[128]{0:T(128)S(1)}, s32[128]{0:T(128)}, u32[]{:S(2)}) copy-start(s32[128]{0:T(128)} %constant.76.clone) | copy-start | bytes 1540
  1.8 1.0 copy-start.1
  2.8 1.0 copy-start.2
  3.9 0.9 copy-start.3
  4.8 43.8 %copy-start = (bf16[512,512]{1,0:T(8,128)(2,1)S(1)}, bf16[512,512]{1,0:T(8,128)(2,1)}, u32[]{:S(2)}) copy-start(bf16[512,512]{1,0:T(8,128)(2,1)} %constant.70.clone.t2i_ref) | copy-start | bytes 1572868
  4.8 43.8 %copy-start.5 = (bf16[256,256]{1,0:T(8,128)(2,1)S(1)}, bf16[256,256]{1,0:T(8,128)(2,1)}, u32[]{:S(2)}) copy-start(bf16[256,256]{1,0:T(8,128)(2,1)} %constant.81.clone.perm_ref) | copy-start | bytes 393220
  4.8 43.8 %copy-start.6 = (f32[128,256]{1,0:T(8,128)S(1)}, f32[128,256]{1,0:T(8,128)}, u32[]{:S(2)}) copy-start(f32[128,256]{1,0:T(8,128)} %constant.72.clone.cos_ref) | copy-start | bytes 393220
  4.8 43.8 %copy-start.7 = (f32[128,256]{1,0:T(8,128)S(1)}, f32[128,256]{1,0:T(8,128)}, u32[]{:S(2)}) copy-start(f32[128,256]{1,0:T(8,128)} %constant.73.clone.sin_ref) | copy-start | bytes 393220
  4.8 43.8 %copy-start.8 = (bf16[128,256]{1,0:T(8,128)(2,1)S(1)}, bf16[128,256]{1,0:T(8,128)(2,1)}, u32[]{:S(2)}) copy-start(bf16[128,256]{1,0:T(8,128)(2,1)} %constant.71.clone.t1i_ref) | copy-start | bytes 196612
  4.8 43.8 %copy-start.9 = (bf16[512,512]{1,0:T(8,128)(2,1)S(1)}, bf16[512,512]{1,0:T(8,128)(2,1)}, u32[]{:S(2)}) copy-start(bf16[512,512]{1,0:T(8,128)(2,1)} %constant.69.clone.t2_ref) | copy-start | bytes 1572868
  4.8 43.8 %copy-start.10 = (bf16[256,128]{1,0:T(8,128)(2,1)S(1)}, bf16[256,128]{1,0:T(8,128)(2,1)}, u32[]{:S(2)}) copy-start(bf16[256,128]{1,0:T(8,128)(2,1)} %constant.68.clone.t1_ref) | copy-start | bytes 196612
  6.3 42.3 %all-to-all-start = ((bf16[16,16,2048]{2,1,0:T(8,128)(2,1)}), bf16[16,16,2048]{2,1,0:T(8,128)(2,1)S(1)}, u32[]{:S(2)}, u32[]{:S(2)}) async-start(bf16[16,16,2048]{2,1,0:T(8,128)(2,1)} %bitcast), calls=%async_computation | async-start | bytes 2097152 | tf_op jit(solution)/shard_map/all_to_all | solution.py:266
  12.0 5.2 %collective-permute-start = (bf16[8,2048]{1,0:T(8,128)(2,1)S(1)}, bf16[8,2048]{1,0:T(8,128)(2,1)S(1)}, u32[]{:S(2)}, u32[]{:S(2)}) collective-permute-start(bf16[8,2048]{1,0:T(8,128)(2,1)S(1)} %get-tuple-element.11), channel_id=1, source_target_pairs={{0,0},{1,16},{2,32},{3,48},{4,64},{5,80},{6,96},{7,112},{8,128},{9... | collective-permute-start | bytes 98312 | tf_op jit(solution)/shard_map/ppermute | solution.py:228
  17.3 17.7 %collective-permute-start.1 = (bf16[8,2048]{1,0:T(8,128)(2,1)S(1)}, bf16[8,2048]{1,0:T(8,128)(2,1)S(1)}, u32[]{:S(2)}, u32[]{:S(2)}) collective-permute-start(bf16[8,2048]{1,0:T(8,128)(2,1)S(1)} %collective-permute-done), channel_id=1, source_target_pairs={{0,4},{4,8},{8,12},{12,0},{1,5},{5,9},{9,13},{13,1},{2,6},{6,10},{... | collective-permute-start | bytes 98312 | tf_op jit(solution)/shard_map/ppermute | solution.py:224
  30.7 7.8 %collective-permute-start.2 = (bf16[8,2048]{1,0:T(8,128)(2,1)S(1)}, bf16[8,2048]{1,0:T(8,128)(2,1)S(1)}, u32[]{:S(2)}, u32[]{:S(2)}) collective-permute-start(bf16[8,2048]{1,0:T(8,128)(2,1)S(1)} %collective-permute-done), channel_id=1, source_target_pairs={{0,8},{4,12},{8,0},{12,4},{1,9},{5,13},{9,1},{13,5},{2,10},{6,14},... | collective-permute-start | bytes 98312 | tf_op jit(solution)/shard_map/ppermute | solution.py:224
  35.0 4.8 %collective-permute-start.3 = (bf16[8,2048]{1,0:T(8,128)(2,1)S(1)}, bf16[8,2048]{1,0:T(8,128)(2,1)S(1)}, u32[]{:S(2)}, u32[]{:S(2)}) collective-permute-start(bf16[8,2048]{1,0:T(8,128)(2,1)S(1)} %collective-permute-done), channel_id=1, source_target_pairs={{0,12},{4,0},{8,4},{12,8},{1,13},{5,1},{9,5},{13,9},{2,14},{6,2},{... | collective-permute-start | bytes 98312 | tf_op jit(solution)/shard_map/ppermute | solution.py:224
  39.8 7.3 %collective-permute-start.4 = (bf16[32,2048]{1,0:T(8,128)(2,1)S(1)}, bf16[32,2048]{1,0:T(8,128)(2,1)S(1)}, u32[]{:S(2)}, u32[]{:S(2)}) collective-permute-start(bf16[32,2048]{1,0:T(8,128)(2,1)S(1)} %get-tuple-element.31), channel_id=1, source_target_pairs={{0,1},{1,2},{2,3},{3,0},{4,5},{5,6},{6,7},{7,4},{8,9},{9,10},{10,1... | collective-permute-start | bytes 393224 | tf_op jit(solution)/shard_map/ppermute | solution.py:224
  41.8 6.7 %collective-permute-start.5 = (bf16[32,2048]{1,0:T(8,128)(2,1)S(1)}, bf16[32,2048]{1,0:T(8,128)(2,1)S(1)}, u32[]{:S(2)}, u32[]{:S(2)}) collective-permute-start(bf16[32,2048]{1,0:T(8,128)(2,1)S(1)} %get-tuple-element.31), channel_id=1, source_target_pairs={{0,2},{1,3},{2,0},{3,1},{4,6},{5,7},{6,4},{7,5},{8,10},{9,11},{10,... | collective-permute-start | bytes 393224 | tf_op jit(solution)/shard_map/ppermute | solution.py:224
  43.3 17.6 %collective-permute-start.6 = (bf16[32,2048]{1,0:T(8,128)(2,1)S(1)}, bf16[32,2048]{1,0:T(8,128)(2,1)S(1)}, u32[]{:S(2)}, u32[]{:S(2)}) collective-permute-start(bf16[32,2048]{1,0:T(8,128)(2,1)S(1)} %get-tuple-element.31), channel_id=1, source_target_pairs={{0,3},{1,0},{2,1},{3,2},{4,7},{5,4},{6,5},{7,6},{8,11},{9,8},{10,9... | collective-permute-start | bytes 393224 | tf_op jit(solution)/shard_map/ppermute | solution.py:224
  55.9 7.1 %collective-permute-start.9 = (bf16[32,2048]{1,0:T(8,128)(2,1)S(1)}, bf16[32,2048]{1,0:T(8,128)(2,1)S(1)}, u32[]{:S(2)}, u32[]{:S(2)}) collective-permute-start(bf16[32,2048]{1,0:T(8,128)(2,1)S(1)} %get-tuple-element.18), channel_id=1, source_target_pairs={{0,3},{1,0},{2,1},{3,2},{4,7},{5,4},{6,5},{7,6},{8,11},{9,8},{10,9... | collective-permute-start | bytes 393224 | tf_op jit(solution)/shard_map/ppermute | solution.py:224
  57.9 6.5 %collective-permute-start.8 = (bf16[32,2048]{1,0:T(8,128)(2,1)S(1)}, bf16[32,2048]{1,0:T(8,128)(2,1)S(1)}, u32[]{:S(2)}, u32[]{:S(2)}) collective-permute-start(bf16[32,2048]{1,0:T(8,128)(2,1)S(1)} %get-tuple-element.19), channel_id=1, source_target_pairs={{0,2},{1,3},{2,0},{3,1},{4,6},{5,7},{6,4},{7,5},{8,10},{9,11},{10,... | collective-permute-start | bytes 393224 | tf_op jit(solution)/shard_map/ppermute | solution.py:224
  58.5 5.9 %collective-permute-start.7 = (bf16[32,2048]{1,0:T(8,128)(2,1)S(1)}, bf16[32,2048]{1,0:T(8,128)(2,1)S(1)}, u32[]{:S(2)}, u32[]{:S(2)}) collective-permute-start(bf16[32,2048]{1,0:T(8,128)(2,1)S(1)} %get-tuple-element.17), channel_id=1, source_target_pairs={{0,1},{1,2},{2,3},{3,0},{4,5},{5,6},{6,7},{7,4},{8,9},{9,10},{10,1... | collective-permute-start | bytes 393224 | tf_op jit(solution)/shard_map/ppermute | solution.py:224
  64.5 18.9 %collective-permute-start.12 = (bf16[8,2048]{1,0:T(8,128)(2,1)S(1)}, bf16[8,2048]{1,0:T(8,128)(2,1)S(1)}, u32[]{:S(2)}, u32[]{:S(2)}) collective-permute-start(bf16[8,2048]{1,0:T(8,128)(2,1)S(1)} %get-tuple-element.21), channel_id=1, source_target_pairs={{0,12},{4,0},{8,4},{12,8},{1,13},{5,1},{9,5},{13,9},{2,14},{6,2},{... | collective-permute-start | bytes 98312 | tf_op jit(solution)/shard_map/ppermute | solution.py:224
  66.9 16.5 %collective-permute-start.11 = (bf16[8,2048]{1,0:T(8,128)(2,1)S(1)}, bf16[8,2048]{1,0:T(8,128)(2,1)S(1)}, u32[]{:S(2)}, u32[]{:S(2)}) collective-permute-start(bf16[8,2048]{1,0:T(8,128)(2,1)S(1)} %get-tuple-element.22), channel_id=1, source_target_pairs={{0,8},{4,12},{8,0},{12,4},{1,9},{5,13},{9,1},{13,5},{2,10},{6,14},... | collective-permute-start | bytes 98312 | tf_op jit(solution)/shard_map/ppermute | solution.py:224
  69.6 13.9 %collective-permute-start.10 = (bf16[8,2048]{1,0:T(8,128)(2,1)S(1)}, bf16[8,2048]{1,0:T(8,128)(2,1)S(1)}, u32[]{:S(2)}, u32[]{:S(2)}) collective-permute-start(bf16[8,2048]{1,0:T(8,128)(2,1)S(1)} %get-tuple-element.20), channel_id=1, source_target_pairs={{0,4},{4,8},{8,12},{12,0},{1,5},{5,9},{9,13},{13,1},{2,6},{6,10},{... | collective-permute-start | bytes 98312 | tf_op jit(solution)/shard_map/ppermute | solution.py:224
  76.3 48.4 %copy-start.4 = (bf16[256,256]{1,0:T(8,128)(2,1)S(1)}, bf16[256,256]{1,0:T(8,128)(2,1)}, u32[]{:S(2)}) copy-start(bf16[256,256]{1,0:T(8,128)(2,1)} %constant.80.clone.perm_ref) | copy-start | bytes 393220
  76.3 48.4 %all-to-all-start.1 = ((bf16[16,16,2048]{2,1,0:T(8,128)(2,1)}), bf16[16,16,2048]{2,1,0:T(8,128)(2,1)S(1)}, u32[]{:S(2)}, u32[]{:S(2)}) async-start(bf16[16,16,2048]{2,1,0:T(8,128)(2,1)} %bitcast.2), calls=%async_computation.1 | async-start | bytes 2097152 | tf_op jit(solution)/shard_map/all_to_all | solution.py:311
  83.5 6.1 %collective-permute-start.13 = (bf16[8,2048]{1,0:T(8,128)(2,1)S(1)}, bf16[8,2048]{1,0:T(8,128)(2,1)S(1)}, u32[]{:S(2)}, u32[]{:S(2)}) collective-permute-start(bf16[8,2048]{1,0:T(8,128)(2,1)S(1)} %add_convert_fusion.1), channel_id=1, source_target_pairs={{0,0},{1,16},{2,32},{3,48},{4,64},{5,80},{6,96},{7,112},{8,128},{9... | collective-permute-start | bytes 98312 | tf_op jit(solution)/shard_map/ppermute | solution.py:228
  89.6 19.0 %collective-permute-start.14 = (bf16[8,2048]{1,0:T(8,128)(2,1)S(1)}, bf16[8,2048]{1,0:T(8,128)(2,1)S(1)}, u32[]{:S(2)}, u32[]{:S(2)}) collective-permute-start(bf16[8,2048]{1,0:T(8,128)(2,1)S(1)} %collective-permute-done.13), channel_id=1, source_target_pairs={{0,4},{4,8},{8,12},{12,0},{1,5},{5,9},{9,13},{13,1},{2,6},{6,10},{... | collective-permute-start | bytes 98312 | tf_op jit(solution)/shard_map/ppermute | solution.py:224
  104.1 7.8 %collective-permute-start.15 = (bf16[8,2048]{1,0:T(8,128)(2,1)S(1)}, bf16[8,2048]{1,0:T(8,128)(2,1)S(1)}, u32[]{:S(2)}, u32[]{:S(2)}) collective-permute-start(bf16[8,2048]{1,0:T(8,128)(2,1)S(1)} %collective-permute-done.13), channel_id=1, source_target_pairs={{0,8},{4,12},{8,0},{12,4},{1,9},{5,13},{9,1},{13,5},{2,10},{6,14},... | collective-permute-start | bytes 98312 | tf_op jit(solution)/shard_map/ppermute | solution.py:224
  108.6 4.8 %collective-permute-start.16 = (bf16[8,2048]{1,0:T(8,128)(2,1)S(1)}, bf16[8,2048]{1,0:T(8,128)(2,1)S(1)}, u32[]{:S(2)}, u32[]{:S(2)}) collective-permute-start(bf16[8,2048]{1,0:T(8,128)(2,1)S(1)} %collective-permute-done.13), channel_id=1, source_target_pairs={{0,12},{4,0},{8,4},{12,8},{1,13},{5,1},{9,5},{13,9},{2,14},{6,2},{... | collective-permute-start | bytes 98312 | tf_op jit(solution)/shard_map/ppermute | solution.py:224
  113.4 5.0 %collective-permute-start.17 = (bf16[32,2048]{1,0:T(8,128)(2,1)S(1)}, bf16[32,2048]{1,0:T(8,128)(2,1)S(1)}, u32[]{:S(2)}, u32[]{:S(2)}) collective-permute-start(bf16[32,2048]{1,0:T(8,128)(2,1)S(1)} %get-tuple-element.23), channel_id=1, source_target_pairs={{0,1},{1,2},{2,3},{3,0},{4,5},{5,6},{6,7},{7,4},{8,9},{9,10},{10,1... | collective-permute-start | bytes 393224 | tf_op jit(solution)/shard_map/ppermute | solution.py:224
  115.4 6.7 %collective-permute-start.18 = (bf16[32,2048]{1,0:T(8,128)(2,1)S(1)}, bf16[32,2048]{1,0:T(8,128)(2,1)S(1)}, u32[]{:S(2)}, u32[]{:S(2)}) collective-permute-start(bf16[32,2048]{1,0:T(8,128)(2,1)S(1)} %get-tuple-element.23), channel_id=1, source_target_pairs={{0,2},{1,3},{2,0},{3,1},{4,6},{5,7},{6,4},{7,5},{8,10},{9,11},{10,... | collective-permute-start | bytes 393224 | tf_op jit(solution)/shard_map/ppermute | solution.py:224
  117.1 6.3 %collective-permute-start.19 = (bf16[32,2048]{1,0:T(8,128)(2,1)S(1)}, bf16[32,2048]{1,0:T(8,128)(2,1)S(1)}, u32[]{:S(2)}, u32[]{:S(2)}) collective-permute-start(bf16[32,2048]{1,0:T(8,128)(2,1)S(1)} %get-tuple-element.23), channel_id=1, source_target_pairs={{0,3},{1,0},{2,1},{3,2},{4,7},{5,4},{6,5},{7,6},{8,11},{9,8},{10,9... | collective-permute-start | bytes 393224 | tf_op jit(solution)/shard_map/ppermute | solution.py:224

commit v2 on v1

v2 whole, which is shorter than its diff:
```python
import math

import jax
import jax.numpy as jnp
import numpy as np
from jax import lax
from jax.experimental import pallas as pl
from jax.experimental.pallas import tpu as pltpu
from jax.sharding import Mesh
from jax.sharding import PartitionSpec as P

BF = jnp.bfloat16
F32 = jnp.float32
FACTOR = 256
HALF = 128
FULL = FACTOR * FACTOR
CTX = 16
SUB = HALF // CTX
TOK = SUB * FACTOR
COLS = 8
PAIR = 2
ZH = 4
Y = 4
STEP = 512
LARGE = 60 * 1024 * 1024
GRAD_SCALE = 1.0 / math.sqrt(524288)


def unit(product, modulus):
    angles = np.float32(2.0 * math.pi / modulus) * (product % modulus).astype(np.float32)
    return np.cos(angles).astype(np.float32), np.sin(angles).astype(np.float32)


def tables():
    row = np.arange(HALF)
    n1 = (row % CTX) * SUB + row // CTX
    k1 = np.arange(HALF)
    n2 = np.arange(FACTOR)
    cos1, sin1 = unit((2 * k1[:, None] + 1) * n1[None, :], 2 * FACTOR)
    cos2, sin2 = unit(n2[:, None] * n2[None, :], FACTOR)
    tw_cos, tw_sin = unit((2 * k1[:, None] + 1) * n2[None, :], 2 * FULL)
    first = np.concatenate([cos1, -sin1], 0)
    second = np.block([[cos2, -sin2], [sin2, cos2]])
    back_last = np.concatenate([cos1.T, -sin1.T], 1) * np.float32(2.0 / FULL)
    back_plain = back_last.reshape(SUB, CTX, FACTOR).transpose(1, 0, 2).reshape(HALF, FACTOR)
    half = lambda a: jnp.asarray(a, dtype=BF)
    return half(first), half(second), half(back_last), half(back_plain), jnp.asarray(tw_cos), jnp.asarray(tw_sin)


def mm(a, b):
    return jnp.dot(a, b, preferred_element_type=F32)


def column(rows):
    return jnp.concatenate([rows[:, k * FACTOR : (k + 1) * FACTOR] for k in range(SUB)], axis=0)


def flat(block):
    return jnp.concatenate([block[k * CTX : (k + 1) * CTX] for k in range(SUB)], axis=1)


def permute_rows(dst, perm, src):
    for at in range(0, TOK, STEP):
        dst[:, at : at + STEP] = mm(perm, src[:, at : at + STEP]).astype(BF)


def sends(row_of):
    row = lax.broadcasted_iota(jnp.int32, (FACTOR, FACTOR), 0)
    col = lax.broadcasted_iota(jnp.int32, (FACTOR, FACTOR), 1)
    return (col == row_of(row)).astype(F32).astype(BF)


def by_block(r):
    return ((r >> 3) & 1) * HALF + (r >> 4) * COLS + (r & 7)


def turned(r):
    return (r & 15) * CTX + (r >> 4)


def to_subs(r):
    return (r & 31) * SUB + (r >> 5)


def twist(first, cos, sin):
    real, imag = first[:HALF], first[HALF:]
    return jnp.concatenate([real * cos + imag * sin, imag * cos - real * sin], axis=1).astype(BF)


def untwist(first, cos, sin):
    real, imag = first[:, :FACTOR], first[:, FACTOR:]
    return jnp.concatenate([real * cos + imag * sin, real * sin - imag * cos], axis=0).astype(BF)


def split(spec):
    return spec[:, :FACTOR].astype(F32), spec[:, FACTOR:].astype(F32)


def spread_kernel(x_ref, dy_ref, out_ref, held, put, in_sems, out_sems):
    nt = (((1,), (1,)), ((), ()))
    chunks = [pl.ds(at, STEP) for at in range(0, TOK, STEP)]
    takes = []
    for k, chunk in enumerate(chunks):
        for s, ref in enumerate((x_ref, dy_ref)):
            take = pltpu.make_async_copy(
                ref.at[chunk], held.at[chunk, pl.ds(s * HALF, HALF)], in_sems.at[2 * k + s]
            )
            take.start()
            takes.append(take)
    perm = sends(by_block)
    gives = []
    for k, chunk in enumerate(chunks):
        takes[2 * k].wait()
        takes[2 * k + 1].wait()
        put[:, chunk] = lax.dot_general(perm, held[chunk], nt, preferred_element_type=F32).astype(BF)
        give = pltpu.make_async_copy(put.at[:, chunk], out_ref.at[:, chunk], out_sems.at[k])
        give.start()
        gives.append(give)
    for give in gives:
        give.wait()


def filter_kernel(a_ref, b_ref, c_ref, d_ref, perm_ref, t1_ref, t2_ref, cos_ref, sin_ref, spec_ref, rp_ref):
    permute_rows(rp_ref, perm_ref[...], jnp.concatenate([r[...] for r in (a_ref, b_ref, c_ref, d_ref)], axis=0))

    def body(at, carry):
        cos, sin = cos_ref[...], sin_ref[...]
        parts = []
        for k in range(4):
            rows = rp_ref[pl.ds(pl.multiple_of((at * 4 + k) * CTX, CTX), CTX), :]
            parts.append(column(rows))
        first = mm(t1_ref[...], jnp.concatenate(parts, axis=1))
        second = jnp.concatenate([twist(first[:, k * FACTOR : (k + 1) * FACTOR], cos, sin) for k in range(4)], axis=0)
        spec = mm(second, t2_ref[...]).astype(BF)
        for k in range(4):
            spec_ref[at * 4 + k] = spec[k * HALF : (k + 1) * HALF]
        return carry

    lax.fori_loop(0, COLS // 4, body, 0)


def forward_kernel(r_ref, t1_ref, t2_ref, t1g_ref, cos_ref, sin_ref, spec_ref, g_ref, rp_ref):
    permute_rows(rp_ref, sends(turned), r_ref)

    def body(pair, carry):
        cos, sin = cos_ref[...], sin_ref[...]
        parts = []
        for k in range(PAIR):
            for s in range(2):
                at = pl.multiple_of(s * HALF + (pair * PAIR + k) * CTX, CTX)
                parts.append(column(rp_ref[pl.ds(at, CTX), :]))
        first = mm(t1_ref[...], jnp.concatenate(parts, axis=1))
        second = jnp.concatenate(
            [twist(first[:, k * FACTOR : (k + 1) * FACTOR], cos, sin) for k in range(2 * PAIR)], axis=0
        )
        spec = mm(second, t2_ref[...])
        groups = []
        for k in range(PAIR):
            both = spec[k * 2 * HALF : (k + 1) * 2 * HALF]
            spec_ref[pair * PAIR + k] = both.astype(BF)
            x_real, x_imag = split(both[:HALF])
            dy_real, dy_imag = split(both[HALF:])
            groups.append(
                jnp.concatenate(
                    [dy_real * x_real + dy_imag * x_imag, dy_real * x_imag - dy_imag * x_real], axis=1
                ).astype(BF)
            )
        back = mm(jnp.concatenate(groups, axis=0), t2_ref[...])
        back = jnp.concatenate([untwist(back[k * HALF : (k + 1) * HALF], cos, sin) for k in range(PAIR)], axis=1)
        out = mm(t1g_ref[...], back) * GRAD_SCALE
        for d in range(CTX):
            rows = [out[d * SUB : (d + 1) * SUB, k * FACTOR : (k + 1) * FACTOR] for k in range(PAIR)]
            g_ref[d * Y + pair] = jnp.concatenate(rows, axis=0).astype(BF)
        return carry

    lax.fori_loop(0, COLS // PAIR, body, 0)


def backward_kernel(spec_ref, h_ref, t2_ref, t1i_ref, cos_ref, sin_ref, out_ref, os_ref):
    def body(pair, carry):
        cos, sin = cos_ref[...], sin_ref[...]
        parts = []
        for k in range(PAIR):
            spec = spec_ref[pair * PAIR + k]
            x_real, x_imag = split(spec[:HALF])
            dy_real, dy_imag = split(spec[HALF:])
            h_real, h_imag = split(h_ref[pair * PAIR + k])
            y = [x_real * h_real - x_imag * h_imag, -(x_real * h_imag + x_imag * h_real)]
            dx = [dy_real * h_real + dy_imag * h_imag, dy_real * h_imag - dy_imag * h_real]
            parts += [jnp.concatenate(y, axis=1).astype(BF), jnp.concatenate(dx, axis=1).astype(BF)]
        first = mm(jnp.concatenate(parts, axis=0), t2_ref[...])
        back = jnp.concatenate(
            [untwist(first[k * HALF : (k + 1) * HALF], cos, sin) for k in range(2 * PAIR)], axis=1
        )
        out = mm(t1i_ref[...], back).astype(BF)
        for k in range(PAIR):
            for s in range(2):
                at = pl.multiple_of(s * HALF + (pair * PAIR + k) * CTX, CTX)
                lane = (2 * k + s) * FACTOR
                os_ref[pl.ds(at, CTX), :] = flat(out[:, lane : lane + FACTOR])
        return carry

    lax.fori_loop(0, COLS // PAIR, body, 0)
    permute_rows(out_ref, sends(turned), os_ref)


def place_kernel(r_ref, a_ref, b_ref, put, sems):
    tn = (((0,), (0,)), ((), ()))
    perm = sends(by_block)
    gives = []
    for k in range(TOK // STEP):
        chunk = pl.ds(k * STEP, STEP)
        both = lax.dot_general(r_ref[:, k * STEP : (k + 1) * STEP], perm, tn, preferred_element_type=F32).astype(BF)
        for s, ref in enumerate((a_ref, b_ref)):
            put[s, chunk] = both[:, s * HALF : (s + 1) * HALF]
            give = pltpu.make_async_copy(put.at[s, chunk], ref.at[chunk], sems.at[2 * k + s])
            give.start()
            gives.append(give)
    for give in gives:
        give.wait()


def grad_kernel(a_ref, b_ref, c_ref, d_ref, perm_ref, out_ref, put, sems):
    tn = (((0,), (0,)), ((), ()))
    sort = sends(to_subs)
    blocks = [mm(sort, r[...]).astype(BF) for r in (a_ref, b_ref, c_ref, d_ref)]
    rows = CTX * PAIR
    gives = []
    for n in range(SUB):
        chunk = pl.ds(n * FACTOR, FACTOR)
        part = jnp.concatenate([block[n * rows : (n + 1) * rows] for block in blocks], axis=0)
        put[chunk] = lax.dot_general(part, perm_ref[...], tn, preferred_element_type=F32)
        give = pltpu.make_async_copy(put.at[chunk], out_ref.at[chunk], sems.at[n])
        give.start()
        gives.append(give)
    for give in gives:
        give.wait()


def call(kernel, outs, scratch, flops, moved, *args, ins=None, space=pltpu.VMEM, limit=40 * 1024 * 1024):
    return pl.pallas_call(
        kernel,
        in_specs=[pl.BlockSpec(memory_space=ins or pltpu.VMEM)] * len(args),
        out_specs=[pl.BlockSpec(memory_space=space)] * len(outs),
        out_shape=[jax.ShapeDtypeStruct(*o) for o in outs],
        scratch_shapes=scratch,
        compiler_params=pltpu.CompilerParams(vmem_limit_bytes=limit),
        cost_estimate=pl.CostEstimate(flops=flops, bytes_accessed=moved, transcendentals=0),
    )(*args)


def rows_of(*sizes):
    return np.unravel_index(np.arange(int(np.prod(sizes))), sizes)


def hot(index):
    return (index[:, None] == jnp.arange(HALF)[None, :]).astype(BF)


def shifted(x, axis, size, k):
    return lax.ppermute(x, axis, [(s, (s + k) % size) for s in range(size)])


def swap(x):
    return lax.ppermute(x, ("ctx", "zh", "y"), [(a * CTX + b, b * CTX + a) for a in range(CTX) for b in range(CTX)])


def arrivals(x, axis, size):
    return [x] + [shifted(x, axis, size, k) for k in range(1, size)]


def added(parts):
    a, b, c, d = (p.astype(F32) for p in parts)
    return ((a + c) + (b + d)).astype(BF)


def local(seq_input, out_grad, filters):
    first, second, back_last, back_plain, tw_cos, tw_sin = tables()
    my_zh, my_y = lax.axis_index("zh"), lax.axis_index("y")
    ky, kzh, c = rows_of(Y, ZH, COLS)
    filter_perm = hot(c * CTX + (my_zh - kzh) % ZH * Y + (my_y - ky) % Y).T
    ky, i, c = rows_of(Y, CTX, PAIR)
    place_grad = hot(i * COLS + (my_y - ky) % Y * PAIR + c)

    taps = swap(filters.T)
    (spread,) = call(
        spread_kernel,
        [((FACTOR, TOK), BF)],
        [
            pltpu.VMEM((TOK, FACTOR), BF),
            pltpu.VMEM((FACTOR, TOK), BF),
            pltpu.SemaphoreType.DMA((2 * TOK // STEP,)),
            pltpu.SemaphoreType.DMA((TOK // STEP,)),
        ],
        2 * 256 * 256 * 2048,
        2 << 20,
        seq_input,
        out_grad,
        ins=pl.ANY,
        space=pl.ANY,
        limit=LARGE,
    )
    arrived = lax.all_to_all(spread.reshape(CTX, 2 * COLS, TOK), "ctx", 0, 0, tiled=True).reshape(2 * HALF, TOK)
    spec, grads = call(
        forward_kernel,
        [((COLS, 2 * HALF, 2 * FACTOR), BF), ((CTX * Y, CTX, FACTOR), BF)],
        [pltpu.VMEM((2 * HALF, TOK), BF)],
        2 * 24 * 42 * 10**6,
        6 << 20,
        arrived,
        first,
        second,
        back_plain,
        tw_cos,
        tw_sin,
    )
    spec, grads, taps = lax.optimization_barrier((spec, grads, taps))
    taps = arrivals(taps, "zh", ZH)
    taps = arrivals(jnp.concatenate(taps, axis=0), "y", Y)
    (h_spec,) = call(
        filter_kernel,
        [((COLS, HALF, 2 * FACTOR), BF)],
        [pltpu.VMEM((HALF, TOK), BF)],
        2 * 8 * 42 * 10**6,
        3 << 20,
        *taps,
        filter_perm,
        first,
        second,
        tw_cos,
        tw_sin,
    )
    grads = lax.all_to_all(grads, ("ctx", "y"), 0, 0, tiled=True).reshape(CTX, Y, CTX, FACTOR)
    grads = jnp.sum(grads.astype(F32), axis=1).astype(BF).reshape(FACTOR, FACTOR)
    (leaving,) = call(
        backward_kernel,
        [((2 * HALF, TOK), BF)],
        [pltpu.VMEM((2 * HALF, TOK), BF)],
        2 * 16 * 42 * 10**6,
        6 << 20,
        spec,
        h_spec,
        second,
        back_last,
        tw_cos,
        tw_sin,
    )
    grads = added(arrivals(grads, "zh", ZH))
    grads, leaving = lax.optimization_barrier((grads, leaving))
    back = lax.all_to_all(leaving.reshape(CTX, 2 * COLS, TOK), "ctx", 0, 0, tiled=True).reshape(2 * HALF, TOK)
    grads = arrivals(grads, "y", Y)
    conv_out, input_grad = call(
        place_kernel,
        [((TOK, HALF), BF), ((TOK, HALF), BF)],
        [pltpu.VMEM((2, TOK, HALF), BF), pltpu.SemaphoreType.DMA((2 * TOK // STEP,))],
        2 * 256 * 256 * 2048,
        2 << 20,
        back,
        space=pl.ANY,
    )
    (filter_grad,) = call(
        grad_kernel,
        [((TOK, HALF), F32)],
        [pltpu.VMEM((TOK, HALF), F32), pltpu.SemaphoreType.DMA((SUB,))],
        2 * 256 * 256 * 1024,
        2 << 20,
        *grads,
        place_grad,
        space=pl.ANY,
    )
    return conv_out, input_grad, filter_grad


def solution(mesh):
    inner = Mesh(mesh.devices.reshape(CTX, ZH, Y), ("ctx", "zh", "y"))
    placed = P("ctx", ("zh", "y"))
    return jax.shard_map(
        local,
        mesh=inner,
        in_specs=(placed, placed, placed),
        out_specs=(placed, placed, P("ctx", None)),
        check_vma=False,
    )
```

time: 127 us -> 103 us (0.81)
  the two profiles are of different devices: /device:TPU:8 before, /device:TPU:1 now
where the time goes in v2:
time: 103 us
  starting transfers between devices  49.6 us (48%)
  waiting for transfers between devices  30.2 us (29%)
  Pallas kernels  16 us (16%)
  local copies, waits for them, and re-layouts  4.57 us (4%)
  other arithmetic  1.32 us (1%)
    ppermute x12, starting transfers between devices, shifted(): return lax.ppermute(x, axis, [(s, (s + k) % size) for s in range(size)])  20.7 us
    pallas_call x6, Pallas kernels, call(): pl.pallas_call(kernel, in_specs=[pl.BlockSpec(memory_space=ins or pltpu.V...  16 us
    all_to_all x1, waiting for transfers between devices, local(): lax.all_to_all(spread.reshape(CTX, 2 * COLS, TOK), 'ctx', 0, 0, tiled=True)  12.5 us
    ppermute x12, waiting for transfers between devices, shifted(): return lax.ppermute(x, axis, [(s, (s + k) % size) for s in range(size)])  12.5 us
    all_to_all x1, starting transfers between devices, local(): lax.all_to_all(leaving.reshape(CTX, 2 * COLS, TOK), 'ctx', 0, 0, tiled=True)  10.3 us
    all_to_all x1, starting transfers between devices, local(): lax.all_to_all(grads, ('ctx', 'y'), 0, 0, tiled=True)  8.26 us
    all_to_all x1, starting transfers between devices, local(): lax.all_to_all(spread.reshape(CTX, 2 * COLS, TOK), 'ctx', 0, 0, tiled=True)  7.19 us
    all_to_all x1, waiting for transfers between devices, local(): lax.all_to_all(leaving.reshape(CTX, 2 * COLS, TOK), 'ctx', 0, 0, tiled=True)  5.07 us
  transfers between devices with their start and end apart: 16, of which 7 were waited for; matrix products, arithmetic and copies ran while one was open for 2% of the time, Pallas kernels for 11%

profile of v2, /device:TPU:1, one launch (start us, length us, event | category | flops | bytes accessed | tf_op | source)
XLA Modules:
  0.0 102.5 jit_solution(14328698664266356914)
XLA Ops:
  0.6 0.0 copy-start.12
  0.6 0.0 copy-start.13
  0.7 0.0 copy-start.10
  0.7 0.0 copy-start.11
  0.7 0.0 copy-start.4
  0.7 0.0 copy-start.5
  0.7 0.0 copy-start.7
  0.7 0.0 copy-start.9
  0.7 2.9 %shard_map.166 = bf16[256,2048]{1,0:T(8,128)(2,1)} custom-call(bf16[2048,128]{1,0:T(8,128)(2,1)} %x_ref.1, bf16[2048,128]{1,0:T(8,128)(2,1)} %dy_ref.1), custom_call_target="tpu_custom_call" | custom-call | flops 268435456 | bytes 2097152 | tf_op jit(solution)/shard_map/pallas_call | solution.py:241
  3.7 7.2 %all-to-all-start = ((bf16[16,16,2048]{2,1,0:T(8,128)(2,1)}), bf16[16,16,2048]{2,1,0:T(8,128)(2,1)S(1)}, u32[]{:S(2)}, u32[]{:S(2)}) async-start(bf16[16,16,2048]{2,1,0:T(8,128)(2,1)} %bitcast.11), calls=%async_computation | async-start | bytes 2097152 | tf_op jit(solution)/shard_map/all_to_all | solution.py:303
  10.8 3.2 %collective-permute-start = (bf16[8,2048]{1,0:T(8,128)(2,1)}, bf16[8,2048]{1,0:T(8,128)(2,1)}, u32[]{:S(2)}, u32[]{:S(2)}) collective-permute-start(bf16[8,2048]{1,0:T(8,128)(2,1)} %bitcast.2), channel_id=1, source_target_pairs={{0,0},{1,16},{2,32},{3,48},{4,64},{5,80},{6,96},{7,112},{8,128},{9... | collective-permute-start | bytes 98312 | tf_op jit(solution)/shard_map/ppermute | solution.py:265
  14.0 0.0 copy-done.12
  14.1 0.0 copy-done.13
  14.1 0.0 copy-done.10
  14.1 0.0 copy-done.11
  14.1 12.5 %all-to-all-done = bf16[16,16,2048]{2,1,0:T(8,128)(2,1)S(1)} async-done(((bf16[16,16,2048]{2,1,0:T(8,128)(2,1)}), bf16[16,16,2048]{2,1,0:T(8,128)(2,1)S(1)}, u32[]{:S(2)}, u32[]{:S(2)}) %all-to-all-start) | async-done | bytes 1048608 | tf_op jit(solution)/shard_map/all_to_all | solution.py:303
  26.7 0.0 copy-done.4
  26.7 0.0 copy-done.5
  26.7 0.0 copy-done.7
  26.7 0.0 copy-done.9
  26.7 0.0 copy-start
  26.7 1.0 %copy-done = bf16[512,512]{1,0:T(8,128)(2,1)S(1)} copy-done((bf16[512,512]{1,0:T(8,128)(2,1)S(1)}, bf16[512,512]{1,0:T(8,128)(2,1)}, u32[]{:S(2)}) %copy-start) | copy-done | bytes 524312
  27.7 4.6 %shard_map.167 = (bf16[8,256,512]{2,1,0:T(8,128)(2,1)S(1)}, bf16[64,16,256]{2,1,0:T(8,128)(2,1)S(1)}) custom-call(bf16[256,2048]{1,0:T(8,128)(2,1)S(1)} %bitcast.10, bf16[256,128]{1,0:T(8,128)(2,1)S(1)} %copy-done.7, bf16[512,512]{1,0:T(8,128)(2,1)S(1)} %copy-done, bf16[128,256]{1,0:T(8,128)(2,1)S(1)} %copy-done.9, f32[128,256]{1,0:T(8,128)S(1)} %copy-done.4, ...), custom_call_target="tpu_custom_call" | custom-call | flops 2016000000 | bytes 6291456 | tf_op jit(solution)/shard_map/pallas_call | solution.py:241
  32.4 0.0 copy-start.3
  32.4 0.8 copy-done.3
  33.2 0.0 collective-permute-done
  33.2 8.3 %all-to-all-start.1 = ((bf16[64,16,256]{2,1,0:T(8,128)(2,1)}), bf16[64,16,256]{2,1,0:T(8,128)(2,1)}, u32[]{:S(2)}, u32[]{:S(2)}) async-start(bf16[64,16,256]{2,1,0:T(8,128)(2,1)} %copy-done.3), calls=%async_computation.1 | async-start | bytes 1048576 | tf_op jit(solution)/shard_map/all_to_all | solution.py:333
  41.5 2.6 %collective-permute-start.4 = (bf16[8,2048]{1,0:T(8,128)(2,1)}, bf16[8,2048]{1,0:T(8,128)(2,1)S(1)}, u32[]{:S(2)}, u32[]{:S(2)}) collective-permute-start(bf16[8,2048]{1,0:T(8,128)(2,1)} %collective-permute-done), channel_id=1, source_target_pairs={{0,4},{4,8},{8,12},{12,0},{1,5},{5,9},{9,13},{13,1},{2,6},{6,10},{... | collective-permute-start | bytes 98312 | tf_op jit(solution)/shard_map/ppermute | solution.py:261
  44.1 0.8 constant_dynamic-update-slice_fusion.3
  44.8 4.1 %collective-permute-start.5 = (bf16[8,2048]{1,0:T(8,128)(2,1)}, bf16[8,2048]{1,0:T(8,128)(2,1)S(1)}, u32[]{:S(2)}, u32[]{:S(2)}) collective-permute-start(bf16[8,2048]{1,0:T(8,128)(2,1)} %collective-permute-done), channel_id=1, source_target_pairs={{0,8},{4,12},{8,0},{12,4},{1,9},{5,13},{9,1},{13,5},{2,10},{6,14},... | collective-permute-start | bytes 98312 | tf_op jit(solution)/shard_map/ppermute | solution.py:261
  49.0 2.5 %collective-permute-start.6 = (bf16[8,2048]{1,0:T(8,128)(2,1)}, bf16[8,2048]{1,0:T(8,128)(2,1)S(1)}, u32[]{:S(2)}, u32[]{:S(2)}) collective-permute-start(bf16[8,2048]{1,0:T(8,128)(2,1)} %collective-permute-done), channel_id=1, source_target_pairs={{0,12},{4,0},{8,4},{12,8},{1,13},{5,1},{9,5},{13,9},{2,14},{6,2},{... | collective-permute-start | bytes 98312 | tf_op jit(solution)/shard_map/ppermute | solution.py:261
  51.4 2.1 %collective-permute-done.4 = bf16[8,2048]{1,0:T(8,128)(2,1)S(1)} collective-permute-done((bf16[8,2048]{1,0:T(8,128)(2,1)}, bf16[8,2048]{1,0:T(8,128)(2,1)S(1)}, u32[]{:S(2)}, u32[]{:S(2)}) %collective-permute-start.4) | collective-permute-done | bytes 32800 | tf_op jit(solution)/shard_map/ppermute | solution.py:261
  53.6 2.0 %collective-permute-done.5 = bf16[8,2048]{1,0:T(8,128)(2,1)S(1)} collective-permute-done((bf16[8,2048]{1,0:T(8,128)(2,1)}, bf16[8,2048]{1,0:T(8,128)(2,1)S(1)}, u32[]{:S(2)}, u32[]{:S(2)}) %collective-permute-start.5) | collective-permute-done | bytes 32800 | tf_op jit(solution)/shard_map/ppermute | solution.py:261
  55.6 0.0 collective-permute-done.6
  55.6 1.4 %collective-permute-start.7 = (bf16[32,2048]{1,0:T(8,128)(2,1)S(1)}, bf16[32,2048]{1,0:T(8,128)(2,1)S(1)}, u32[]{:S(2)}, u32[]{:S(2)}) collective-permute-start(bf16[32,2048]{1,0:T(8,128)(2,1)S(1)} %constant_dynamic-update-slice_fusion.a_ref), channel_id=1, source_target_pairs={{0,1},{1,2},{2,3},{3,0},{4,5},{5,6},{6,7},{7,4},{8,9},{9,10},{10,1... | collective-permute-start | bytes 393224 | tf_op jit(solution)/shard_map/ppermute | solution.py:261
  57.0 2.4 %collective-permute-start.8 = (bf16[32,2048]{1,0:T(8,128)(2,1)S(1)}, bf16[32,2048]{1,0:T(8,128)(2,1)S(1)}, u32[]{:S(2)}, u32[]{:S(2)}) collective-permute-start(bf16[32,2048]{1,0:T(8,128)(2,1)S(1)} %constant_dynamic-update-slice_fusion.a_ref), channel_id=1, source_target_pairs={{0,2},{1,3},{2,0},{3,1},{4,6},{5,7},{6,4},{7,5},{8,10},{9,11},{10,... | collective-permute-start | bytes 393224 | tf_op jit(solution)/shard_map/ppermute | solution.py:261
  59.4 1.2 %collective-permute-start.9 = (bf16[32,2048]{1,0:T(8,128)(2,1)S(1)}, bf16[32,2048]{1,0:T(8,128)(2,1)S(1)}, u32[]{:S(2)}, u32[]{:S(2)}) collective-permute-start(bf16[32,2048]{1,0:T(8,128)(2,1)S(1)} %constant_dynamic-update-slice_fusion.a_ref), channel_id=1, source_target_pairs={{0,3},{1,0},{2,1},{3,2},{4,7},{5,4},{6,5},{7,6},{8,11},{9,8},{10,9... | collective-permute-start | bytes 393224 | tf_op jit(solution)/shard_map/ppermute | solution.py:261
  60.6 0.0 all-to-all-done.1
  60.6 1.1 %bitcast_reduce_fusion = bf16[16,16,256]{2,1,0:T(8,128)(2,1)S(1)} fusion(bf16[64,16,256]{2,1,0:T(8,128)(2,1)} %all-to-all-done.1), kind=kLoop, calls=%fused_computation | loop fusion | flops 196608 | bytes 655360 | tf_op jit(solution)/shard_map/reduce_sum | solution.py:334
  61.7 1.3 %collective-permute-start.3 = (bf16[256,256]{1,0:T(8,128)(2,1)S(1)}, bf16[256,256]{1,0:T(8,128)(2,1)S(1)}, u32[]{:S(2)}, u32[]{:S(2)}) collective-permute-start(bf16[256,256]{1,0:T(8,128)(2,1)S(1)} %bitcast.12), channel_id=1, source_target_pairs={{0,12},{4,0},{8,4},{12,8},{1,13},{5,1},{9,5},{13,9},{2,14},{6,2},{... | collective-permute-start | bytes 393224 | tf_op jit(solution)/shard_map/ppermute | solution.py:261
  63.0 1.1 %collective-permute-start.2 = (bf16[256,256]{1,0:T(8,128)(2,1)S(1)}, bf16[256,256]{1,0:T(8,128)(2,1)S(1)}, u32[]{:S(2)}, u32[]{:S(2)}) collective-permute-start(bf16[256,256]{1,0:T(8,128)(2,1)S(1)} %bitcast.13), channel_id=1, source_target_pairs={{0,4},{4,8},{8,12},{12,0},{1,5},{5,9},{9,13},{13,1},{2,6},{6,10},{... | collective-permute-start | bytes 393224 | tf_op jit(solution)/shard_map/ppermute | solution.py:261
  64.1 0.0 collective-permute-done.7.b_ref
  64.1 1.3 %collective-permute-start.1 = (bf16[256,256]{1,0:T(8,128)(2,1)S(1)}, bf16[256,256]{1,0:T(8,128)(2,1)S(1)}, u32[]{:S(2)}, u32[]{:S(2)}) collective-permute-start(bf16[256,256]{1,0:T(8,128)(2,1)S(1)} %bitcast.14), channel_id=1, source_target_pairs={{0,8},{4,12},{8,0},{12,4},{1,9},{5,13},{9,1},{13,5},{2,10},{6,14},... | collective-permute-start | bytes 393224 | tf_op jit(solution)/shard_map/ppermute | solution.py:261
  65.5 0.0 collective-permute-done.8.c_ref
  65.5 0.0 collective-permute-done.9.d_ref
  65.5 1.0 %copy-done.1 = bf16[512,512]{1,0:T(8,128)(2,1)S(1)} copy-done((bf16[512,512]{1,0:T(8,128)(2,1)S(1)}, bf16[512,512]{1,0:T(8,128)(2,1)}, u32[]{:S(2)}) %copy-start.1) | copy-done | bytes 524312
  66.5 0.8 copy-done.8
  67.4 1.7 %shard_map.168.h_ref = bf16[8,128,512]{2,1,0:T(8,128)(2,1)S(1)} custom-call(bf16[32,2048]{1,0:T(8,128)(2,1)S(1)} %constant_dynamic-update-slice_fusion.a_ref, bf16[32,2048]{1,0:T(8,128)(2,1)S(1)} %collective-permute-done.7.b_ref, bf16[32,2048]{1,0:T(8,128)(2,1)S(1)} %collective-permute-done.8.c_ref, bf16[32,2048]{1,0:T(8,128)(2,1)S(1)} %collective-permute-done.9.d_ref, ...), custom_call_target="tpu_custom_call" | custom-call | flops 672000000 | bytes 3145728 | tf_op jit(solution)/shard_map/pallas_call | solution.py:241
  69.1 3.9 %shard_map.169 = bf16[256,2048]{1,0:T(8,128)(2,1)} custom-call(bf16[8,256,512]{2,1,0:T(8,128)(2,1)S(1)} %get-tuple-element.15.spec_ref, bf16[8,128,512]{2,1,0:T(8,128)(2,1)S(1)} %shard_map.168.h_ref, bf16[512,512]{1,0:T(8,128)(2,1)S(1)} %copy-done.2, bf16[128,256]{1,0:T(8,128)(2,1)S(1)} %copy-done.6, f32[128,256]{1,0:T(8,128)S(1)} %copy-done.4, ...), custom_call_target="tpu_custom_call" | custom-call | flops 1344000000 | bytes 6291456 | tf_op jit(solution)/shard_map/pallas_call | solution.py:241
  73.0 0.0 collective-permute-done.3
  73.0 0.0 collective-permute-done.2
  73.0 2.0 %collective-permute-done.1 = bf16[256,256]{1,0:T(8,128)(2,1)S(1)} collective-permute-done((bf16[256,256]{1,0:T(8,128)(2,1)S(1)}, bf16[256,256]{1,0:T(8,128)(2,1)S(1)}, u32[]{:S(2)}, u32[]{:S(2)}) %collective-permute-start.1) | collective-permute-done | bytes 131104 | tf_op jit(solution)/shard_map/ppermute | solution.py:261
  75.0 0.1 add_convert_fusion.a_ref
  75.1 10.3 %all-to-all-start.2 = ((bf16[16,16,2048]{2,1,0:T(8,128)(2,1)}), bf16[16,16,2048]{2,1,0:T(8,128)(2,1)S(1)}, u32[]{:S(2)}, u32[]{:S(2)}) async-start(bf16[16,16,2048]{2,1,0:T(8,128)(2,1)} %bitcast.5), calls=%async_computation.2 | async-start | bytes 2097152 | tf_op jit(solution)/shard_map/all_to_all | solution.py:350
  85.4 0.3 collective-permute-start.10
  85.6 1.2 %collective-permute-start.11 = (bf16[256,256]{1,0:T(8,128)(2,1)S(1)}, bf16[256,256]{1,0:T(8,128)(2,1)S(1)}, u32[]{:S(2)}, u32[]{:S(2)}) collective-permute-start(bf16[256,256]{1,0:T(8,128)(2,1)S(1)} %add_convert_fusion.a_ref), channel_id=1, source_target_pairs={{0,2},{1,3},{2,0},{3,1},{4,6},{5,7},{6,4},{7,5},{8,10},{9,11},{10,... | collective-permute-start | bytes 393224 | tf_op jit(solution)/shard_map/ppermute | solution.py:261
  86.8 1.3 %collective-permute-start.12 = (bf16[256,256]{1,0:T(8,128)(2,1)S(1)}, bf16[256,256]{1,0:T(8,128)(2,1)S(1)}, u32[]{:S(2)}, u32[]{:S(2)}) collective-permute-start(bf16[256,256]{1,0:T(8,128)(2,1)S(1)} %add_convert_fusion.a_ref), channel_id=1, source_target_pairs={{0,3},{1,0},{2,1},{3,2},{4,7},{5,4},{6,5},{7,6},{8,11},{9,8},{10,9... | collective-permute-start | bytes 393224 | tf_op jit(solution)/shard_map/ppermute | solution.py:261
  88.1 0.1 fusion.1.perm_ref
  88.2 6.1 %collective-permute-done.10.b_ref = bf16[256,256]{1,0:T(8,128)(2,1)S(1)} collective-permute-done((bf16[256,256]{1,0:T(8,128)(2,1)S(1)}, bf16[256,256]{1,0:T(8,128)(2,1)S(1)}, u32[]{:S(2)}, u32[]{:S(2)}) %collective-permute-start.10) | collective-permute-done | bytes 131104 | tf_op jit(solution)/shard_map/ppermute | solution.py:261
  94.3 0.0 collective-permute-done.11.c_ref
  94.3 0.3 collective-permute-done.12.d_ref
  94.6 1.5 %shard_map.171 = f32[2048,128]{1,0:T(8,128)} custom-call(bf16[256,256]{1,0:T(8,128)(2,1)S(1)} %add_convert_fusion.a_ref, bf16[256,256]{1,0:T(8,128)(2,1)S(1)} %collective-permute-done.10.b_ref, bf16[256,256]{1,0:T(8,128)(2,1)S(1)} %collective-permute-done.11.c_ref, bf16[256,256]{1,0:T(8,128)(2,1)S(1)} %collective-permute-done.12.d_ref, ...), custom_call_target="tpu_custom_call" | custom-call | flops 134217728 | bytes 2097152 | tf_op jit(solution)/shard_map/pallas_call | solution.py:241
  96.1 5.1 %all-to-all-done.2 = bf16[16,16,2048]{2,1,0:T(8,128)(2,1)S(1)} async-done(((bf16[16,16,2048]{2,1,0:T(8,128)(2,1)}), bf16[16,16,2048]{2,1,0:T(8,128)(2,1)S(1)}, u32[]{:S(2)}, u32[]{:S(2)}) %all-to-all-start.2) | async-done | bytes 1048608 | tf_op jit(solution)/shard_map/all_to_all | solution.py:350
  101.2 1.4 %shard_map.170 = (bf16[2048,128]{1,0:T(8,128)(2,1)}, bf16[2048,128]{1,0:T(8,128)(2,1)}) custom-call(bf16[256,2048]{1,0:T(8,128)(2,1)S(1)} %bitcast.9), custom_call_target="tpu_custom_call" | custom-call | flops 268435456 | bytes 2097152 | tf_op jit(solution)/shard_map/pallas_call | solution.py:241
  (12 shorter events, 0.1 us)
Async XLA Ops:
  0.6 13.4 %copy-start.12 = (s32[128]{0:T(128)S(1)}, s32[128]{0:T(128)}, u32[]{:S(2)}) copy-start(s32[128]{0:T(128)} %constant.74) | copy-start | bytes 1540
  0.6 13.4 %copy-start.13 = (s32[128]{0:T(128)S(1)}, s32[128]{0:T(128)}, u32[]{:S(2)}) copy-start(s32[128]{0:T(128)} %constant.73) | copy-start | bytes 1540
  0.7 13.4 %copy-start.10 = (s32[128]{0:T(128)S(1)}, s32[128]{0:T(128)}, u32[]{:S(2)}) copy-start(s32[128]{0:T(128)} %constant.67.clone) | copy-start | bytes 1540
  0.7 13.4 %copy-start.11 = (s32[128]{0:T(128)S(1)}, s32[128]{0:T(128)}, u32[]{:S(2)}) copy-start(s32[128]{0:T(128)} %constant.72) | copy-start | bytes 1540
  0.7 26.0 %copy-start.4 = (f32[128,256]{1,0:T(8,128)S(1)}, f32[128,256]{1,0:T(8,128)}, u32[]{:S(2)}) copy-start(f32[128,256]{1,0:T(8,128)} %constant.64.clone.cos_ref) | copy-start | bytes 393220
  0.7 26.0 %copy-start.5 = (f32[128,256]{1,0:T(8,128)S(1)}, f32[128,256]{1,0:T(8,128)}, u32[]{:S(2)}) copy-start(f32[128,256]{1,0:T(8,128)} %constant.65.clone.sin_ref) | copy-start | bytes 393220
  0.7 26.0 %copy-start.7 = (bf16[256,128]{1,0:T(8,128)(2,1)S(1)}, bf16[256,128]{1,0:T(8,128)(2,1)}, u32[]{:S(2)}) copy-start(bf16[256,128]{1,0:T(8,128)(2,1)} %constant.60.clone.t1_ref) | copy-start | bytes 196612
  0.7 26.0 %copy-start.9 = (bf16[128,256]{1,0:T(8,128)(2,1)S(1)}, bf16[128,256]{1,0:T(8,128)(2,1)}, u32[]{:S(2)}) copy-start(bf16[128,256]{1,0:T(8,128)(2,1)} %constant.63.clone.t1g_ref) | copy-start | bytes 196612
  3.7 23.0 %all-to-all-start = ((bf16[16,16,2048]{2,1,0:T(8,128)(2,1)}), bf16[16,16,2048]{2,1,0:T(8,128)(2,1)S(1)}, u32[]{:S(2)}, u32[]{:S(2)}) async-start(bf16[16,16,2048]{2,1,0:T(8,128)(2,1)} %bitcast.11), calls=%async_computation | async-start | bytes 2097152 | tf_op jit(solution)/shard_map/all_to_all | solution.py:303
  10.8 22.4 %collective-permute-start = (bf16[8,2048]{1,0:T(8,128)(2,1)}, bf16[8,2048]{1,0:T(8,128)(2,1)}, u32[]{:S(2)}, u32[]{:S(2)}) collective-permute-start(bf16[8,2048]{1,0:T(8,128)(2,1)} %bitcast.2), channel_id=1, source_target_pairs={{0,0},{1,16},{2,32},{3,48},{4,64},{5,80},{6,96},{7,112},{8,128},{9... | collective-permute-start | bytes 98312 | tf_op jit(solution)/shard_map/ppermute | solution.py:265
  26.7 1.0 %copy-start = (bf16[512,512]{1,0:T(8,128)(2,1)S(1)}, bf16[512,512]{1,0:T(8,128)(2,1)}, u32[]{:S(2)}) copy-start(bf16[512,512]{1,0:T(8,128)(2,1)} %constant.61.clone.t2_ref) | copy-start | bytes 1572868
  32.4 0.8 copy-start.3
  33.2 35.9 %copy-start.2 = (bf16[512,512]{1,0:T(8,128)(2,1)S(1)}, bf16[512,512]{1,0:T(8,128)(2,1)}, u32[]{:S(2)}) copy-start(bf16[512,512]{1,0:T(8,128)(2,1)} %constant.61.clone.t2_ref) | copy-start | bytes 1572868
  33.2 35.9 %copy-start.6 = (bf16[128,256]{1,0:T(8,128)(2,1)S(1)}, bf16[128,256]{1,0:T(8,128)(2,1)}, u32[]{:S(2)}) copy-start(bf16[128,256]{1,0:T(8,128)(2,1)} %constant.62.clone.t1i_ref) | copy-start | bytes 196612
  33.2 27.4 %all-to-all-start.1 = ((bf16[64,16,256]{2,1,0:T(8,128)(2,1)}), bf16[64,16,256]{2,1,0:T(8,128)(2,1)}, u32[]{:S(2)}, u32[]{:S(2)}) async-start(bf16[64,16,256]{2,1,0:T(8,128)(2,1)} %copy-done.3), calls=%async_computation.1 | async-start | bytes 1048576 | tf_op jit(solution)/shard_map/all_to_all | solution.py:333
  41.5 12.1 %collective-permute-start.4 = (bf16[8,2048]{1,0:T(8,128)(2,1)}, bf16[8,2048]{1,0:T(8,128)(2,1)S(1)}, u32[]{:S(2)}, u32[]{:S(2)}) collective-permute-start(bf16[8,2048]{1,0:T(8,128)(2,1)} %collective-permute-done), channel_id=1, source_target_pairs={{0,4},{4,8},{8,12},{12,0},{1,5},{5,9},{9,13},{13,1},{2,6},{6,10},{... | collective-permute-start | bytes 98312 | tf_op jit(solution)/shard_map/ppermute | solution.py:261
  44.8 10.7 %collective-permute-start.5 = (bf16[8,2048]{1,0:T(8,128)(2,1)}, bf16[8,2048]{1,0:T(8,128)(2,1)S(1)}, u32[]{:S(2)}, u32[]{:S(2)}) collective-permute-start(bf16[8,2048]{1,0:T(8,128)(2,1)} %collective-permute-done), channel_id=1, source_target_pairs={{0,8},{4,12},{8,0},{12,4},{1,9},{5,13},{9,1},{13,5},{2,10},{6,14},... | collective-permute-start | bytes 98312 | tf_op jit(solution)/shard_map/ppermute | solution.py:261
  49.0 6.6 %collective-permute-start.6 = (bf16[8,2048]{1,0:T(8,128)(2,1)}, bf16[8,2048]{1,0:T(8,128)(2,1)S(1)}, u32[]{:S(2)}, u32[]{:S(2)}) collective-permute-start(bf16[8,2048]{1,0:T(8,128)(2,1)} %collective-permute-done), channel_id=1, source_target_pairs={{0,12},{4,0},{8,4},{12,8},{1,13},{5,1},{9,5},{13,9},{2,14},{6,2},{... | collective-permute-start | bytes 98312 | tf_op jit(solution)/shard_map/ppermute | solution.py:261
  55.6 8.6 %collective-permute-start.7 = (bf16[32,2048]{1,0:T(8,128)(2,1)S(1)}, bf16[32,2048]{1,0:T(8,128)(2,1)S(1)}, u32[]{:S(2)}, u32[]{:S(2)}) collective-permute-start(bf16[32,2048]{1,0:T(8,128)(2,1)S(1)} %constant_dynamic-update-slice_fusion.a_ref), channel_id=1, source_target_pairs={{0,1},{1,2},{2,3},{3,0},{4,5},{5,6},{6,7},{7,4},{8,9},{9,10},{10,1... | collective-permute-start | bytes 393224 | tf_op jit(solution)/shard_map/ppermute | solution.py:261
  57.0 8.5 %collective-permute-start.8 = (bf16[32,2048]{1,0:T(8,128)(2,1)S(1)}, bf16[32,2048]{1,0:T(8,128)(2,1)S(1)}, u32[]{:S(2)}, u32[]{:S(2)}) collective-permute-start(bf16[32,2048]{1,0:T(8,128)(2,1)S(1)} %constant_dynamic-update-slice_fusion.a_ref), channel_id=1, source_target_pairs={{0,2},{1,3},{2,0},{3,1},{4,6},{5,7},{6,4},{7,5},{8,10},{9,11},{10,... | collective-permute-start | bytes 393224 | tf_op jit(solution)/shard_map/ppermute | solution.py:261
  59.4 6.1 %collective-permute-start.9 = (bf16[32,2048]{1,0:T(8,128)(2,1)S(1)}, bf16[32,2048]{1,0:T(8,128)(2,1)S(1)}, u32[]{:S(2)}, u32[]{:S(2)}) collective-permute-start(bf16[32,2048]{1,0:T(8,128)(2,1)S(1)} %constant_dynamic-update-slice_fusion.a_ref), channel_id=1, source_target_pairs={{0,3},{1,0},{2,1},{3,2},{4,7},{5,4},{6,5},{7,6},{8,11},{9,8},{10,9... | collective-permute-start | bytes 393224 | tf_op jit(solution)/shard_map/ppermute | solution.py:261
  61.7 11.3 %collective-permute-start.3 = (bf16[256,256]{1,0:T(8,128)(2,1)S(1)}, bf16[256,256]{1,0:T(8,128)(2,1)S(1)}, u32[]{:S(2)}, u32[]{:S(2)}) collective-permute-start(bf16[256,256]{1,0:T(8,128)(2,1)S(1)} %bitcast.12), channel_id=1, source_target_pairs={{0,12},{4,0},{8,4},{12,8},{1,13},{5,1},{9,5},{13,9},{2,14},{6,2},{... | collective-permute-start | bytes 393224 | tf_op jit(solution)/shard_map/ppermute | solution.py:261
  63.0 10.0 %collective-permute-start.2 = (bf16[256,256]{1,0:T(8,128)(2,1)S(1)}, bf16[256,256]{1,0:T(8,128)(2,1)S(1)}, u32[]{:S(2)}, u32[]{:S(2)}) collective-permute-start(bf16[256,256]{1,0:T(8,128)(2,1)S(1)} %bitcast.13), channel_id=1, source_target_pairs={{0,4},{4,8},{8,12},{12,0},{1,5},{5,9},{9,13},{13,1},{2,6},{6,10},{... | collective-permute-start | bytes 393224 | tf_op jit(solution)/shard_map/ppermute | solution.py:261
  64.1 10.9 %collective-permute-start.1 = (bf16[256,256]{1,0:T(8,128)(2,1)S(1)}, bf16[256,256]{1,0:T(8,128)(2,1)S(1)}, u32[]{:S(2)}, u32[]{:S(2)}) collective-permute-start(bf16[256,256]{1,0:T(8,128)(2,1)S(1)} %bitcast.14), channel_id=1, source_target_pairs={{0,8},{4,12},{8,0},{12,4},{1,9},{5,13},{9,1},{13,5},{2,10},{6,14},... | collective-permute-start | bytes 393224 | tf_op jit(solution)/shard_map/ppermute | solution.py:261
  65.5 1.0 %copy-start.1 = (bf16[512,512]{1,0:T(8,128)(2,1)S(1)}, bf16[512,512]{1,0:T(8,128)(2,1)}, u32[]{:S(2)}) copy-start(bf16[512,512]{1,0:T(8,128)(2,1)} %constant.61.clone.t2_ref) | copy-start | bytes 1572868
  66.5 0.8 copy-start.8
  75.1 26.1 %all-to-all-start.2 = ((bf16[16,16,2048]{2,1,0:T(8,128)(2,1)}), bf16[16,16,2048]{2,1,0:T(8,128)(2,1)S(1)}, u32[]{:S(2)}, u32[]{:S(2)}) async-start(bf16[16,16,2048]{2,1,0:T(8,128)(2,1)} %bitcast.5), calls=%async_computation.2 | async-start | bytes 2097152 | tf_op jit(solution)/shard_map/all_to_all | solution.py:350
  85.4 8.9 %collective-permute-start.10 = (bf16[256,256]{1,0:T(8,128)(2,1)S(1)}, bf16[256,256]{1,0:T(8,128)(2,1)S(1)}, u32[]{:S(2)}, u32[]{:S(2)}) collective-permute-start(bf16[256,256]{1,0:T(8,128)(2,1)S(1)} %add_convert_fusion.a_ref), channel_id=1, source_target_pairs={{0,1},{1,2},{2,3},{3,0},{4,5},{5,6},{6,7},{7,4},{8,9},{9,10},{10,1... | collective-permute-start | bytes 393224 | tf_op jit(solution)/shard_map/ppermute | solution.py:261
  85.6 8.7 %collective-permute-start.11 = (bf16[256,256]{1,0:T(8,128)(2,1)S(1)}, bf16[256,256]{1,0:T(8,128)(2,1)S(1)}, u32[]{:S(2)}, u32[]{:S(2)}) collective-permute-start(bf16[256,256]{1,0:T(8,128)(2,1)S(1)} %add_convert_fusion.a_ref), channel_id=1, source_target_pairs={{0,2},{1,3},{2,0},{3,1},{4,6},{5,7},{6,4},{7,5},{8,10},{9,11},{10,... | collective-permute-start | bytes 393224 | tf_op jit(solution)/shard_map/ppermute | solution.py:261
  86.8 7.8 %collective-permute-start.12 = (bf16[256,256]{1,0:T(8,128)(2,1)S(1)}, bf16[256,256]{1,0:T(8,128)(2,1)S(1)}, u32[]{:S(2)}, u32[]{:S(2)}) collective-permute-start(bf16[256,256]{1,0:T(8,128)(2,1)S(1)} %add_convert_fusion.a_ref), channel_id=1, source_target_pairs={{0,3},{1,0},{2,1},{3,2},{4,7},{5,4},{6,5},{7,6},{8,11},{9,8},{10,9... | collective-permute-start | bytes 393224 | tf_op jit(solution)/shard_map/ppermute | solution.py:261

commit v3 on v2

v3 whole, which is shorter than its diff:
```python
import math

import jax
import jax.numpy as jnp
import numpy as np
from jax import lax
from jax.experimental import pallas as pl
from jax.experimental.pallas import tpu as pltpu
from jax.sharding import Mesh
from jax.sharding import PartitionSpec as P

BF = jnp.bfloat16
F32 = jnp.float32
FACTOR = 256
HALF = 128
FULL = FACTOR * FACTOR
CTX = 16
SUB = HALF // CTX
TOK = SUB * FACTOR
PAIR = 2
ZH = 4
Y = 4
LARGE = 60 * 1024 * 1024
GRAD_SCALE = 1.0 / math.sqrt(524288)


def unit(product, modulus):
    angles = np.float32(2.0 * math.pi / modulus) * (product % modulus).astype(np.float32)
    return np.cos(angles).astype(np.float32), np.sin(angles).astype(np.float32)


def tables():
    n1 = np.arange(HALF)
    k1 = np.arange(HALF)
    n2 = np.arange(FACTOR)
    cos1, sin1 = unit((2 * k1[:, None] + 1) * n1[None, :], 2 * FACTOR)
    cos2, sin2 = unit(n2[:, None] * n2[None, :], FACTOR)
    tw_cos, tw_sin = unit((2 * k1[:, None] + 1) * n2[None, :], 2 * FULL)
    first = np.concatenate([cos1, -sin1], 0)
    second = np.block([[cos2, -sin2], [sin2, cos2]])
    back_last = np.concatenate([cos1.T, -sin1.T], 1) * np.float32(2.0 / FULL)
    half = lambda a: jnp.asarray(a, dtype=BF)
    return half(first), half(second), half(back_last), jnp.asarray(tw_cos), jnp.asarray(tw_sin)


def mm(a, b):
    return jnp.dot(a, b, preferred_element_type=F32)


def ones_at(row_of, size=FACTOR):
    row = lax.broadcasted_iota(jnp.int32, (size, size), 0)
    col = lax.broadcasted_iota(jnp.int32, (size, size), 1)
    return (col == row_of(row)).astype(F32).astype(BF)


def to_owners(r):
    return (r & 7) * 32 + ((r >> 4) & 1) * 16 + (r >> 5) * PAIR + ((r >> 3) & 1)


def to_subs(r):
    return ((r >> 1) & 7) * 32 + ((r >> 4) & 1) * 16 + (r & 1) * 8 + (r >> 5)


def subs_first(r):
    return (r & 31) * SUB + (r >> 5)


def twist(first, cos, sin):
    real, imag = first[:HALF], first[HALF:]
    return jnp.concatenate([real * cos + imag * sin, imag * cos - real * sin], axis=1).astype(BF)


def untwist(first, cos, sin):
    real, imag = first[:, :FACTOR], first[:, FACTOR:]
    return jnp.concatenate([real * cos + imag * sin, real * sin - imag * cos], axis=0).astype(BF)


def split(spec):
    return spec[:, :FACTOR].astype(F32), spec[:, FACTOR:].astype(F32)


def forward(columns, t1, t2, cos, sin):
    first = mm(t1, jnp.concatenate(columns, axis=1))
    count = len(columns)
    second = [twist(first[:, k * FACTOR : (k + 1) * FACTOR], cos, sin) for k in range(count)]
    return mm(jnp.concatenate(second, axis=0), t2)


def backward(spectra, t2, t1i, cos, sin):
    first = mm(jnp.concatenate(spectra, axis=0), t2)
    count = len(spectra)
    back = [untwist(first[k * HALF : (k + 1) * HALF], cos, sin) for k in range(count)]
    return mm(t1i, jnp.concatenate(back, axis=1))


def spread_kernel(x_ref, dy_ref, out_ref, held, put, in_sems, out_sems):
    takes = []
    for n in range(SUB):
        chunk = pl.ds(n * FACTOR, FACTOR)
        for s, ref in enumerate((x_ref, dy_ref)):
            take = pltpu.make_async_copy(
                ref.at[chunk], held.at[s, chunk], in_sems.at[2 * n + s]
            )
            take.start()
            takes.append(take)
    sort = ones_at(to_owners)
    turned = []
    for n in range(SUB):
        takes[2 * n].wait()
        takes[2 * n + 1].wait()
        turned.append([held[s, n * FACTOR : (n + 1) * FACTOR].T for s in range(2)])
    gives = []
    for g in range(SUB):
        chunk = pl.ds(g * SUB, SUB)
        rows = jnp.concatenate([t[g * 16 : (g + 1) * 16] for pair in turned for t in pair], axis=0)
        rows = mm(sort, rows).astype(BF)
        for k in range(2):
            put[chunk, 32 * k : 32 * (k + 1)] = rows[:, k * HALF : (k + 1) * HALF].reshape(SUB, 32, HALF)
        give = pltpu.make_async_copy(put.at[chunk], out_ref.at[chunk], out_sems.at[g])
        give.start()
        gives.append(give)
    for give in gives:
        give.wait()


def forward_kernel(r_ref, t1_ref, t2_ref, t1i_ref, cos_ref, sin_ref, spec_ref, g_ref, acc_ref):
    acc_ref[...] = jnp.zeros_like(acc_ref)

    def body(j):
        tiles = [
            jnp.concatenate([r_ref[i * Y + j, :32], r_ref[i * Y + j, 32:]], axis=1).astype(F32) for i in range(CTX)
        ]
        columns = [
            jnp.concatenate([t[q * SUB : (q + 1) * SUB] for t in tiles], axis=0).astype(BF) for q in range(4)
        ]
        spec = forward(columns, t1_ref[...], t2_ref[...], cos_ref[...], sin_ref[...])
        spec_ref[j] = spec.astype(BF)
        for f in range(PAIR):
            x_real, x_imag = split(spec[f * HALF : (f + 1) * HALF])
            dy_real, dy_imag = split(spec[(PAIR + f) * HALF : (PAIR + f + 1) * HALF])
            acc_ref[f] += jnp.concatenate(
                [dy_real * x_real + dy_imag * x_imag, dy_real * x_imag - dy_imag * x_real], axis=1
            )

    for j in range(Y):
        body(j)
    groups = [acc_ref[f].astype(BF) for f in range(PAIR)]
    out = backward(groups, t2_ref[...], t1i_ref[...], cos_ref[...], sin_ref[...]) * GRAD_SCALE
    for d in range(CTX):
        rows = [out[d * SUB : (d + 1) * SUB, f * FACTOR : (f + 1) * FACTOR] for f in range(PAIR)]
        g_ref[d] = jnp.concatenate(rows, axis=0).astype(BF)


def pack_kernel(part_ref, a_ref, b_ref, out_ref):
    out_ref[:CTX] = part_ref[...]
    out_ref[CTX : CTX + 2] = a_ref[...]
    out_ref[CTX + 2 :] = b_ref[...]


def backward_kernel(
    spec_ref, all_ref, me_ref, t1_ref, t2_ref, t1i_ref, cos_ref, sin_ref, out_ref, h_ref
):
    my_y = me_ref[0]
    parts = [all_ref.at[z] for z in range(ZH)]

    def arrival(r):
        block = r >> 3
        return ((block >> 2 << 2) + ((block & 3) ^ my_y)) * SUB + (r & 7)

    order = ones_at(arrival, HALF)
    tiles = [ref[CTX + k].astype(F32) for ref in parts for k in range(Y)]
    taps = [jnp.concatenate([t[f * SUB : (f + 1) * SUB] for t in tiles], axis=0).astype(BF) for f in range(PAIR)]
    taps = mm(order, jnp.concatenate(taps, axis=1)).astype(BF)
    columns = [taps[:, f * FACTOR : (f + 1) * FACTOR] for f in range(PAIR)]
    h_ref[...] = forward(columns, t1_ref[...], t2_ref[...], cos_ref[...], sin_ref[...])

    def body(j):
        spectra = []
        for s in range(2):
            for f in range(PAIR):
                at = (s * PAIR + f) * HALF
                real, imag = split(spec_ref[j, at : at + HALF])
                h_real, h_imag = split(h_ref[f * HALF : (f + 1) * HALF])
                if s == 0:
                    both = [real * h_real - imag * h_imag, -(real * h_imag + imag * h_real)]
                else:
                    both = [real * h_real + imag * h_imag, real * h_imag - imag * h_real]
                spectra.append(jnp.concatenate(both, axis=1).astype(BF))
        out = backward(spectra, t2_ref[...], t1i_ref[...], cos_ref[...], sin_ref[...])
        for d in range(CTX):
            rows = [out[d * SUB : (d + 1) * SUB, q * FACTOR : (q + 1) * FACTOR] for q in range(4)]
            rows = jnp.concatenate(rows, axis=0).astype(BF)
            for k in range(2):
                out_ref[d, j, 48 * k : 48 * k + 32] = rows[:, k * HALF : (k + 1) * HALF]

    for d in range(CTX):
        a, b, c, e = (ref[d].astype(F32) for ref in parts)
        rows = ((a + c) + (b + e)).astype(BF)
        for j in range(Y):
            for k in range(2):
                out_ref[d, j, 48 * k + 32 : 48 * (k + 1)] = rows[:, k * HALF : (k + 1) * HALF]
    for j in range(Y):
        body(j)


def place_kernel(r_ref, a_ref, b_ref, g_ref, put, grad, sems):
    outer, sort = ones_at(subs_first), ones_at(to_subs)

    def sorted_rows(order, first, count, at, size):
        halves = [
            r_ref[first : first + count, at + 48 * k : at + 48 * k + size].reshape(FACTOR, HALF) for k in range(2)
        ]
        return mm(order, jnp.concatenate(halves, axis=1))

    turned = [sorted_rows(sort, 8 * k, 8, 0, 32).astype(BF) for k in range(8)]
    grads = [sorted_rows(outer, 16 * k, 16, 32, 16) for k in range(4)]
    gives = []
    for n in range(SUB):
        chunk = pl.ds(n * FACTOR, FACTOR)
        for s in range(2):
            at = n * 32 + s * 16
            put[s, chunk] = jnp.concatenate([t[at : at + 16] for t in turned], axis=0).T
        grad[chunk] = jnp.concatenate([t[n * 32 : (n + 1) * 32] for t in grads], axis=0).T
        for k, (src, dst) in enumerate(((put.at[0], a_ref), (put.at[1], b_ref), (grad, g_ref))):
            give = pltpu.make_async_copy(src.at[chunk], dst.at[chunk], sems.at[3 * n + k])
            give.start()
            gives.append(give)
    for give in gives:
        give.wait()


def call(kernel, outs, scratch, flops, *args, ins=None, space=pltpu.VMEM, limit=24 * 1024 * 1024):
    return pl.pallas_call(
        kernel,
        in_specs=[
            pl.BlockSpec(memory_space=pltpu.SMEM if a.dtype == jnp.int32 else ins or pltpu.VMEM) for a in args
        ],
        out_specs=[pl.BlockSpec(memory_space=space)] * len(outs),
        out_shape=[jax.ShapeDtypeStruct(*o) for o in outs],
        scratch_shapes=scratch,
        compiler_params=pltpu.CompilerParams(vmem_limit_bytes=limit),
        cost_estimate=pl.CostEstimate(flops=flops, bytes_accessed=3 << 20, transcendentals=0),
    )(*args)


def handed(x, k):
    pairs = [(a * CTX + b, b * CTX + a // Y * Y + (a ^ 2 * k) % Y) for a in range(CTX) for b in range(CTX)]
    return lax.ppermute(x, ("ctx", "zh", "y"), pairs)


def local(seq_input, out_grad, filters):
    first, second, back_last, tw_cos, tw_sin = tables()
    my_ctx = lax.axis_index("ctx")

    taps = filters.T.reshape(2, 2, PAIR * SUB, FACTOR)
    core, row = my_ctx % 2, my_ctx // 2 % 2
    mine = lax.dynamic_index_in_dim(taps, core, 1, keepdims=False)
    other = lax.dynamic_index_in_dim(taps, 1 - core, 1, keepdims=False)
    other = lax.ppermute(other, "ctx", [(a, a ^ 1) for a in range(CTX)])
    taps = jnp.stack([mine, other], axis=1)
    taps = [handed(lax.dynamic_index_in_dim(taps, row ^ k, 0, keepdims=False), k) for k in range(2)]
    (spread,) = call(
        spread_kernel,
        [((CTX * Y, 64, HALF), BF)],
        [
            pltpu.VMEM((2, TOK, HALF), BF),
            pltpu.VMEM((CTX * Y, 64, HALF), BF),
            pltpu.SemaphoreType.DMA((2 * SUB,)),
            pltpu.SemaphoreType.DMA((SUB,)),
        ],
        4 * 256 * 256 * 2048,
        seq_input,
        out_grad,
        ins=pl.ANY,
        space=pl.ANY,
        limit=LARGE,
    )
    arrived = lax.all_to_all(spread, ("ctx", "y"), 0, 0, tiled=True)
    spec, partial = call(
        forward_kernel,
        [((Y, 4 * HALF, 2 * FACTOR), BF), ((CTX, CTX, FACTOR), BF)],
        [pltpu.VMEM((PAIR, HALF, 2 * FACTOR), F32)],
        2 * 18 * 42 * 10**6,
        arrived,
        first,
        second,
        back_last,
        tw_cos,
        tw_sin,
    )
    (partial,) = call(
        pack_kernel,
        [((CTX + Y, CTX, FACTOR), BF)],
        [],
        1 << 10,
        partial,
        *taps,
        limit=4 << 20,
    )
    partial = lax.all_gather(partial, "zh", axis=0)
    (leaving,) = call(
        backward_kernel,
        [((CTX, Y, 96, HALF), BF)],
        [pltpu.VMEM((PAIR * HALF, 2 * FACTOR), F32)],
        2 * 18 * 42 * 10**6,
        spec,
        partial,
        lax.axis_index("y").reshape(1),
        first,
        second,
        back_last,
        tw_cos,
        tw_sin,
    )
    back = lax.all_to_all(leaving.reshape(CTX * Y, 96, HALF), ("ctx", "y"), 0, 0, tiled=True)
    return call(
        place_kernel,
        [((TOK, HALF), BF), ((TOK, HALF), BF), ((TOK, HALF), F32)],
        [
            pltpu.VMEM((2, TOK, HALF), BF),
            pltpu.VMEM((TOK, HALF), F32),
            pltpu.SemaphoreType.DMA((3 * SUB,)),
        ],
        6 * 256 * 256 * 2048,
        back,
        space=pl.ANY,
    )


def solution(mesh):
    inner = Mesh(mesh.devices.reshape(CTX, ZH, Y), ("ctx", "zh", "y"))
    placed = P("ctx", ("zh", "y"))
    return jax.shard_map(
        local,
        mesh=inner,
        in_specs=(placed, placed, placed),
        out_specs=(placed, placed, P("ctx", None)),
        check_vma=False,
    )
```

time: 103 us -> 88.1 us (0.86)
  blocking collectives: 0 us -> 48.5 us
  starting transfers between devices: 49.6 us -> 15.7 us
  waiting for transfers between devices: 30.2 us -> 12.2 us
  Pallas kernels: 16 us -> 10.5 us
  local copies, waits for them, and re-layouts: 4.57 us -> 0.07 us
  other arithmetic: 1.32 us -> 0.01 us
    all_to_all x0 -> x1, blocking collectives: none -> 29.7 us  [local(): lax.all_to_all(leaving.reshape(CTX * Y, 96, HALF), ('ctx', 'y'), 0, 0, ti...]
    all_gather x0 -> x1, blocking collectives: none -> 18.8 us  [local(): partial = lax.all_gather(partial, 'zh', axis=0)]
    ppermute x13 -> x3, starting transfers between devices: 23.9 us -> 5.19 us  [the longest x2 4.65 us: handed(): return lax.ppermute(x, ('ctx', 'zh', 'y'), pairs)]
    all_to_all x3 -> x1, starting transfers between devices: 25.7 us -> 10.5 us  [local(): arrived = lax.all_to_all(spread, ('ctx', 'y'), 0, 0, tiled=True)]
    ppermute x13 -> x3, waiting for transfers between devices: 12.5 us -> 0.84 us  [the longest x1 0.84 us: local(): other = lax.ppermute(other, 'ctx', [(a, a ^ 1) for a in range(CTX)])]
    all_to_all x3 -> x1, waiting for transfers between devices: 17.6 us -> 11.4 us  [local(): arrived = lax.all_to_all(spread, ('ctx', 'y'), 0, 0, tiled=True)]
    pallas_call x6 -> x5, Pallas kernels: 16 us -> 10.5 us  [call(): pl.pallas_call(kernel, in_specs=[pl.BlockSpec(memory_space=pltpu.SMEM if...]
    unnamed x31 -> x12, local copies, waits for them, and re-layouts: 4.57 us -> 0.04 us
  transfers between devices with their start and end apart: 16 -> 4, of which waited for: 7 -> 2; matrix products, arithmetic and copies ran while one was open for 2% -> 0% of each run, Pallas kernels for 11% -> 3%
where the time goes in v3:
time: 88.1 us; the launch traced here: 87.8 us
  blocking collectives  48.5 us (55%)
  starting transfers between devices  15.7 us (18%)
  waiting for transfers between devices  12.2 us (14%)
  Pallas kernels  10.5 us (12%)
    all_to_all x1, blocking collectives, local(): lax.all_to_all(leaving.reshape(CTX * Y, 96, HALF), ('ctx', 'y'), 0, 0, ti...  29.7 us
    all_gather x1, blocking collectives, local(): partial = lax.all_gather(partial, 'zh', axis=0)  18.8 us
    all_to_all x1, waiting for transfers between devices, local(): arrived = lax.all_to_all(spread, ('ctx', 'y'), 0, 0, tiled=True)  11.4 us
    all_to_all x1, starting transfers between devices, local(): arrived = lax.all_to_all(spread, ('ctx', 'y'), 0, 0, tiled=True)  10.5 us
    pallas_call x5, Pallas kernels, call(): pl.pallas_call(kernel, in_specs=[pl.BlockSpec(memory_space=pltpu.SMEM if...  10.5 us
    ppermute x2, starting transfers between devices, handed(): return lax.ppermute(x, ('ctx', 'zh', 'y'), pairs)  4.65 us
  transfers between devices with their start and end apart: 4, of which 2 were waited for; matrix products, arithmetic and copies ran while one was open for 0% of the time, Pallas kernels for 3%

profile of v3, /device:TPU:1, one launch (start us, length us, event | category | flops | bytes accessed | tf_op | source)
XLA Modules:
  0.0 87.8 jit_solution(10152085623668955593)
XLA Ops:
  0.6 2.9 %shard_map.103 = bf16[64,64,128]{2,1,0:T(8,128)(2,1)} custom-call(bf16[2048,128]{1,0:T(8,128)(2,1)} %x_ref.1, bf16[2048,128]{1,0:T(8,128)(2,1)} %dy_ref.1), custom_call_target="tpu_custom_call" | custom-call | flops 536870912 | bytes 3145728 | tf_op jit(solution)/shard_map/pallas_call | solution.py:233
  3.6 0.0 copy-start.5
  3.6 0.0 copy-start
  3.6 0.0 copy-start.1
  3.6 0.0 copy-start.2
  3.6 0.0 copy-start.3
  3.6 0.0 copy-start.4
  3.7 10.5 %all-to-all-start = ((bf16[64,64,128]{2,1,0:T(8,128)(2,1)}), bf16[64,64,128]{2,1,0:T(8,128)(2,1)S(1)}, u32[]{:S(2)}, u32[]{:S(2)}) async-start(bf16[64,64,128]{2,1,0:T(8,128)(2,1)} %shard_map.103), calls=%async_computation | async-start | bytes 2097152 | tf_op jit(solution)/shard_map/all_to_all | solution.py:278
  14.2 0.0 copy-done.5
  14.2 0.5 collective-permute-start
  14.8 0.8 collective-permute-done
  15.6 2.7 %collective-permute-start.2 = (bf16[2,16,256]{2,1,0:T(8,128)(2,1)S(1)}, bf16[2,16,256]{2,1,0:T(8,128)(2,1)S(1)}, u32[]{:S(2)}, u32[]{:S(2)}) collective-permute-start(bf16[2,16,256]{2,1,0:T(8,128)(2,1)S(1)} %get-tuple-element.7), channel_id=1, source_target_pairs={{0,2},{1,18},{2,34},{3,50},{4,66},{5,82},{6,98},{7,114},{8,130},{9... | collective-permute-start | bytes 49160 | tf_op jit(solution)/shard_map/ppermute | solution.py:248
  18.4 1.9 %collective-permute-start.1 = (bf16[2,16,256]{2,1,0:T(8,128)(2,1)S(1)}, bf16[2,16,256]{2,1,0:T(8,128)(2,1)S(1)}, u32[]{:S(2)}, u32[]{:S(2)}) collective-permute-start(bf16[2,16,256]{2,1,0:T(8,128)(2,1)S(1)} %get-tuple-element.8), channel_id=1, source_target_pairs={{0,0},{1,16},{2,32},{3,48},{4,64},{5,80},{6,96},{7,112},{8,128},{9... | collective-permute-start | bytes 49160 | tf_op jit(solution)/shard_map/ppermute | solution.py:248
  20.3 11.4 %all-to-all-done.r_ref = bf16[64,64,128]{2,1,0:T(8,128)(2,1)S(1)} async-done(((bf16[64,64,128]{2,1,0:T(8,128)(2,1)}), bf16[64,64,128]{2,1,0:T(8,128)(2,1)S(1)}, u32[]{:S(2)}, u32[]{:S(2)}) %all-to-all-start) | async-done | bytes 1048608 | tf_op jit(solution)/shard_map/all_to_all | solution.py:278
  31.7 0.0 copy-done
  31.7 0.0 copy-done.1
  31.7 0.0 copy-done.2
  31.7 0.0 copy-done.3
  31.7 0.0 copy-done.4
  31.7 2.6 %shard_map.104 = (bf16[4,512,512]{2,1,0:T(8,128)(2,1)S(1)}, bf16[16,16,256]{2,1,0:T(8,128)(2,1)S(1)}) custom-call(bf16[64,64,128]{2,1,0:T(8,128)(2,1)S(1)} %all-to-all-done.r_ref, bf16[256,128]{1,0:T(8,128)(2,1)S(1)} %copy-done.4, bf16[512,512]{1,0:T(8,128)(2,1)S(1)} %copy-done, bf16[128,256]{1,0:T(8,128)(2,1)S(1)} %copy-done.3, f32[128,256]{1,0:T(8,128)S(1)} %copy-done.2, ...), custom_call_target="tpu_custom_call" | custom-call | flops 1512000000 | bytes 3145728 | tf_op jit(solution)/shard_map/pallas_call | solution.py:233
  34.3 0.0 collective-permute-done.2.b_ref
  34.3 0.0 collective-permute-done.1.a_ref
  34.3 18.8 %all-gather = bf16[80,16,256]{2,1,0:T(8,128)(2,1)S(1)} all-gather(bf16[20,16,256]{2,1,0:T(8,128)(2,1)S(1)} %shard_map.105), channel_id=2, replica_groups=mesh['ctx'=16,'zh'=4,'y'=4] {'zh'}, dimensions={0}, use_global_device_ids=true | all-gather | bytes 819200 | tf_op jit(solution)/shard_map/all_gather | solution.py:300
  53.1 2.7 %shard_map.106 = bf16[16,4,96,128]{3,2,1,0:T(8,128)(2,1)S(1)} custom-call(bf16[4,512,512]{2,1,0:T(8,128)(2,1)S(1)} %get-tuple-element.5.spec_ref, bf16[4,20,16,256]{3,2,1,0:T(8,128)(2,1)S(1)} %bitcast.12, s32[1]{0:T(128)} %bitcast.6.me_ref, bf16[256,128]{1,0:T(8,128)(2,1)S(1)} %copy-done.4, bf16[512,512]{1,0:T(8,128)(2,1)S(1)} %copy-done, ...), custom_call_target="tpu_custom_call" | custom-call | flops 1512000000 | bytes 3145728 | tf_op jit(solution)/shard_map/pallas_call | solution.py:233
  55.9 29.7 %all_to_all.10.r_ref = bf16[64,96,128]{2,1,0:T(8,128)(2,1)S(1)} all-to-all(bf16[64,96,128]{2,1,0:T(8,128)(2,1)S(1)} %bitcast.11), channel_id=1, replica_groups=mesh['ctx'=16,'zh'=4,'y'=4] {'ctx','y'}, dimensions={0} | all-to-all | bytes 3145728 | tf_op jit(solution)/shard_map/all_to_all | solution.py:315
  85.6 2.2 %shard_map.107 = (bf16[2048,128]{1,0:T(8,128)(2,1)}, bf16[2048,128]{1,0:T(8,128)(2,1)}, f32[2048,128]{1,0:T(8,128)}) custom-call(bf16[64,96,128]{2,1,0:T(8,128)(2,1)S(1)} %all_to_all.10.r_ref), custom_call_target="tpu_custom_call" | custom-call | flops 805306368 | bytes 3145728 | tf_op jit(solution)/shard_map/pallas_call | solution.py:233
  (4 shorter events, 0.0 us)
Async XLA Ops:
  3.6 10.6 %copy-start.5 = (bf16[2048,8]{0,1:T(8,128)(2,1)S(1)}, bf16[2048,8]{0,1:T(8,128)(2,1)}, u32[]{:S(2)}) copy-start(bf16[2048,8]{0,1:T(8,128)(2,1)} %param.10) | copy-start | bytes 98308
  3.6 28.1 %copy-start = (bf16[512,512]{1,0:T(8,128)(2,1)S(1)}, bf16[512,512]{1,0:T(8,128)(2,1)}, u32[]{:S(2)}) copy-start(bf16[512,512]{1,0:T(8,128)(2,1)} %constant.63.clone.t2_ref) | copy-start | bytes 1572868
  3.6 28.1 %copy-start.1 = (f32[128,256]{1,0:T(8,128)S(1)}, f32[128,256]{1,0:T(8,128)}, u32[]{:S(2)}) copy-start(f32[128,256]{1,0:T(8,128)} %constant.66.clone.sin_ref) | copy-start | bytes 393220
  3.6 28.1 %copy-start.2 = (f32[128,256]{1,0:T(8,128)S(1)}, f32[128,256]{1,0:T(8,128)}, u32[]{:S(2)}) copy-start(f32[128,256]{1,0:T(8,128)} %constant.65.clone.cos_ref) | copy-start | bytes 393220
  3.6 28.0 %copy-start.3 = (bf16[128,256]{1,0:T(8,128)(2,1)S(1)}, bf16[128,256]{1,0:T(8,128)(2,1)}, u32[]{:S(2)}) copy-start(bf16[128,256]{1,0:T(8,128)(2,1)} %constant.64.clone.t1i_ref) | copy-start | bytes 196612
  3.6 28.0 %copy-start.4 = (bf16[256,128]{1,0:T(8,128)(2,1)S(1)}, bf16[256,128]{1,0:T(8,128)(2,1)}, u32[]{:S(2)}) copy-start(bf16[256,128]{1,0:T(8,128)(2,1)} %constant.62.clone.t1_ref) | copy-start | bytes 196612
  3.7 28.0 %all-to-all-start = ((bf16[64,64,128]{2,1,0:T(8,128)(2,1)}), bf16[64,64,128]{2,1,0:T(8,128)(2,1)S(1)}, u32[]{:S(2)}, u32[]{:S(2)}) async-start(bf16[64,64,128]{2,1,0:T(8,128)(2,1)} %shard_map.103), calls=%async_computation | async-start | bytes 2097152 | tf_op jit(solution)/shard_map/all_to_all | solution.py:278
  14.2 1.4 %collective-permute-start = (bf16[2,16,256]{2,1,0:T(8,128)(2,1)S(1)}, bf16[2,16,256]{2,1,0:T(8,128)(2,1)S(1)}, u32[]{:S(2)}, u32[]{:S(2)}) collective-permute-start(bf16[2,16,256]{2,1,0:T(8,128)(2,1)S(1)} %get-tuple-element.9), channel_id=1, source_target_pairs={{0,16},{16,0},{32,48},{48,32},{64,80},{80,64},{96,112},{112,96},{1... | collective-permute-start | bytes 49160 | tf_op jit(solution)/shard_map/ppermute | solution.py:259
  15.6 18.7 %collective-permute-start.2 = (bf16[2,16,256]{2,1,0:T(8,128)(2,1)S(1)}, bf16[2,16,256]{2,1,0:T(8,128)(2,1)S(1)}, u32[]{:S(2)}, u32[]{:S(2)}) collective-permute-start(bf16[2,16,256]{2,1,0:T(8,128)(2,1)S(1)} %get-tuple-element.7), channel_id=1, source_target_pairs={{0,2},{1,18},{2,34},{3,50},{4,66},{5,82},{6,98},{7,114},{8,130},{9... | collective-permute-start | bytes 49160 | tf_op jit(solution)/shard_map/ppermute | solution.py:248
  18.4 15.9 %collective-permute-start.1 = (bf16[2,16,256]{2,1,0:T(8,128)(2,1)S(1)}, bf16[2,16,256]{2,1,0:T(8,128)(2,1)S(1)}, u32[]{:S(2)}, u32[]{:S(2)}) collective-permute-start(bf16[2,16,256]{2,1,0:T(8,128)(2,1)S(1)} %get-tuple-element.8), channel_id=1, source_target_pairs={{0,0},{1,16},{2,32},{3,48},{4,64},{5,80},{6,96},{7,112},{8,128},{9... | collective-permute-start | bytes 49160 | tf_op jit(solution)/shard_map/ppermute | solution.py:248

commit v4 on v3

--- a/solution.py
+++ b/solution.py
@@ -95,19 +95,18 @@
 
 def spread_kernel(x_ref, dy_ref, out_ref, held, put, in_sems, out_sems):
     takes = []
-    for n in range(SUB):
-        chunk = pl.ds(n * FACTOR, FACTOR)
+    for n in range(SUB // 2):
+        chunk = pl.ds(2 * n * FACTOR, 2 * FACTOR)
         for s, ref in enumerate((x_ref, dy_ref)):
-            take = pltpu.make_async_copy(
-                ref.at[chunk], held.at[s, chunk], in_sems.at[2 * n + s]
-            )
+            take = pltpu.make_async_copy(ref.at[chunk], held.at[s, chunk], in_sems.at[2 * n + s])
             take.start()
             takes.append(take)
     sort = ones_at(to_owners)
     turned = []
     for n in range(SUB):
-        takes[2 * n].wait()
-        takes[2 * n + 1].wait()
+        if n % 2 == 0:
+            takes[n].wait()
+            takes[n + 1].wait()
         turned.append([held[s, n * FACTOR : (n + 1) * FACTOR].T for s in range(2)])
     gives = []
     for g in range(SUB):
@@ -116,9 +115,11 @@
         rows = mm(sort, rows).astype(BF)
         for k in range(2):
             put[chunk, 32 * k : 32 * (k + 1)] = rows[:, k * HALF : (k + 1) * HALF].reshape(SUB, 32, HALF)
-        give = pltpu.make_async_copy(put.at[chunk], out_ref.at[chunk], out_sems.at[g])
-        give.start()
-        gives.append(give)
+        if g % 2 == 1:
+            chunk = pl.ds((g - 1) * SUB, 2 * SUB)
+            give = pltpu.make_async_copy(put.at[chunk], out_ref.at[chunk], out_sems.at[g])
+            give.start()
+            gives.append(give)
     for give in gives:
         give.wait()
 
@@ -126,24 +127,26 @@
 def forward_kernel(r_ref, t1_ref, t2_ref, t1i_ref, cos_ref, sin_ref, spec_ref, g_ref, acc_ref):
     acc_ref[...] = jnp.zeros_like(acc_ref)
 
-    def body(j):
-        tiles = [
-            jnp.concatenate([r_ref[i * Y + j, :32], r_ref[i * Y + j, 32:]], axis=1).astype(F32) for i in range(CTX)
-        ]
-        columns = [
-            jnp.concatenate([t[q * SUB : (q + 1) * SUB] for t in tiles], axis=0).astype(BF) for q in range(4)
-        ]
-        spec = forward(columns, t1_ref[...], t2_ref[...], cos_ref[...], sin_ref[...])
-        spec_ref[j] = spec.astype(BF)
-        for f in range(PAIR):
-            x_real, x_imag = split(spec[f * HALF : (f + 1) * HALF])
-            dy_real, dy_imag = split(spec[(PAIR + f) * HALF : (PAIR + f + 1) * HALF])
-            acc_ref[f] += jnp.concatenate(
-                [dy_real * x_real + dy_imag * x_imag, dy_real * x_imag - dy_imag * x_real], axis=1
-            )
-
-    for j in range(Y):
-        body(j)
+    for both in range(0, Y, 2):
+        columns = []
+        for j in (both, both + 1):
+            tiles = [
+                jnp.concatenate([r_ref[i * Y + j, :32], r_ref[i * Y + j, 32:]], axis=1).astype(F32)
+                for i in range(CTX)
+            ]
+            for q in range(4):
+                rows = [t[q * SUB : (q + 1) * SUB] for t in tiles]
+                columns.append(jnp.concatenate(rows, axis=0).astype(BF))
+        spectra = forward(columns, t1_ref[...], t2_ref[...], cos_ref[...], sin_ref[...])
+        for j in (both, both + 1):
+            spec = spectra[(j - both) * 4 * HALF : (j - both + 1) * 4 * HALF]
+            spec_ref[j] = spec.astype(BF)
+            for f in range(PAIR):
+                x_real, x_imag = split(spec[f * HALF : (f + 1) * HALF])
+                dy_real, dy_imag = split(spec[(PAIR + f) * HALF : (PAIR + f + 1) * HALF])
+                acc_ref[f] += jnp.concatenate(
+                    [dy_real * x_real + dy_imag * x_imag, dy_real * x_imag - dy_imag * x_real], axis=1
+                )
     groups = [acc_ref[f].astype(BF) for f in range(PAIR)]
     out = backward(groups, t2_ref[...], t1i_ref[...], cos_ref[...], sin_ref[...]) * GRAD_SCALE
     for d in range(CTX):
@@ -174,24 +177,29 @@
     columns = [taps[:, f * FACTOR : (f + 1) * FACTOR] for f in range(PAIR)]
     h_ref[...] = forward(columns, t1_ref[...], t2_ref[...], cos_ref[...], sin_ref[...])
 
-    def body(j):
+    for both in range(0, Y, 2):
         spectra = []
-        for s in range(2):
-            for f in range(PAIR):
-                at = (s * PAIR + f) * HALF
-                real, imag = split(spec_ref[j, at : at + HALF])
-                h_real, h_imag = split(h_ref[f * HALF : (f + 1) * HALF])
-                if s == 0:
-                    both = [real * h_real - imag * h_imag, -(real * h_imag + imag * h_real)]
-                else:
-                    both = [real * h_real + imag * h_imag, real * h_imag - imag * h_real]
-                spectra.append(jnp.concatenate(both, axis=1).astype(BF))
+        for j in (both, both + 1):
+            for s in range(2):
+                for f in range(PAIR):
+                    at = (s * PAIR + f) * HALF
+                    real, imag = split(spec_ref[j, at : at + HALF])
+                    h_real, h_imag = split(h_ref[f * HALF : (f + 1) * HALF])
+                    if s == 0:
+                        pair = [real * h_real - imag * h_imag, -(real * h_imag + imag * h_real)]
+                    else:
+                        pair = [real * h_real + imag * h_imag, real * h_imag - imag * h_real]
+                    spectra.append(jnp.concatenate(pair, axis=1).astype(BF))
         out = backward(spectra, t2_ref[...], t1i_ref[...], cos_ref[...], sin_ref[...])
-        for d in range(CTX):
-            rows = [out[d * SUB : (d + 1) * SUB, q * FACTOR : (q + 1) * FACTOR] for q in range(4)]
-            rows = jnp.concatenate(rows, axis=0).astype(BF)
-            for k in range(2):
-                out_ref[d, j, 48 * k : 48 * k + 32] = rows[:, k * HALF : (k + 1) * HALF]
+        for j in (both, both + 1):
+            for d in range(CTX):
+                first = (j - both) * 4
+                rows = [
+                    out[d * SUB : (d + 1) * SUB, q * FACTOR : (q + 1) * FACTOR] for q in range(first, first + 4)
+                ]
+                rows = jnp.concatenate(rows, axis=0).astype(BF)
+                for k in range(2):
+                    out_ref[d, j, 48 * k : 48 * k + 32] = rows[:, k * HALF : (k + 1) * HALF]
 
     for d in range(CTX):
         a, b, c, e = (ref[d].astype(F32) for ref in parts)
@@ -199,8 +207,6 @@
         for j in range(Y):
             for k in range(2):
                 out_ref[d, j, 48 * k + 32 : 48 * (k + 1)] = rows[:, k * HALF : (k + 1) * HALF]
-    for j in range(Y):
-        body(j)
 
 
 def place_kernel(r_ref, a_ref, b_ref, g_ref, put, grad, sems):
@@ -212,19 +218,25 @@
         ]
         return mm(order, jnp.concatenate(halves, axis=1))
 
+    gives = []
+
+    def send(src, dst, n, k):
+        chunk = pl.ds(n * FACTOR, FACTOR)
+        give = pltpu.make_async_copy(src.at[chunk], dst.at[chunk], sems.at[3 * n + k])
+        give.start()
+        gives.append(give)
+
+    grads = [sorted_rows(outer, 16 * k, 16, 32, 16).astype(BF) for k in range(4)]
+    for n in range(SUB):
+        rows = jnp.concatenate([t[n * 32 : (n + 1) * 32] for t in grads], axis=0)
+        grad[n * FACTOR : (n + 1) * FACTOR] = rows.T.astype(F32)
+        send(grad, g_ref, n, 2)
     turned = [sorted_rows(sort, 8 * k, 8, 0, 32).astype(BF) for k in range(8)]
-    grads = [sorted_rows(outer, 16 * k, 16, 32, 16) for k in range(4)]
-    gives = []
     for n in range(SUB):
-        chunk = pl.ds(n * FACTOR, FACTOR)
-        for s in range(2):
+        for s, dst in enumerate((a_ref, b_ref)):
             at = n * 32 + s * 16
-            put[s, chunk] = jnp.concatenate([t[at : at + 16] for t in turned], axis=0).T
-        grad[chunk] = jnp.concatenate([t[n * 32 : (n + 1) * 32] for t in grads], axis=0).T
-        for k, (src, dst) in enumerate(((put.at[0], a_ref), (put.at[1], b_ref), (grad, g_ref))):
-            give = pltpu.make_async_copy(src.at[chunk], dst.at[chunk], sems.at[3 * n + k])
-            give.start()
-            gives.append(give)
+            put[s, n * FACTOR : (n + 1) * FACTOR] = jnp.concatenate([t[at : at + 16] for t in turned], axis=0).T
+            send(put.at[s], dst, n, s)
     for give in gives:
         give.wait()
 

time: 88.1 us -> 87.1 us (0.989)
  Pallas kernels: 10.5 us -> 9.46 us
    pallas_call x5, Pallas kernels: 10.5 us -> 9.46 us  [call(): pl.pallas_call(kernel, in_specs=[pl.BlockSpec(memory_space=pltpu.SMEM if...]
where the time goes in v4:
time: 87.1 us; the launch traced here: 86.8 us
  blocking collectives  48.5 us (56%)
  starting transfers between devices  15.7 us (18%)
  waiting for transfers between devices  12.2 us (14%)
  Pallas kernels  9.46 us (11%)
    all_to_all x1, blocking collectives, local(): lax.all_to_all(leaving.reshape(CTX * Y, 96, HALF), ('ctx', 'y'), 0, 0, ti...  29.8 us
    all_gather x1, blocking collectives, local(): partial = lax.all_gather(partial, 'zh', axis=0)  18.7 us
    all_to_all x1, waiting for transfers between devices, local(): arrived = lax.all_to_all(spread, ('ctx', 'y'), 0, 0, tiled=True)  11.4 us
    all_to_all x1, starting transfers between devices, local(): arrived = lax.all_to_all(spread, ('ctx', 'y'), 0, 0, tiled=True)  10.5 us
    pallas_call x5, Pallas kernels, call(): pl.pallas_call(kernel, in_specs=[pl.BlockSpec(memory_space=pltpu.SMEM if...  9.46 us
    ppermute x2, starting transfers between devices, handed(): return lax.ppermute(x, ('ctx', 'zh', 'y'), pairs)  4.65 us
  transfers between devices with their start and end apart: 4, of which 2 were waited for; matrix products, arithmetic and copies ran while one was open for 0% of the time, Pallas kernels for 3%

profile of v4, /device:TPU:1, one launch (start us, length us, event | category | flops | bytes accessed | tf_op | source)
XLA Modules:
  0.0 86.8 jit_solution(14138747003526745435)
XLA Ops:
  0.6 2.8 %shard_map.103 = bf16[64,64,128]{2,1,0:T(8,128)(2,1)} custom-call(bf16[2048,128]{1,0:T(8,128)(2,1)} %x_ref.1, bf16[2048,128]{1,0:T(8,128)(2,1)} %dy_ref.1), custom_call_target="tpu_custom_call" | custom-call | flops 536870912 | bytes 3145728 | tf_op jit(solution)/shard_map/pallas_call | solution.py:245
  3.5 0.0 copy-start.5
  3.5 0.0 copy-start
  3.5 0.0 copy-start.1
  3.5 0.0 copy-start.2
  3.5 0.0 copy-start.3
  3.5 0.0 copy-start.4
  3.5 10.5 %all-to-all-start = ((bf16[64,64,128]{2,1,0:T(8,128)(2,1)}), bf16[64,64,128]{2,1,0:T(8,128)(2,1)S(1)}, u32[]{:S(2)}, u32[]{:S(2)}) async-start(bf16[64,64,128]{2,1,0:T(8,128)(2,1)} %shard_map.103), calls=%async_computation | async-start | bytes 2097152 | tf_op jit(solution)/shard_map/all_to_all | solution.py:290
  14.1 0.0 copy-done.5
  14.1 0.5 collective-permute-start
  14.7 0.8 collective-permute-done
  15.5 2.7 %collective-permute-start.2 = (bf16[2,16,256]{2,1,0:T(8,128)(2,1)S(1)}, bf16[2,16,256]{2,1,0:T(8,128)(2,1)S(1)}, u32[]{:S(2)}, u32[]{:S(2)}) collective-permute-start(bf16[2,16,256]{2,1,0:T(8,128)(2,1)S(1)} %get-tuple-element.7), channel_id=1, source_target_pairs={{0,2},{1,18},{2,34},{3,50},{4,66},{5,82},{6,98},{7,114},{8,130},{9... | collective-permute-start | bytes 49160 | tf_op jit(solution)/shard_map/ppermute | solution.py:260
  18.2 1.9 %collective-permute-start.1 = (bf16[2,16,256]{2,1,0:T(8,128)(2,1)S(1)}, bf16[2,16,256]{2,1,0:T(8,128)(2,1)S(1)}, u32[]{:S(2)}, u32[]{:S(2)}) collective-permute-start(bf16[2,16,256]{2,1,0:T(8,128)(2,1)S(1)} %get-tuple-element.8), channel_id=1, source_target_pairs={{0,0},{1,16},{2,32},{3,48},{4,64},{5,80},{6,96},{7,112},{8,128},{9... | collective-permute-start | bytes 49160 | tf_op jit(solution)/shard_map/ppermute | solution.py:260
  20.2 11.4 %all-to-all-done.r_ref = bf16[64,64,128]{2,1,0:T(8,128)(2,1)S(1)} async-done(((bf16[64,64,128]{2,1,0:T(8,128)(2,1)}), bf16[64,64,128]{2,1,0:T(8,128)(2,1)S(1)}, u32[]{:S(2)}, u32[]{:S(2)}) %all-to-all-start) | async-done | bytes 1048608 | tf_op jit(solution)/shard_map/all_to_all | solution.py:290
  31.5 0.0 copy-done
  31.5 0.0 copy-done.1
  31.6 0.0 copy-done.2
  31.6 0.0 copy-done.3
  31.6 0.0 copy-done.4
  31.6 2.4 %shard_map.104 = (bf16[4,512,512]{2,1,0:T(8,128)(2,1)S(1)}, bf16[16,16,256]{2,1,0:T(8,128)(2,1)S(1)}) custom-call(bf16[64,64,128]{2,1,0:T(8,128)(2,1)S(1)} %all-to-all-done.r_ref, bf16[256,128]{1,0:T(8,128)(2,1)S(1)} %copy-done.4, bf16[512,512]{1,0:T(8,128)(2,1)S(1)} %copy-done, bf16[128,256]{1,0:T(8,128)(2,1)S(1)} %copy-done.3, f32[128,256]{1,0:T(8,128)S(1)} %copy-done.2, ...), custom_call_target="tpu_custom_call" | custom-call | flops 1512000000 | bytes 3145728 | tf_op jit(solution)/shard_map/pallas_call | solution.py:245
  34.0 0.0 collective-permute-done.2.b_ref
  34.0 0.0 collective-permute-done.1.a_ref
  34.1 18.7 %all-gather = bf16[80,16,256]{2,1,0:T(8,128)(2,1)S(1)} all-gather(bf16[20,16,256]{2,1,0:T(8,128)(2,1)S(1)} %shard_map.105), channel_id=2, replica_groups=mesh['ctx'=16,'zh'=4,'y'=4] {'zh'}, dimensions={0}, use_global_device_ids=true | all-gather | bytes 819200 | tf_op jit(solution)/shard_map/all_gather | solution.py:312
  52.8 2.3 %shard_map.106 = bf16[16,4,96,128]{3,2,1,0:T(8,128)(2,1)S(1)} custom-call(bf16[4,512,512]{2,1,0:T(8,128)(2,1)S(1)} %get-tuple-element.5.spec_ref, bf16[4,20,16,256]{3,2,1,0:T(8,128)(2,1)S(1)} %bitcast.12, s32[1]{0:T(128)} %bitcast.6.me_ref, bf16[256,128]{1,0:T(8,128)(2,1)S(1)} %copy-done.4, bf16[512,512]{1,0:T(8,128)(2,1)S(1)} %copy-done, ...), custom_call_target="tpu_custom_call" | custom-call | flops 1512000000 | bytes 3145728 | tf_op jit(solution)/shard_map/pallas_call | solution.py:245
  55.1 29.8 %all_to_all.10.r_ref = bf16[64,96,128]{2,1,0:T(8,128)(2,1)S(1)} all-to-all(bf16[64,96,128]{2,1,0:T(8,128)(2,1)S(1)} %bitcast.11), channel_id=1, replica_groups=mesh['ctx'=16,'zh'=4,'y'=4] {'ctx','y'}, dimensions={0} | all-to-all | bytes 3145728 | tf_op jit(solution)/shard_map/all_to_all | solution.py:327
  84.9 1.8 %shard_map.107 = (bf16[2048,128]{1,0:T(8,128)(2,1)}, bf16[2048,128]{1,0:T(8,128)(2,1)}, f32[2048,128]{1,0:T(8,128)}) custom-call(bf16[64,96,128]{2,1,0:T(8,128)(2,1)S(1)} %all_to_all.10.r_ref), custom_call_target="tpu_custom_call" | custom-call | flops 805306368 | bytes 3145728 | tf_op jit(solution)/shard_map/pallas_call | solution.py:245
  (4 shorter events, 0.0 us)
Async XLA Ops:
  3.5 10.6 %copy-start.5 = (bf16[2048,8]{0,1:T(8,128)(2,1)S(1)}, bf16[2048,8]{0,1:T(8,128)(2,1)}, u32[]{:S(2)}) copy-start(bf16[2048,8]{0,1:T(8,128)(2,1)} %param.10) | copy-start | bytes 98308
  3.5 28.1 %copy-start = (bf16[512,512]{1,0:T(8,128)(2,1)S(1)}, bf16[512,512]{1,0:T(8,128)(2,1)}, u32[]{:S(2)}) copy-start(bf16[512,512]{1,0:T(8,128)(2,1)} %constant.63.clone.t2_ref) | copy-start | bytes 1572868
  3.5 28.1 %copy-start.1 = (f32[128,256]{1,0:T(8,128)S(1)}, f32[128,256]{1,0:T(8,128)}, u32[]{:S(2)}) copy-start(f32[128,256]{1,0:T(8,128)} %constant.66.clone.sin_ref) | copy-start | bytes 393220
  3.5 28.0 %copy-start.2 = (f32[128,256]{1,0:T(8,128)S(1)}, f32[128,256]{1,0:T(8,128)}, u32[]{:S(2)}) copy-start(f32[128,256]{1,0:T(8,128)} %constant.65.clone.cos_ref) | copy-start | bytes 393220
  3.5 28.0 %copy-start.3 = (bf16[128,256]{1,0:T(8,128)(2,1)S(1)}, bf16[128,256]{1,0:T(8,128)(2,1)}, u32[]{:S(2)}) copy-start(bf16[128,256]{1,0:T(8,128)(2,1)} %constant.64.clone.t1i_ref) | copy-start | bytes 196612
  3.5 28.0 %copy-start.4 = (bf16[256,128]{1,0:T(8,128)(2,1)S(1)}, bf16[256,128]{1,0:T(8,128)(2,1)}, u32[]{:S(2)}) copy-start(bf16[256,128]{1,0:T(8,128)(2,1)} %constant.62.clone.t1_ref) | copy-start | bytes 196612
  3.5 28.0 %all-to-all-start = ((bf16[64,64,128]{2,1,0:T(8,128)(2,1)}), bf16[64,64,128]{2,1,0:T(8,128)(2,1)S(1)}, u32[]{:S(2)}, u32[]{:S(2)}) async-start(bf16[64,64,128]{2,1,0:T(8,128)(2,1)} %shard_map.103), calls=%async_computation | async-start | bytes 2097152 | tf_op jit(solution)/shard_map/all_to_all | solution.py:290
  14.1 1.4 %collective-permute-start = (bf16[2,16,256]{2,1,0:T(8,128)(2,1)S(1)}, bf16[2,16,256]{2,1,0:T(8,128)(2,1)S(1)}, u32[]{:S(2)}, u32[]{:S(2)}) collective-permute-start(bf16[2,16,256]{2,1,0:T(8,128)(2,1)S(1)} %get-tuple-element.9), channel_id=1, source_target_pairs={{0,16},{16,0},{32,48},{48,32},{64,80},{80,64},{96,112},{112,96},{1... | collective-permute-start | bytes 49160 | tf_op jit(solution)/shard_map/ppermute | solution.py:271
  15.5 18.5 %collective-permute-start.2 = (bf16[2,16,256]{2,1,0:T(8,128)(2,1)S(1)}, bf16[2,16,256]{2,1,0:T(8,128)(2,1)S(1)}, u32[]{:S(2)}, u32[]{:S(2)}) collective-permute-start(bf16[2,16,256]{2,1,0:T(8,128)(2,1)S(1)} %get-tuple-element.7), channel_id=1, source_target_pairs={{0,2},{1,18},{2,34},{3,50},{4,66},{5,82},{6,98},{7,114},{8,130},{9... | collective-permute-start | bytes 49160 | tf_op jit(solution)/shard_map/ppermute | solution.py:260
  18.2 15.8 %collective-permute-start.1 = (bf16[2,16,256]{2,1,0:T(8,128)(2,1)S(1)}, bf16[2,16,256]{2,1,0:T(8,128)(2,1)S(1)}, u32[]{:S(2)}, u32[]{:S(2)}) collective-permute-start(bf16[2,16,256]{2,1,0:T(8,128)(2,1)S(1)} %get-tuple-element.8), channel_id=1, source_target_pairs={{0,0},{1,16},{2,32},{3,48},{4,64},{5,80},{6,96},{7,112},{8,128},{9... | collective-permute-start | bytes 49160 | tf_op jit(solution)/shard_map/ppermute | solution.py:260

commit v5 on v4

--- a/solution.py
+++ b/solution.py
@@ -54,7 +54,7 @@
 
 
 def to_owners(r):
-    return (r & 7) * 32 + ((r >> 4) & 1) * 16 + (r >> 5) * PAIR + ((r >> 3) & 1)
+    return (r & 7) * 16 + (r >> 4) * PAIR + ((r >> 3) & 1)
 
 
 def to_subs(r):
@@ -94,34 +94,42 @@
 
 
 def spread_kernel(x_ref, dy_ref, out_ref, held, put, in_sems, out_sems):
+    half = SUB // 2
     takes = []
-    for n in range(SUB // 2):
-        chunk = pl.ds(2 * n * FACTOR, 2 * FACTOR)
-        for s, ref in enumerate((x_ref, dy_ref)):
-            take = pltpu.make_async_copy(ref.at[chunk], held.at[s, chunk], in_sems.at[2 * n + s])
+    for s, ref in enumerate((x_ref, dy_ref)):
+        for n in range(half):
+            chunk = pl.ds(2 * n * FACTOR, 2 * FACTOR)
+            take = pltpu.make_async_copy(ref.at[chunk], held.at[s, chunk], in_sems.at[half * s + n])
             take.start()
             takes.append(take)
-    sort = ones_at(to_owners)
-    turned = []
-    for n in range(SUB):
-        if n % 2 == 0:
-            takes[n].wait()
-            takes[n + 1].wait()
-        turned.append([held[s, n * FACTOR : (n + 1) * FACTOR].T for s in range(2)])
+    sort = ones_at(to_owners, HALF)
     gives = []
-    for g in range(SUB):
-        chunk = pl.ds(g * SUB, SUB)
-        rows = jnp.concatenate([t[g * 16 : (g + 1) * 16] for pair in turned for t in pair], axis=0)
-        rows = mm(sort, rows).astype(BF)
-        for k in range(2):
-            put[chunk, 32 * k : 32 * (k + 1)] = rows[:, k * HALF : (k + 1) * HALF].reshape(SUB, 32, HALF)
-        if g % 2 == 1:
-            chunk = pl.ds((g - 1) * SUB, 2 * SUB)
-            give = pltpu.make_async_copy(put.at[chunk], out_ref.at[chunk], out_sems.at[g])
-            give.start()
-            gives.append(give)
+    for s in range(2):
+        turned = []
+        for n in range(SUB):
+            if n % 2 == 0:
+                takes[half * s + n // 2].wait()
+            turned.append(held[s, n * FACTOR : (n + 1) * FACTOR].T)
+        for g in range(SUB):
+            rows = jnp.concatenate([t[g * 16 : (g + 1) * 16] for t in turned], axis=0)
+            rows = mm(sort, rows).astype(BF)
+            for k in range(2):
+                part = rows[:, k * HALF : (k + 1) * HALF].reshape(SUB, 16, HALF)
+                put[s, g * SUB : (g + 1) * SUB, 16 * k : 16 * (k + 1)] = part
+            if g % 4 == 3:
+                chunk = pl.ds((g - 3) * SUB, 4 * SUB)
+                give = pltpu.make_async_copy(
+                    put.at[s, chunk], out_ref.at[chunk, pl.ds(32 * s, 32)], out_sems.at[2 * s + g // 4]
+                )
+                give.start()
+                gives.append(give)
     for give in gives:
         give.wait()
+
+
+def arrived_rows(r_ref, owner, s):
+    at = 32 * s
+    return jnp.concatenate([r_ref[owner, at : at + 16], r_ref[owner, at + 16 : at + 32]], axis=1)
 
 
 def forward_kernel(r_ref, t1_ref, t2_ref, t1i_ref, cos_ref, sin_ref, spec_ref, g_ref, acc_ref):
@@ -131,7 +139,7 @@
         columns = []
         for j in (both, both + 1):
             tiles = [
-                jnp.concatenate([r_ref[i * Y + j, :32], r_ref[i * Y + j, 32:]], axis=1).astype(F32)
+                jnp.concatenate([arrived_rows(r_ref, i * Y + j, s) for s in range(2)], axis=0).astype(F32)
                 for i in range(CTX)
             ]
             for q in range(4):
@@ -276,7 +284,7 @@
         [((CTX * Y, 64, HALF), BF)],
         [
             pltpu.VMEM((2, TOK, HALF), BF),
-            pltpu.VMEM((CTX * Y, 64, HALF), BF),
+            pltpu.VMEM((2, CTX * Y, 32, HALF), BF),
             pltpu.SemaphoreType.DMA((2 * SUB,)),
             pltpu.SemaphoreType.DMA((SUB,)),
         ],

time: 87.1 us -> 87.3 us (level)
  no operation moved by 1% of the time
where the time goes in v5:
time: 87.3 us; the launch traced here: 87 us
  blocking collectives  48.5 us (56%)
  starting transfers between devices  15.7 us (18%)
  waiting for transfers between devices  12.2 us (14%)
  Pallas kernels  9.69 us (11%)
    all_to_all x1, blocking collectives, local(): lax.all_to_all(leaving.reshape(CTX * Y, 96, HALF), ('ctx', 'y'), 0, 0, ti...  29.9 us
    all_gather x1, blocking collectives, local(): partial = lax.all_gather(partial, 'zh', axis=0)  18.7 us
    all_to_all x1, waiting for transfers between devices, local(): arrived = lax.all_to_all(spread, ('ctx', 'y'), 0, 0, tiled=True)  11.4 us
    all_to_all x1, starting transfers between devices, local(): arrived = lax.all_to_all(spread, ('ctx', 'y'), 0, 0, tiled=True)  10.5 us
    pallas_call x5, Pallas kernels, call(): pl.pallas_call(kernel, in_specs=[pl.BlockSpec(memory_space=pltpu.SMEM if...  9.69 us
    ppermute x2, starting transfers between devices, handed(): return lax.ppermute(x, ('ctx', 'zh', 'y'), pairs)  4.65 us
  transfers between devices with their start and end apart: 4, of which 2 were waited for; matrix products, arithmetic and copies ran while one was open for 0% of the time, Pallas kernels for 3%

profile of v5, /device:TPU:1, one launch (start us, length us, event | category | flops | bytes accessed | tf_op | source)
XLA Modules:
  0.0 87.0 jit_solution(13191417836398008998)
XLA Ops:
  0.6 3.1 %shard_map.103 = bf16[64,64,128]{2,1,0:T(8,128)(2,1)} custom-call(bf16[2048,128]{1,0:T(8,128)(2,1)} %x_ref.1, bf16[2048,128]{1,0:T(8,128)(2,1)} %dy_ref.1), custom_call_target="tpu_custom_call" | custom-call | flops 536870912 | bytes 3145728 | tf_op jit(solution)/shard_map/pallas_call | solution.py:253
  3.7 0.0 copy-start.5
  3.7 0.0 copy-start
  3.7 0.0 copy-start.1
  3.7 0.0 copy-start.2
  3.8 0.0 copy-start.3
  3.8 0.0 copy-start.4
  3.8 10.5 %all-to-all-start = ((bf16[64,64,128]{2,1,0:T(8,128)(2,1)}), bf16[64,64,128]{2,1,0:T(8,128)(2,1)S(1)}, u32[]{:S(2)}, u32[]{:S(2)}) async-start(bf16[64,64,128]{2,1,0:T(8,128)(2,1)} %shard_map.103), calls=%async_computation | async-start | bytes 2097152 | tf_op jit(solution)/shard_map/all_to_all | solution.py:298
  14.3 0.0 copy-done.5
  14.4 0.5 collective-permute-start
  14.9 0.8 collective-permute-done
  15.8 2.7 %collective-permute-start.2 = (bf16[2,16,256]{2,1,0:T(8,128)(2,1)S(1)}, bf16[2,16,256]{2,1,0:T(8,128)(2,1)S(1)}, u32[]{:S(2)}, u32[]{:S(2)}) collective-permute-start(bf16[2,16,256]{2,1,0:T(8,128)(2,1)S(1)} %get-tuple-element.7), channel_id=1, source_target_pairs={{0,2},{1,18},{2,34},{3,50},{4,66},{5,82},{6,98},{7,114},{8,130},{9... | collective-permute-start | bytes 49160 | tf_op jit(solution)/shard_map/ppermute | solution.py:268
  18.5 1.9 %collective-permute-start.1 = (bf16[2,16,256]{2,1,0:T(8,128)(2,1)S(1)}, bf16[2,16,256]{2,1,0:T(8,128)(2,1)S(1)}, u32[]{:S(2)}, u32[]{:S(2)}) collective-permute-start(bf16[2,16,256]{2,1,0:T(8,128)(2,1)S(1)} %get-tuple-element.8), channel_id=1, source_target_pairs={{0,0},{1,16},{2,32},{3,48},{4,64},{5,80},{6,96},{7,112},{8,128},{9... | collective-permute-start | bytes 49160 | tf_op jit(solution)/shard_map/ppermute | solution.py:268
  20.4 11.4 %all-to-all-done.r_ref = bf16[64,64,128]{2,1,0:T(8,128)(2,1)S(1)} async-done(((bf16[64,64,128]{2,1,0:T(8,128)(2,1)}), bf16[64,64,128]{2,1,0:T(8,128)(2,1)S(1)}, u32[]{:S(2)}, u32[]{:S(2)}) %all-to-all-start) | async-done | bytes 1048608 | tf_op jit(solution)/shard_map/all_to_all | solution.py:298
  31.8 0.0 copy-done
  31.8 0.0 copy-done.1
  31.8 0.0 copy-done.2
  31.8 0.0 copy-done.3
  31.8 0.0 copy-done.4
  31.8 2.4 %shard_map.104 = (bf16[4,512,512]{2,1,0:T(8,128)(2,1)S(1)}, bf16[16,16,256]{2,1,0:T(8,128)(2,1)S(1)}) custom-call(bf16[64,64,128]{2,1,0:T(8,128)(2,1)S(1)} %all-to-all-done.r_ref, bf16[256,128]{1,0:T(8,128)(2,1)S(1)} %copy-done.4, bf16[512,512]{1,0:T(8,128)(2,1)S(1)} %copy-done, bf16[128,256]{1,0:T(8,128)(2,1)S(1)} %copy-done.3, f32[128,256]{1,0:T(8,128)S(1)} %copy-done.2, ...), custom_call_target="tpu_custom_call" | custom-call | flops 1512000000 | bytes 3145728 | tf_op jit(solution)/shard_map/pallas_call | solution.py:253
  34.2 0.0 collective-permute-done.2.b_ref
  34.3 0.0 collective-permute-done.1.a_ref
  34.3 18.7 %all-gather = bf16[80,16,256]{2,1,0:T(8,128)(2,1)S(1)} all-gather(bf16[20,16,256]{2,1,0:T(8,128)(2,1)S(1)} %shard_map.105), channel_id=2, replica_groups=mesh['ctx'=16,'zh'=4,'y'=4] {'zh'}, dimensions={0}, use_global_device_ids=true | all-gather | bytes 819200 | tf_op jit(solution)/shard_map/all_gather | solution.py:320
  53.0 2.3 %shard_map.106 = bf16[16,4,96,128]{3,2,1,0:T(8,128)(2,1)S(1)} custom-call(bf16[4,512,512]{2,1,0:T(8,128)(2,1)S(1)} %get-tuple-element.5.spec_ref, bf16[4,20,16,256]{3,2,1,0:T(8,128)(2,1)S(1)} %bitcast.12, s32[1]{0:T(128)} %bitcast.6.me_ref, bf16[256,128]{1,0:T(8,128)(2,1)S(1)} %copy-done.4, bf16[512,512]{1,0:T(8,128)(2,1)S(1)} %copy-done, ...), custom_call_target="tpu_custom_call" | custom-call | flops 1512000000 | bytes 3145728 | tf_op jit(solution)/shard_map/pallas_call | solution.py:253
  55.3 29.9 %all_to_all.10.r_ref = bf16[64,96,128]{2,1,0:T(8,128)(2,1)S(1)} all-to-all(bf16[64,96,128]{2,1,0:T(8,128)(2,1)S(1)} %bitcast.11), channel_id=1, replica_groups=mesh['ctx'=16,'zh'=4,'y'=4] {'ctx','y'}, dimensions={0} | all-to-all | bytes 3145728 | tf_op jit(solution)/shard_map/all_to_all | solution.py:335
  85.2 1.8 %shard_map.107 = (bf16[2048,128]{1,0:T(8,128)(2,1)}, bf16[2048,128]{1,0:T(8,128)(2,1)}, f32[2048,128]{1,0:T(8,128)}) custom-call(bf16[64,96,128]{2,1,0:T(8,128)(2,1)S(1)} %all_to_all.10.r_ref), custom_call_target="tpu_custom_call" | custom-call | flops 805306368 | bytes 3145728 | tf_op jit(solution)/shard_map/pallas_call | solution.py:253
  (4 shorter events, 0.0 us)
Async XLA Ops:
  3.7 10.6 %copy-start.5 = (bf16[2048,8]{0,1:T(8,128)(2,1)S(1)}, bf16[2048,8]{0,1:T(8,128)(2,1)}, u32[]{:S(2)}) copy-start(bf16[2048,8]{0,1:T(8,128)(2,1)} %param.10) | copy-start | bytes 98308
  3.7 28.1 %copy-start = (bf16[512,512]{1,0:T(8,128)(2,1)S(1)}, bf16[512,512]{1,0:T(8,128)(2,1)}, u32[]{:S(2)}) copy-start(bf16[512,512]{1,0:T(8,128)(2,1)} %constant.63.clone.t2_ref) | copy-start | bytes 1572868
  3.7 28.1 %copy-start.1 = (f32[128,256]{1,0:T(8,128)S(1)}, f32[128,256]{1,0:T(8,128)}, u32[]{:S(2)}) copy-start(f32[128,256]{1,0:T(8,128)} %constant.66.clone.sin_ref) | copy-start | bytes 393220
  3.7 28.1 %copy-start.2 = (f32[128,256]{1,0:T(8,128)S(1)}, f32[128,256]{1,0:T(8,128)}, u32[]{:S(2)}) copy-start(f32[128,256]{1,0:T(8,128)} %constant.65.clone.cos_ref) | copy-start | bytes 393220
  3.8 28.0 %copy-start.3 = (bf16[128,256]{1,0:T(8,128)(2,1)S(1)}, bf16[128,256]{1,0:T(8,128)(2,1)}, u32[]{:S(2)}) copy-start(bf16[128,256]{1,0:T(8,128)(2,1)} %constant.64.clone.t1i_ref) | copy-start | bytes 196612
  3.8 28.0 %copy-start.4 = (bf16[256,128]{1,0:T(8,128)(2,1)S(1)}, bf16[256,128]{1,0:T(8,128)(2,1)}, u32[]{:S(2)}) copy-start(bf16[256,128]{1,0:T(8,128)(2,1)} %constant.62.clone.t1_ref) | copy-start | bytes 196612
  3.8 28.0 %all-to-all-start = ((bf16[64,64,128]{2,1,0:T(8,128)(2,1)}), bf16[64,64,128]{2,1,0:T(8,128)(2,1)S(1)}, u32[]{:S(2)}, u32[]{:S(2)}) async-start(bf16[64,64,128]{2,1,0:T(8,128)(2,1)} %shard_map.103), calls=%async_computation | async-start | bytes 2097152 | tf_op jit(solution)/shard_map/all_to_all | solution.py:298
  14.4 1.4 %collective-permute-start = (bf16[2,16,256]{2,1,0:T(8,128)(2,1)S(1)}, bf16[2,16,256]{2,1,0:T(8,128)(2,1)S(1)}, u32[]{:S(2)}, u32[]{:S(2)}) collective-permute-start(bf16[2,16,256]{2,1,0:T(8,128)(2,1)S(1)} %get-tuple-element.9), channel_id=1, source_target_pairs={{0,16},{16,0},{32,48},{48,32},{64,80},{80,64},{96,112},{112,96},{1... | collective-permute-start | bytes 49160 | tf_op jit(solution)/shard_map/ppermute | solution.py:279
  15.8 18.5 %collective-permute-start.2 = (bf16[2,16,256]{2,1,0:T(8,128)(2,1)S(1)}, bf16[2,16,256]{2,1,0:T(8,128)(2,1)S(1)}, u32[]{:S(2)}, u32[]{:S(2)}) collective-permute-start(bf16[2,16,256]{2,1,0:T(8,128)(2,1)S(1)} %get-tuple-element.7), channel_id=1, source_target_pairs={{0,2},{1,18},{2,34},{3,50},{4,66},{5,82},{6,98},{7,114},{8,130},{9... | collective-permute-start | bytes 49160 | tf_op jit(solution)/shard_map/ppermute | solution.py:268
  18.5 15.8 %collective-permute-start.1 = (bf16[2,16,256]{2,1,0:T(8,128)(2,1)S(1)}, bf16[2,16,256]{2,1,0:T(8,128)(2,1)S(1)}, u32[]{:S(2)}, u32[]{:S(2)}) collective-permute-start(bf16[2,16,256]{2,1,0:T(8,128)(2,1)S(1)} %get-tuple-element.8), channel_id=1, source_target_pairs={{0,0},{1,16},{2,32},{3,48},{4,64},{5,80},{6,96},{7,112},{8,128},{9... | collective-permute-start | bytes 49160 | tf_op jit(solution)/shard_map/ppermute | solution.py:268

commit v6 on v4

--- a/solution.py
+++ b/solution.py
@@ -125,7 +125,6 @@
 
 
 def forward_kernel(r_ref, t1_ref, t2_ref, t1i_ref, cos_ref, sin_ref, spec_ref, g_ref, acc_ref):
-    acc_ref[...] = jnp.zeros_like(acc_ref)
 
     for both in range(0, Y, 2):
         columns = []
@@ -144,9 +143,9 @@
             for f in range(PAIR):
                 x_real, x_imag = split(spec[f * HALF : (f + 1) * HALF])
                 dy_real, dy_imag = split(spec[(PAIR + f) * HALF : (PAIR + f + 1) * HALF])
-                acc_ref[f] += jnp.concatenate(
-                    [dy_real * x_real + dy_imag * x_imag, dy_real * x_imag - dy_imag * x_real], axis=1
-                )
+                part = [dy_real * x_real + dy_imag * x_imag, dy_real * x_imag - dy_imag * x_real]
+                part = jnp.concatenate(part, axis=1)
+                acc_ref[f] = part if j == 0 else acc_ref[f] + part
     groups = [acc_ref[f].astype(BF) for f in range(PAIR)]
     out = backward(groups, t2_ref[...], t1i_ref[...], cos_ref[...], sin_ref[...]) * GRAD_SCALE
     for d in range(CTX):

time: 87.1 us -> 87.1 us (level)
  no operation moved by 1% of the time
where the time goes in v6:
time: 87.1 us; the launch traced here: 86.8 us
  blocking collectives  48.5 us (56%)
  starting transfers between devices  15.7 us (18%)
  waiting for transfers between devices  12.2 us (14%)
  Pallas kernels  9.46 us (11%)
    all_to_all x1, blocking collectives, local(): lax.all_to_all(leaving.reshape(CTX * Y, 96, HALF), ('ctx', 'y'), 0, 0, ti...  29.8 us
    all_gather x1, blocking collectives, local(): partial = lax.all_gather(partial, 'zh', axis=0)  18.7 us
    all_to_all x1, waiting for transfers between devices, local(): arrived = lax.all_to_all(spread, ('ctx', 'y'), 0, 0, tiled=True)  11.4 us
    all_to_all x1, starting transfers between devices, local(): arrived = lax.all_to_all(spread, ('ctx', 'y'), 0, 0, tiled=True)  10.5 us
    pallas_call x5, Pallas kernels, call(): pl.pallas_call(kernel, in_specs=[pl.BlockSpec(memory_space=pltpu.SMEM if...  9.46 us
    ppermute x2, starting transfers between devices, handed(): return lax.ppermute(x, ('ctx', 'zh', 'y'), pairs)  4.65 us
  transfers between devices with their start and end apart: 4, of which 2 were waited for; matrix products, arithmetic and copies ran while one was open for 0% of the time, Pallas kernels for 3%

profile of v6, /device:TPU:1, one launch (start us, length us, event | category | flops | bytes accessed | tf_op | source)
XLA Modules:
  0.0 86.8 jit_solution(14138747003526745435)
XLA Ops:
  0.6 2.8 %shard_map.103 = bf16[64,64,128]{2,1,0:T(8,128)(2,1)} custom-call(bf16[2048,128]{1,0:T(8,128)(2,1)} %x_ref.1, bf16[2048,128]{1,0:T(8,128)(2,1)} %dy_ref.1), custom_call_target="tpu_custom_call" | custom-call | flops 536870912 | bytes 3145728 | tf_op jit(solution)/shard_map/pallas_call | solution.py:244
  3.5 0.0 copy-start.5
  3.5 0.0 copy-start
  3.5 0.0 copy-start.1
  3.5 0.0 copy-start.2
  3.5 0.0 copy-start.3
  3.5 0.0 copy-start.4
  3.5 10.5 %all-to-all-start = ((bf16[64,64,128]{2,1,0:T(8,128)(2,1)}), bf16[64,64,128]{2,1,0:T(8,128)(2,1)S(1)}, u32[]{:S(2)}, u32[]{:S(2)}) async-start(bf16[64,64,128]{2,1,0:T(8,128)(2,1)} %shard_map.103), calls=%async_computation | async-start | bytes 2097152 | tf_op jit(solution)/shard_map/all_to_all | solution.py:289
  14.1 0.0 copy-done.5
  14.1 0.5 collective-permute-start
  14.7 0.8 collective-permute-done
  15.5 2.7 %collective-permute-start.2 = (bf16[2,16,256]{2,1,0:T(8,128)(2,1)S(1)}, bf16[2,16,256]{2,1,0:T(8,128)(2,1)S(1)}, u32[]{:S(2)}, u32[]{:S(2)}) collective-permute-start(bf16[2,16,256]{2,1,0:T(8,128)(2,1)S(1)} %get-tuple-element.7), channel_id=1, source_target_pairs={{0,2},{1,18},{2,34},{3,50},{4,66},{5,82},{6,98},{7,114},{8,130},{9... | collective-permute-start | bytes 49160 | tf_op jit(solution)/shard_map/ppermute | solution.py:259
  18.2 1.9 %collective-permute-start.1 = (bf16[2,16,256]{2,1,0:T(8,128)(2,1)S(1)}, bf16[2,16,256]{2,1,0:T(8,128)(2,1)S(1)}, u32[]{:S(2)}, u32[]{:S(2)}) collective-permute-start(bf16[2,16,256]{2,1,0:T(8,128)(2,1)S(1)} %get-tuple-element.8), channel_id=1, source_target_pairs={{0,0},{1,16},{2,32},{3,48},{4,64},{5,80},{6,96},{7,112},{8,128},{9... | collective-permute-start | bytes 49160 | tf_op jit(solution)/shard_map/ppermute | solution.py:259
  20.2 11.4 %all-to-all-done.r_ref = bf16[64,64,128]{2,1,0:T(8,128)(2,1)S(1)} async-done(((bf16[64,64,128]{2,1,0:T(8,128)(2,1)}), bf16[64,64,128]{2,1,0:T(8,128)(2,1)S(1)}, u32[]{:S(2)}, u32[]{:S(2)}) %all-to-all-start) | async-done | bytes 1048608 | tf_op jit(solution)/shard_map/all_to_all | solution.py:289
  31.5 0.0 copy-done
  31.5 0.0 copy-done.1
  31.6 0.0 copy-done.2
  31.6 0.0 copy-done.3
  31.6 0.0 copy-done.4
  31.6 2.4 %shard_map.104 = (bf16[4,512,512]{2,1,0:T(8,128)(2,1)S(1)}, bf16[16,16,256]{2,1,0:T(8,128)(2,1)S(1)}) custom-call(bf16[64,64,128]{2,1,0:T(8,128)(2,1)S(1)} %all-to-all-done.r_ref, bf16[256,128]{1,0:T(8,128)(2,1)S(1)} %copy-done.4, bf16[512,512]{1,0:T(8,128)(2,1)S(1)} %copy-done, bf16[128,256]{1,0:T(8,128)(2,1)S(1)} %copy-done.3, f32[128,256]{1,0:T(8,128)S(1)} %copy-done.2, ...), custom_call_target="tpu_custom_call" | custom-call | flops 1512000000 | bytes 3145728 | tf_op jit(solution)/shard_map/pallas_call | solution.py:244
  34.0 0.0 collective-permute-done.2.b_ref
  34.0 0.0 collective-permute-done.1.a_ref
  34.1 18.7 %all-gather = bf16[80,16,256]{2,1,0:T(8,128)(2,1)S(1)} all-gather(bf16[20,16,256]{2,1,0:T(8,128)(2,1)S(1)} %shard_map.105), channel_id=2, replica_groups=mesh['ctx'=16,'zh'=4,'y'=4] {'zh'}, dimensions={0}, use_global_device_ids=true | all-gather | bytes 819200 | tf_op jit(solution)/shard_map/all_gather | solution.py:311
  52.8 2.3 %shard_map.106 = bf16[16,4,96,128]{3,2,1,0:T(8,128)(2,1)S(1)} custom-call(bf16[4,512,512]{2,1,0:T(8,128)(2,1)S(1)} %get-tuple-element.5.spec_ref, bf16[4,20,16,256]{3,2,1,0:T(8,128)(2,1)S(1)} %bitcast.12, s32[1]{0:T(128)} %bitcast.6.me_ref, bf16[256,128]{1,0:T(8,128)(2,1)S(1)} %copy-done.4, bf16[512,512]{1,0:T(8,128)(2,1)S(1)} %copy-done, ...), custom_call_target="tpu_custom_call" | custom-call | flops 1512000000 | bytes 3145728 | tf_op jit(solution)/shard_map/pallas_call | solution.py:244
  55.1 29.8 %all_to_all.10.r_ref = bf16[64,96,128]{2,1,0:T(8,128)(2,1)S(1)} all-to-all(bf16[64,96,128]{2,1,0:T(8,128)(2,1)S(1)} %bitcast.11), channel_id=1, replica_groups=mesh['ctx'=16,'zh'=4,'y'=4] {'ctx','y'}, dimensions={0} | all-to-all | bytes 3145728 | tf_op jit(solution)/shard_map/all_to_all | solution.py:326
  84.9 1.8 %shard_map.107 = (bf16[2048,128]{1,0:T(8,128)(2,1)}, bf16[2048,128]{1,0:T(8,128)(2,1)}, f32[2048,128]{1,0:T(8,128)}) custom-call(bf16[64,96,128]{2,1,0:T(8,128)(2,1)S(1)} %all_to_all.10.r_ref), custom_call_target="tpu_custom_call" | custom-call | flops 805306368 | bytes 3145728 | tf_op jit(solution)/shard_map/pallas_call | solution.py:244
  (4 shorter events, 0.0 us)
Async XLA Ops:
  3.5 10.6 %copy-start.5 = (bf16[2048,8]{0,1:T(8,128)(2,1)S(1)}, bf16[2048,8]{0,1:T(8,128)(2,1)}, u32[]{:S(2)}) copy-start(bf16[2048,8]{0,1:T(8,128)(2,1)} %param.10) | copy-start | bytes 98308
  3.5 28.1 %copy-start = (bf16[512,512]{1,0:T(8,128)(2,1)S(1)}, bf16[512,512]{1,0:T(8,128)(2,1)}, u32[]{:S(2)}) copy-start(bf16[512,512]{1,0:T(8,128)(2,1)} %constant.63.clone.t2_ref) | copy-start | bytes 1572868
  3.5 28.1 %copy-start.1 = (f32[128,256]{1,0:T(8,128)S(1)}, f32[128,256]{1,0:T(8,128)}, u32[]{:S(2)}) copy-start(f32[128,256]{1,0:T(8,128)} %constant.66.clone.sin_ref) | copy-start | bytes 393220
  3.5 28.0 %copy-start.2 = (f32[128,256]{1,0:T(8,128)S(1)}, f32[128,256]{1,0:T(8,128)}, u32[]{:S(2)}) copy-start(f32[128,256]{1,0:T(8,128)} %constant.65.clone.cos_ref) | copy-start | bytes 393220
  3.5 28.0 %copy-start.3 = (bf16[128,256]{1,0:T(8,128)(2,1)S(1)}, bf16[128,256]{1,0:T(8,128)(2,1)}, u32[]{:S(2)}) copy-start(bf16[128,256]{1,0:T(8,128)(2,1)} %constant.64.clone.t1i_ref) | copy-start | bytes 196612
  3.5 28.0 %copy-start.4 = (bf16[256,128]{1,0:T(8,128)(2,1)S(1)}, bf16[256,128]{1,0:T(8,128)(2,1)}, u32[]{:S(2)}) copy-start(bf16[256,128]{1,0:T(8,128)(2,1)} %constant.62.clone.t1_ref) | copy-start | bytes 196612
  3.5 28.0 %all-to-all-start = ((bf16[64,64,128]{2,1,0:T(8,128)(2,1)}), bf16[64,64,128]{2,1,0:T(8,128)(2,1)S(1)}, u32[]{:S(2)}, u32[]{:S(2)}) async-start(bf16[64,64,128]{2,1,0:T(8,128)(2,1)} %shard_map.103), calls=%async_computation | async-start | bytes 2097152 | tf_op jit(solution)/shard_map/all_to_all | solution.py:289
  14.1 1.4 %collective-permute-start = (bf16[2,16,256]{2,1,0:T(8,128)(2,1)S(1)}, bf16[2,16,256]{2,1,0:T(8,128)(2,1)S(1)}, u32[]{:S(2)}, u32[]{:S(2)}) collective-permute-start(bf16[2,16,256]{2,1,0:T(8,128)(2,1)S(1)} %get-tuple-element.9), channel_id=1, source_target_pairs={{0,16},{16,0},{32,48},{48,32},{64,80},{80,64},{96,112},{112,96},{1... | collective-permute-start | bytes 49160 | tf_op jit(solution)/shard_map/ppermute | solution.py:270
  15.5 18.5 %collective-permute-start.2 = (bf16[2,16,256]{2,1,0:T(8,128)(2,1)S(1)}, bf16[2,16,256]{2,1,0:T(8,128)(2,1)S(1)}, u32[]{:S(2)}, u32[]{:S(2)}) collective-permute-start(bf16[2,16,256]{2,1,0:T(8,128)(2,1)S(1)} %get-tuple-element.7), channel_id=1, source_target_pairs={{0,2},{1,18},{2,34},{3,50},{4,66},{5,82},{6,98},{7,114},{8,130},{9... | collective-permute-start | bytes 49160 | tf_op jit(solution)/shard_map/ppermute | solution.py:259
  18.2 15.8 %collective-permute-start.1 = (bf16[2,16,256]{2,1,0:T(8,128)(2,1)S(1)}, bf16[2,16,256]{2,1,0:T(8,128)(2,1)S(1)}, u32[]{:S(2)}, u32[]{:S(2)}) collective-permute-start(bf16[2,16,256]{2,1,0:T(8,128)(2,1)S(1)} %get-tuple-element.8), channel_id=1, source_target_pairs={{0,0},{1,16},{2,32},{3,48},{4,64},{5,80},{6,96},{7,112},{8,128},{9... | collective-permute-start | bytes 49160 | tf_op jit(solution)/shard_map/ppermute | solution.py:259
